TPU v7x, 32 devices: a whole 2x2x4 slice. The times are simulated.
32 devices in a mesh: ka: 32 (over z, y, x, core).
Axes of the slice: x: 2, y: 2, z: 4, core: 2. Of those that a mesh axis runs over, the one named last changes fastest.
Arguments:
- density: float32 [256, 128, 128], P('ka'), may hold values from 0 to 1
- hamiltonian: float32 [256, 128, 128], P('ka'), may hold values from -1 to 1
- occupations: int32 [256], P('ka'), may hold values from 56 to 72
- form_factors: bfloat16 [33, 2, 128, 128], replicated, may hold values from -0.5 to 0.5
- hartree_forms: bfloat16 [32, 128, 128], replicated, may hold values from -0.5 to 0.5
- coupling: float32 [32], replicated, may hold values from 2 to 8
Outputs:
- fock_matrix: float32 [256, 128, 128], P('ka')
- new_density: float32 [256, 128, 128], P('ka')
All inputs are finite; a program needn't handle non-finite values.
Results may differ from a plain program's by a relative error of at most 0.0015.
Values may be sent and summed in bfloat16 or wider, within the bound.
No kernel may reach another device: no remote copies, remote signals or barrier semaphores. Data moves between devices by JAX's collectives and lax.ppermute only.
A program may use at most 64 MiB of HBM per device.

v0:
```python
import jax
import jax.numpy as jnp
from jax import lax
from jax.sharding import PartitionSpec as P

SPAN = 16
NPUR = 6


def passed_along(value, axis, steps):
    count = lax.axis_size(axis)
    pairs = [(source, (source + steps) % count) for source in range(count)]
    return lax.ppermute(value, axis, pairs)


def exchange_rows(window, form_factors, kpoint_count):
    shift_count = form_factors.shape[0]

    def one_kpoint(local_index):
        window_part = lax.dynamic_slice_in_dim(window, local_index, shift_count, 0)
        half_prod = jnp.einsum(
            "sgab,sbc->sgac", form_factors, window_part, preferred_element_type=jnp.float32
        ).astype(jnp.bfloat16)
        return jnp.einsum(
            "sgac,sgdc->ad", half_prod, form_factors, preferred_element_type=jnp.float32
        )

    return lax.map(one_kpoint, jnp.arange(kpoint_count, dtype=jnp.int32))


def per_device(density, hamiltonian, occupations, form_factors, hartree_forms, coupling):
    kpoint_count = density.shape[0]
    orbitals = density.shape[1]
    total_kpoints = kpoint_count * lax.axis_size("ka")
    hop_count = SPAN // kpoint_count
    identity = jnp.eye(orbitals, dtype=jnp.float32)
    deviation = (density - 0.5 * identity).astype(jnp.bfloat16)
    forms_flat = hartree_forms.reshape(hartree_forms.shape[0], orbitals * orbitals)
    partial_charge = jnp.sum(
        lax.dot_general(
            deviation.reshape(kpoint_count, orbitals * orbitals),
            forms_flat,
            (((1,), (1,)), ((), ())),
            preferred_element_type=jnp.float32,
        ),
        axis=0,
    )
    charge = lax.psum(partial_charge, "ka") / total_kpoints
    hartree = jnp.dot(
        coupling * charge, forms_flat.astype(jnp.float32), precision=lax.Precision.HIGHEST
    ).reshape(orbitals, orbitals)
    below_blocks = []
    above_blocks = []
    below_block = deviation
    above_block = deviation
    for hop_index in range(hop_count):
        below_block = passed_along(below_block, "ka", 1)
        above_block = passed_along(above_block, "ka", -1)
        below_blocks.append(below_block)
        above_blocks.append(above_block)
    window = jnp.concatenate(below_blocks[::-1] + [deviation] + above_blocks, axis=0)
    exchange = exchange_rows(window, form_factors, kpoint_count)
    combined = hamiltonian + hartree[None, :, :] - exchange
    fock_matrix = 0.5 * (combined + jnp.swapaxes(combined, 1, 2))
    traces = jnp.trace(fock_matrix, axis1=1, axis2=2)
    level_mean = lax.psum(jnp.sum(traces), "ka") / (total_kpoints * orbitals)
    centred = fock_matrix - level_mean * identity
    largest = lax.pmax(jnp.max(jnp.sum(centred * centred, axis=(1, 2))), "ka")
    radius = jnp.sqrt(1e-06 + largest)
    filling = occupations.astype(jnp.float32) / orbitals
    purified = filling[:, None, None] * identity - 0.5 / radius * centred
    for sweep_index in range(NPUR):
        square = jnp.einsum("kab,kbc->kac", purified, purified, precision=lax.Precision.HIGHEST)
        cubed = jnp.einsum("kab,kbc->kac", square, purified, precision=lax.Precision.HIGHEST)
        purified = 3.0 * square - 2.0 * cubed
    return (fock_matrix, purified)


def solution(mesh):
    placed = (P("ka", None, None), P("ka", None, None), P("ka"), P(), P(), P())
    return jax.shard_map(
        per_device,
        mesh=mesh,
        in_specs=placed,
        out_specs=(P("ka", None, None), P("ka", None, None)),
        check_vma=False,
    )
```

profile of v0, /device:TPU:0, one launch (start us, length us, event | category | flops | bytes accessed | tf_op | source)
XLA Modules:
  0.0 203.3 jit_solution(13004620019561055414)
XLA Ops:
  0.7 1.2 subtract_convert_fusion
  2.3 2.1 %fusion.23 = f32[32]{0:T(128)S(1)} fusion(bf16[32,128,128]{2,1,0:T(8,128)(2,1)} %param.12, bf16[8,128,128]{2,1,0:T(8,128)(2,1)S(1)} %subtract_convert_fusion), kind=kOutput, calls=%fused_computation.22 | convolution fusion | flops 8388832 | bytes 1310848 | tf_op jit(solution)/shard_map/dot_general | solution.py:40
  4.5 5.9 %collective-permute-start.2 = (bf16[8,128,128]{2,1,0:T(8,128)(2,1)S(1)}, bf16[8,128,128]{2,1,0:T(8,128)(2,1)}, u32[]{:S(2)}, u32[]{:S(2)}) collective-permute-start(bf16[8,128,128]{2,1,0:T(8,128)(2,1)S(1)} %subtract_convert_fusion), channel_id=1, source_target_pairs={{0,31},{1,0},{2,1},{3,2},{4,3},{5,4},{6,5},{7,6},{8,7},{9,8},{10,9... | collective-permute-start | bytes 786440 | tf_op jit(solution)/shard_map/ppermute | solution.py:13
  10.4 38.9 %psum.14 = f32[32]{0:T(128)S(1)} all-reduce(f32[32]{0:T(128)S(1)} %fusion.23), channel_id=1, replica_groups=mesh['ka'=32] {'ka'}, use_global_device_ids=true, to_apply=%region_1.0 | all-reduce | flops 32 | bytes 256 | tf_op jit(solution)/shard_map/psum | solution.py:48
  49.3 1.0 fusion.24
  50.4 1.8 copy.13
  52.2 0.7 copy.20
  52.9 1.0 copy.12
  54.5 5.3 %collective-permute-start.3 = (bf16[8,128,128]{2,1,0:T(8,128)(2,1)}, bf16[8,128,128]{2,1,0:T(8,128)(2,1)S(1)}, u32[]{:S(2)}, u32[]{:S(2)}) collective-permute-start(bf16[8,128,128]{2,1,0:T(8,128)(2,1)} %collective-permute-done.2), channel_id=1, source_target_pairs={{0,31},{1,0},{2,1},{3,2},{4,3},{5,4},{6,5},{7,6},{8,7},{9,8},{10,9... | collective-permute-start | bytes 786440 | tf_op jit(solution)/shard_map/ppermute | solution.py:13
  59.8 1.0 constant_dynamic-update-slice_fusion.4
  60.8 1.0 constant_dynamic-update-slice_fusion.3
  61.8 1.1 constant_dynamic-update-slice_fusion.2
  62.9 1.0 constant_dynamic-update-slice_fusion.1
  64.0 0.6 iota.47
  64.6 44.2 %while.10 = (s32[]{:T(128)}, f32[8,128,128]{1,2,0:T(8,128)}, s32[8]{0:T(128)}, bf16[40,128,128]{2,1,0:T(8,128)(2,1)S(1)}, bf16[33,2,128,128]{3,2,0,1:T(8,128)(2,1)S(1)}, /*index=5*/s32[]{:T(128)}, s32[]{:T(128)}, s32[]{:T(128)}) while((s32[]{:T(128)}, f32[8,128,128]{1,2,0:T(8,128)}, s32[8]{0:T(128)}, bf16[40,128,128]{2,1,0:T(8,128)(2,1)S(1)}, ...), condition=%wide.region_3.4_spmd, body=%wide.region_2.3_spmd.sunk | while | flops 554729472 | bytes 5472903 | solution.py:28
  64.6 1.3 dynamic_slice.15
  67.6 2.6 %fusion.85 = f32[8,128,128]{1,2,0:T(8,128)} fusion(f32[8,128,128]{1,2,0:T(8,128)} %get-tuple-element.92, s32[]{:T(128)} %get-tuple-element.91, bf16[33,2,128,128]{3,2,0,1:T(8,128)(2,1)S(1)} %get-tuple-element.103, bf16[40,128,128]{2,1,0:T(8,128)(2,1)S(1)} %get-tuple-element.102, s32[]{:T(128)S(6)} %select_n.11), kind=kOutput, calls=%fused_computation.5.clone.1 | convolution fusion | flops 554729472 | bytes 5472772 | tf_op jit(solution)/shard_map/while/body/eval_jaxpr/sgac,sgdc->ad/dot_general | solution.py:24
  70.2 1.3 dynamic_slice.15
  73.1 2.6 %fusion.85 = f32[8,128,128]{1,2,0:T(8,128)} fusion(f32[8,128,128]{1,2,0:T(8,128)} %get-tuple-element.92, s32[]{:T(128)} %get-tuple-element.91, bf16[33,2,128,128]{3,2,0,1:T(8,128)(2,1)S(1)} %get-tuple-element.103, bf16[40,128,128]{2,1,0:T(8,128)(2,1)S(1)} %get-tuple-element.102, s32[]{:T(128)S(6)} %select_n.11), kind=kOutput, calls=%fused_computation.5.clone.1 | convolution fusion | flops 554729472 | bytes 5472772 | tf_op jit(solution)/shard_map/while/body/eval_jaxpr/sgac,sgdc->ad/dot_general | solution.py:24
  75.7 1.3 dynamic_slice.15
  78.7 2.6 %fusion.85 = f32[8,128,128]{1,2,0:T(8,128)} fusion(f32[8,128,128]{1,2,0:T(8,128)} %get-tuple-element.92, s32[]{:T(128)} %get-tuple-element.91, bf16[33,2,128,128]{3,2,0,1:T(8,128)(2,1)S(1)} %get-tuple-element.103, bf16[40,128,128]{2,1,0:T(8,128)(2,1)S(1)} %get-tuple-element.102, s32[]{:T(128)S(6)} %select_n.11), kind=kOutput, calls=%fused_computation.5.clone.1 | convolution fusion | flops 554729472 | bytes 5472772 | tf_op jit(solution)/shard_map/while/body/eval_jaxpr/sgac,sgdc->ad/dot_general | solution.py:24
  81.2 1.3 dynamic_slice.15
  84.2 2.6 %fusion.85 = f32[8,128,128]{1,2,0:T(8,128)} fusion(f32[8,128,128]{1,2,0:T(8,128)} %get-tuple-element.92, s32[]{:T(128)} %get-tuple-element.91, bf16[33,2,128,128]{3,2,0,1:T(8,128)(2,1)S(1)} %get-tuple-element.103, bf16[40,128,128]{2,1,0:T(8,128)(2,1)S(1)} %get-tuple-element.102, s32[]{:T(128)S(6)} %select_n.11), kind=kOutput, calls=%fused_computation.5.clone.1 | convolution fusion | flops 554729472 | bytes 5472772 | tf_op jit(solution)/shard_map/while/body/eval_jaxpr/sgac,sgdc->ad/dot_general | solution.py:24
  86.8 1.3 dynamic_slice.15
  89.7 2.6 %fusion.85 = f32[8,128,128]{1,2,0:T(8,128)} fusion(f32[8,128,128]{1,2,0:T(8,128)} %get-tuple-element.92, s32[]{:T(128)} %get-tuple-element.91, bf16[33,2,128,128]{3,2,0,1:T(8,128)(2,1)S(1)} %get-tuple-element.103, bf16[40,128,128]{2,1,0:T(8,128)(2,1)S(1)} %get-tuple-element.102, s32[]{:T(128)S(6)} %select_n.11), kind=kOutput, calls=%fused_computation.5.clone.1 | convolution fusion | flops 554729472 | bytes 5472772 | tf_op jit(solution)/shard_map/while/body/eval_jaxpr/sgac,sgdc->ad/dot_general | solution.py:24
  92.3 1.3 dynamic_slice.15
  95.2 2.6 %fusion.85 = f32[8,128,128]{1,2,0:T(8,128)} fusion(f32[8,128,128]{1,2,0:T(8,128)} %get-tuple-element.92, s32[]{:T(128)} %get-tuple-element.91, bf16[33,2,128,128]{3,2,0,1:T(8,128)(2,1)S(1)} %get-tuple-element.103, bf16[40,128,128]{2,1,0:T(8,128)(2,1)S(1)} %get-tuple-element.102, s32[]{:T(128)S(6)} %select_n.11), kind=kOutput, calls=%fused_computation.5.clone.1 | convolution fusion | flops 554729472 | bytes 5472772 | tf_op jit(solution)/shard_map/while/body/eval_jaxpr/sgac,sgdc->ad/dot_general | solution.py:24
  97.8 1.3 dynamic_slice.15
  100.7 2.6 %fusion.85 = f32[8,128,128]{1,2,0:T(8,128)} fusion(f32[8,128,128]{1,2,0:T(8,128)} %get-tuple-element.92, s32[]{:T(128)} %get-tuple-element.91, bf16[33,2,128,128]{3,2,0,1:T(8,128)(2,1)S(1)} %get-tuple-element.103, bf16[40,128,128]{2,1,0:T(8,128)(2,1)S(1)} %get-tuple-element.102, s32[]{:T(128)S(6)} %select_n.11), kind=kOutput, calls=%fused_computation.5.clone.1 | convolution fusion | flops 554729472 | bytes 5472772 | tf_op jit(solution)/shard_map/while/body/eval_jaxpr/sgac,sgdc->ad/dot_general | solution.py:24
  103.3 1.3 dynamic_slice.15
  106.3 2.6 %fusion.85 = f32[8,128,128]{1,2,0:T(8,128)} fusion(f32[8,128,128]{1,2,0:T(8,128)} %get-tuple-element.92, s32[]{:T(128)} %get-tuple-element.91, bf16[33,2,128,128]{3,2,0,1:T(8,128)(2,1)S(1)} %get-tuple-element.103, bf16[40,128,128]{2,1,0:T(8,128)(2,1)S(1)} %get-tuple-element.102, s32[]{:T(128)S(6)} %select_n.11), kind=kOutput, calls=%fused_computation.5.clone.1 | convolution fusion | flops 554729472 | bytes 5472772 | tf_op jit(solution)/shard_map/while/body/eval_jaxpr/sgac,sgdc->ad/dot_general | solution.py:24
  108.8 1.3 add_subtract_fusion
  110.3 0.7 select_reduce_fusion
  111.1 38.4 %psum.15 = f32[]{:T(128)} all-reduce(f32[]{:T(128)} %get-tuple-element.50), channel_id=1, replica_groups=mesh['ka'=32] {'ka'}, use_global_device_ids=true, to_apply=%region_5.6 | all-reduce | flops 1 | bytes 8 | tf_op jit(solution)/shard_map/psum | solution.py:66
  150.3 0.6 reduce_max.9
  150.9 42.7 %pmax.7 = f32[]{:T(128)} all-reduce(f32[]{:T(128)} %reduce_max.9), channel_id=1, replica_groups=mesh['ka'=32] {'ka'}, use_global_device_ids=true, to_apply=%region_8.9 | all-reduce | flops 1 | bytes 8 | tf_op jit(solution)/shard_map/pmax | solution.py:68
  194.4 0.8 fusion.29
  195.2 0.7 fusion.22
  196.0 0.6 fusion.48
  196.6 0.7 fusion.21
  197.3 0.6 fusion.49
  197.9 0.7 fusion.20
  198.6 0.6 fusion.50
  199.2 0.7 fusion.19
  199.9 0.6 fusion.51
  200.5 0.7 fusion.18
  201.2 0.6 fusion.52
  201.9 1.5 fusion.17
  (31 shorter events, 1.7 us)
Async XLA Ops:
  0.6 48.7 %copy-start.5 = (bf16[32,128,128]{2,1,0:T(8,128)(2,1)S(1)}, bf16[32,128,128]{2,1,0:T(8,128)(2,1)}, u32[]{:S(2)}) copy-start(bf16[32,128,128]{2,1,0:T(8,128)(2,1)} %param.12) | copy-start | bytes 3145732
  0.6 48.6 %copy-start.6 = (f32[32]{0:T(128)S(1)}, f32[32]{0:T(128)}, u32[]{:S(2)}) copy-start(f32[32]{0:T(128)} %param.13) | copy-start | bytes 388
  1.8 48.4 %collective-permute-start = (bf16[8,128,128]{2,1,0:T(8,128)(2,1)S(1)}, bf16[8,128,128]{2,1,0:T(8,128)(2,1)S(1)}, u32[]{:S(2)}, u32[]{:S(2)}) collective-permute-start(bf16[8,128,128]{2,1,0:T(8,128)(2,1)S(1)} %subtract_convert_fusion), channel_id=1, source_target_pairs={{0,1},{1,2},{2,3},{3,4},{4,5},{5,6},{6,7},{7,8},{8,9},{9,10},{10,1... | collective-permute-start | bytes 786440 | tf_op jit(solution)/shard_map/ppermute | solution.py:13
  4.5 50.0 %collective-permute-start.2 = (bf16[8,128,128]{2,1,0:T(8,128)(2,1)S(1)}, bf16[8,128,128]{2,1,0:T(8,128)(2,1)}, u32[]{:S(2)}, u32[]{:S(2)}) collective-permute-start(bf16[8,128,128]{2,1,0:T(8,128)(2,1)S(1)} %subtract_convert_fusion), channel_id=1, source_target_pairs={{0,31},{1,0},{2,1},{3,2},{4,3},{5,4},{6,5},{7,6},{8,7},{9,8},{10,9... | collective-permute-start | bytes 786440 | tf_op jit(solution)/shard_map/ppermute | solution.py:13
  50.3 1.9 copy-start.3
  50.3 9.6 %collective-permute-start.1 = (bf16[8,128,128]{2,1,0:T(8,128)(2,1)S(1)}, bf16[8,128,128]{2,1,0:T(8,128)(2,1)}, u32[]{:S(2)}, u32[]{:S(2)}) collective-permute-start(bf16[8,128,128]{2,1,0:T(8,128)(2,1)S(1)} %collective-permute-done), channel_id=1, source_target_pairs={{0,1},{1,2},{2,3},{3,4},{4,5},{5,6},{6,7},{7,8},{8,9},{9,10},{10,1... | collective-permute-start | bytes 786440 | tf_op jit(solution)/shard_map/ppermute | solution.py:13
  50.4 2.6 %copy-start.1 = (f32[8,128,128]{2,1,0:T(8,128)S(1)}, f32[8,128,128]{2,1,0:T(8,128)}, u32[]{:S(2)}) copy-start(f32[8,128,128]{2,1,0:T(8,128)} %param.9) | copy-start | bytes 1572868
  50.4 3.5 %copy-start.7 = (s32[8]{0:T(128)S(1)}, s32[8]{0:T(128)}, u32[]{:S(2)}) copy-start(s32[8]{0:T(128)} %param.10) | copy-start | bytes 100
  54.5 9.5 %collective-permute-start.3 = (bf16[8,128,128]{2,1,0:T(8,128)(2,1)}, bf16[8,128,128]{2,1,0:T(8,128)(2,1)S(1)}, u32[]{:S(2)}, u32[]{:S(2)}) collective-permute-start(bf16[8,128,128]{2,1,0:T(8,128)(2,1)} %collective-permute-done.2), channel_id=1, source_target_pairs={{0,31},{1,0},{2,1},{3,2},{4,3},{5,4},{6,5},{7,6},{8,7},{9,8},{10,9... | collective-permute-start | bytes 786440 | tf_op jit(solution)/shard_map/ppermute | solution.py:13
  64.6 44.2 %copy-start.2 = (f32[1,128,128]{1,2,0:T(8,128)S(1)}, f32[1,128,128]{1,2,0:T(8,128)}, u32[]{:S(2)}) copy-start(f32[1,128,128]{1,2,0:T(8,128)} %copy.20) | copy-start | bytes 196612
  110.3 84.1 %copy-start.4 = (f32[8]{0:T(128)S(1)}, f32[8]{0:T(128)}, u32[]{:S(2)}) copy-start(f32[8]{0:T(128)} %convert_multiply_fusion) | copy-start | bytes 100
  111.1 84.9 %copy-start = (f32[8,128,128]{2,1,0:T(8,128)}, f32[8,128,128]{2,1,0:T(8,128)S(1)}, u32[]{:S(2)}) copy-start(f32[8,128,128]{2,1,0:T(8,128)S(1)} %get-tuple-element.51) | copy-start | bytes 1572868
where the time goes:
time: 204 us; the launch traced here: 203 us
  blocking collectives  120 us (59%)
  matrix products  32.6 us (16%)
  local copies, waits for them, and re-layouts  17.4 us (9%)
  loops' own time  13.5 us (7%)
  starting transfers between devices  11.8 us (6%)
  other arithmetic  5.63 us (3%)
  between operations  2.24 us (1%)
    pmax x1, blocking collectives, per_device(): largest = lax.pmax(jnp.max(jnp.sum(centred * centred, axis=(1, 2))), 'ka')  42.7 us
    psum x1, blocking collectives, per_device(): charge = lax.psum(partial_charge, 'ka') / total_kpoints  38.9 us
    psum x1, blocking collectives, per_device(): level_mean = lax.psum(jnp.sum(traces), 'ka') / (total_kpoints * orbitals)  38.4 us
    dot_general x8, matrix products, one_kpoint(): jnp.einsum('sgac,sgdc->ad', half_prod, form_factors, preferred_element_ty...  20.7 us
    another operation x1, loops' own time, exchange_rows(): return lax.map(one_kpoint, jnp.arange(kpoint_count, dtype=jnp.int32))  13.5 us
    ppermute x4, starting transfers between devices, passed_along(): return lax.ppermute(value, axis, pairs)  11.8 us
    dynamic_slice x8, local copies, waits for them, and re-layouts, exchange_rows(): return lax.map(one_kpoint, jnp.arange(kpoint_count, dtype=jnp.int32))  10.1 us
    dot_general x6, matrix products, per_device(): jnp.einsum('kab,kbc->kac', square, purified, precision=lax.Precision.HIGH...  4.95 us
  transfers between devices with their start and end apart: 4, of which 1 were waited for; matrix products, arithmetic and copies ran while one was open for 6% of the time, Pallas kernels for 0%

commit v1 on v0

v1 whole, which is shorter than its diff:
```python
import functools

import jax
import jax.numpy as jnp
from jax import lax
from jax.experimental import pallas as pl
from jax.experimental.pallas import tpu as pltpu
from jax.sharding import PartitionSpec as P

SPAN = 16
NPUR = 6
N = 128
KL = 8
CORES = 2
PACK = KL // 2 * N + 16
F32 = jnp.float32
BF16 = jnp.bfloat16
VMEM = pl.BlockSpec(memory_space=pltpu.VMEM)
SMEM = pl.BlockSpec(memory_space=pltpu.SMEM)
LANES_LAST = (((1,), (1,)), ((), ()))


def square_iota():
    row = lax.broadcasted_iota(jnp.int32, (N, N), 0)
    col = lax.broadcasted_iota(jnp.int32, (N, N), 1)
    return row, col


def params(mib):
    return pltpu.CompilerParams(vmem_limit_bytes=mib << 20)


def pack_kernel(density_ref, packed_ref, sum_ref):
    row, col = square_iota()
    half_eye = jnp.where(row == col, 0.5, 0.0).astype(F32)
    total = jnp.zeros((N, N), F32)
    diagonals = []
    for pair in range(KL // 2):
        parts = []
        for member in range(2):
            deviation = (density_ref[2 * pair + member] - half_eye).astype(BF16).astype(F32)
            total = total + deviation
            parts.append(0.5 * (deviation + deviation.T))
        packed_ref[pair * N : (pair + 1) * N, :] = jnp.where(row <= col, parts[0], parts[1]).astype(BF16)
        diagonals.append(jnp.sum(jnp.where(row == col, parts[1], 0.0), axis=0, keepdims=True))
    diagonals.append(jnp.zeros((16 - KL // 2, N), F32))
    packed_ref[KL // 2 * N :, :] = jnp.concatenate(diagonals, axis=0).astype(BF16)
    sum_ref[...] = total


def unpack(packed, blocks_ref, start):
    row, col = square_iota()
    diagonals = packed[KL // 2 * N :, :].astype(F32)
    for pair in range(KL // 2):
        both = packed[pair * N : (pair + 1) * N, :].astype(F32)
        flipped = both.T
        blocks_ref[start + 2 * pair] = jnp.where(row <= col, both, flipped).astype(BF16)
        second = jnp.where(row > col, both, jnp.where(row < col, flipped, diagonals[pair : pair + 1, :]))
        blocks_ref[start + 2 * pair + 1] = second.astype(BF16)


def both_terms(factors_ref, index):
    return jnp.concatenate([factors_ref[index, 0], factors_ref[index, 1]], axis=1)


def inner_kernel(packed_ref, factors_ref, sum_ref, forms_ref, exchange_ref, charge_ref, blocks, halves, rows):
    core = lax.rem(lax.axis_index("ka"), CORES)
    base = SPAN - (KL - 1) - KL * core
    for member in range(CORES):
        unpack(packed_ref.at[member], blocks, member * KL)

    def first(step, carry):
        right = jnp.concatenate([blocks[2 * step], blocks[2 * step + 1]], axis=1)
        left = factors_ref[pl.ds(base + 2 * step, KL + 1)].reshape((KL + 1) * 2 * N, N)
        product = jnp.dot(left, right, preferred_element_type=F32).astype(BF16)
        for shift in range(KL + 1):
            for member in range(2):
                k = member + KL - 1 - shift
                if 0 <= k < KL:
                    for term in range(2):
                        at = (shift * 2 + term) * N
                        halves[2 * step + shift, k * N : (k + 1) * N, term * N : (term + 1) * N] = product[
                            at : at + N, member * N : (member + 1) * N
                        ]
        return carry

    lax.fori_loop(0, CORES * KL // 2, first, 0)
    exchange_ref[...] = jnp.zeros_like(exchange_ref)
    for shift in range(CORES * KL + KL - 1):
        low = max(0, KL - 1 - shift)
        high = min(KL, CORES * KL + KL - 1 - shift)
        exchange_ref[low * N : high * N, :] += lax.dot_general(
            halves[shift, low * N : high * N, :],
            both_terms(factors_ref, base + shift),
            LANES_LAST,
            preferred_element_type=F32,
        )
    form_count = forms_ref.shape[0]
    for j in range(form_count):
        rows[j : j + 1, :] = jnp.sum(sum_ref[...] * forms_ref[j].astype(F32), axis=0, keepdims=True)
    charge_ref[...] = lax.dot_general(
        jnp.ones((8, N), F32), rows[...], LANES_LAST, precision=lax.Precision.HIGHEST, preferred_element_type=F32
    )


def outer_kernel(
    packed_ref, factors_ref, inner_ref, hamiltonian_ref, forms_ref, charge_ref, level_ref, stats_ref,
    blocks, near, far, exchange, traceless, rows,
):
    core = lax.rem(lax.axis_index("ka"), CORES)
    flipped = core == 1
    last = 2 * SPAN
    for member in range(CORES):
        unpack(packed_ref.at[1 - core, member], blocks, member * KL)
    unpack(packed_ref.at[core, core], blocks, CORES * KL)

    def near_factor(distance):
        return jnp.where(flipped, last - distance, distance)

    def far_factor(distance):
        return jnp.where(flipped, distance, last - distance)

    def near_block(t):
        return jnp.where(flipped, CORES * KL - 1 - t, t)

    def far_block(t):
        return CORES * KL + jnp.where(flipped, KL - 1 - t, t)

    def pair_product(first_block, second_block, shifts):
        right = jnp.concatenate([blocks[first_block], blocks[second_block]], axis=1)
        left = jnp.concatenate([factors_ref[shift].reshape(2 * N, N) for shift in shifts], axis=0)
        return jnp.dot(left, right, preferred_element_type=F32).astype(BF16)

    for step in range(CORES * KL // 2):
        distances = list(range(max(0, 2 * step - KL + 1), 2 * step + 2))
        product = pair_product(near_block(2 * step), near_block(2 * step + 1), [near_factor(d) for d in distances])
        for place, distance in enumerate(distances):
            for member in range(2):
                k = 2 * step + member - distance
                if 0 <= k < KL:
                    for term in range(2):
                        at = (place * 2 + term) * N
                        near[distance, k * N : (k + 1) * N, term * N : (term + 1) * N] = product[
                            at : at + N, member * N : (member + 1) * N
                        ]
    for step in range(KL // 2):
        distances = list(range(0, KL - 2 * step))
        product = pair_product(far_block(2 * step), far_block(2 * step + 1), [far_factor(d) for d in distances])
        for place, distance in enumerate(distances):
            for member in range(2):
                k = 2 * step + member + distance
                if 0 <= k < KL:
                    for term in range(2):
                        at = (place * 2 + term) * N
                        far[distance, k * N : (k + 1) * N, term * N : (term + 1) * N] = product[
                            at : at + N, member * N : (member + 1) * N
                        ]
    exchange[...] = jnp.zeros_like(exchange)
    for distance in range(CORES * KL):
        high = min(KL, CORES * KL - distance)
        exchange[: high * N, :] += lax.dot_general(
            near[distance, : high * N, :],
            both_terms(factors_ref, near_factor(distance)),
            LANES_LAST,
            preferred_element_type=F32,
        )
    for distance in range(KL):
        exchange[distance * N :, :] += lax.dot_general(
            far[distance, distance * N :, :],
            both_terms(factors_ref, far_factor(distance)),
            LANES_LAST,
            preferred_element_type=F32,
        )

    row, col = square_iota()
    stat_row = lax.broadcasted_iota(jnp.int32, (KL, N), 0)
    stat_col = lax.broadcasted_iota(jnp.int32, (KL, N), 1)
    stats = jnp.zeros((KL, N), F32)
    form_count = forms_ref.shape[0]
    for k in range(KL):
        mirrored = pl.multiple_of(jnp.where(flipped, KL - 1 - k, k) * N, N)
        combined = hamiltonian_ref[k] - inner_ref[k * N : (k + 1) * N, :] - exchange[pl.ds(mirrored, N), :]
        level = 0.5 * (combined + combined.T)
        level_ref[k] = level
        mean = jnp.sum(jnp.where(row == col, level, 0.0), keepdims=True) / N
        rest = level - jnp.where(row == col, mean, 0.0)
        traceless[k] = rest
        norm = jnp.sum(rest * rest, keepdims=True)
        stats = jnp.where((stat_row == k) & (stat_col == 2 * form_count), norm, stats)
        stats = jnp.where((stat_row == k) & (stat_col == 2 * form_count + 1), mean, stats)

    group = 4

    def overlaps(step, carry):
        sums = [[jnp.zeros((8, N), F32) for _ in range(group)] for _ in range(KL)]
        for part in range(N // 16):
            forms = [forms_ref[step * group + j, part * 16 : (part + 1) * 16, :].astype(F32) for j in range(group)]
            for k in range(KL):
                upper = traceless[k, part * 16 : part * 16 + 8, :]
                lower = traceless[k, part * 16 + 8 : part * 16 + 16, :]
                for j in range(group):
                    sums[k][j] = sums[k][j] + upper * forms[j][:8] + lower * forms[j][8:]
        for k in range(KL):
            for j in range(group):
                rows[k, pl.ds(step * group + j, 1), :] = jnp.sum(sums[k][j], axis=0, keepdims=True)
        return carry

    lax.fori_loop(0, form_count // group, overlaps, 0)
    pieces = jnp.zeros((KL, form_count), F32)
    short_row = lax.broadcasted_iota(jnp.int32, (KL, form_count), 0)
    for k in range(KL):
        dots = lax.dot_general(
            jnp.ones((KL, N), F32), rows[k], LANES_LAST, precision=lax.Precision.HIGHEST, preferred_element_type=F32
        )
        pieces = jnp.where(short_row == k, dots, pieces)
    charge = jnp.where(short_row == 0, charge_ref[...], 0.0)
    rest_lanes = jnp.zeros((KL, N - 2 * form_count), F32)
    stats = stats + jnp.concatenate([pieces, charge, rest_lanes], axis=1)
    stats_ref[...] = jnp.broadcast_to(stats[None], stats_ref.shape)


def final_kernel(stats_ref, level_ref, forms_ref, coupling_ref, occupations_ref, fock_ref, density_ref):
    form_count = forms_ref.shape[0]
    total = stats_ref.shape[0] * KL
    stats = stats_ref[...].reshape(total, N)
    charge = jnp.sum(stats[:, form_count : 2 * form_count], axis=0, keepdims=True) / total
    weights = coupling_ref[...] * charge
    row, col = square_iota()
    hartree = jnp.zeros((N, N), F32)
    for j in range(form_count):
        hartree = hartree + weights[:, j : j + 1] * forms_ref[j].astype(F32)
    hartree = 0.5 * (hartree + hartree.T)
    offset = jnp.sum(jnp.where(row == col, hartree, 0.0), keepdims=True) / N
    traceless = hartree - jnp.where(row == col, offset, 0.0)
    own = jnp.sum(traceless * traceless, keepdims=True)
    cross = jnp.sum(stats[:, :form_count] * weights, axis=1, keepdims=True)
    means = stats[:, 2 * form_count + 1 : 2 * form_count + 2]
    mean = jnp.sum(means, axis=0, keepdims=True) / total
    norms = stats[:, 2 * form_count : 2 * form_count + 1] + 2.0 * cross + own + N * (means - mean) ** 2
    radius = jnp.sqrt(1e-06 + jnp.max(norms, axis=0, keepdims=True))
    scale = 0.5 / radius
    shift = offset + mean
    eye = jnp.where(row == col, 1.0, 0.0).astype(F32)
    current = []
    for k in range(KL):
        fock = level_ref[k] + hartree
        fock_ref[k] = fock
        filling = occupations_ref[k].astype(F32) / N - 0.5
        current.append((filling + scale * shift) * eye - scale * fock)
    for _ in range(NPUR):
        for k in range(KL):
            short = current[k].astype(BF16)
            square = jnp.dot(short, short, preferred_element_type=F32).astype(BF16)
            cube = jnp.dot(square, short, preferred_element_type=F32)
            current[k] = 1.5 * current[k] - 2.0 * cube
    for k in range(KL):
        density_ref[k] = current[k] + 0.5 * eye


def per_device(density, hamiltonian, occupations, form_factors, hartree_forms, coupling):
    kpoint_count = density.shape[0]
    count = lax.axis_size("ka")
    form_count = hartree_forms.shape[0]
    assert kpoint_count == KL and KL * CORES == SPAN and count % CORES == 0
    shape = jax.ShapeDtypeStruct
    chips = [list(range(first, first + CORES)) for first in range(0, count, CORES)]
    packed, deviation_sum = pl.pallas_call(
        pack_kernel,
        out_shape=(shape((PACK, N), BF16), shape((N, N), F32)),
        in_specs=[VMEM],
        out_specs=(VMEM, VMEM),
        compiler_params=params(16),
    )(density)
    own_chip = lax.all_gather(packed, "ka", axis_index_groups=chips)
    pairs = [(d, (d - CORES) % count if d % CORES == 0 else (d + CORES) % count) for d in range(count)]
    neighbour = lax.ppermute(own_chip, "ka", pairs)
    inner, charge = pl.pallas_call(
        inner_kernel,
        out_shape=(shape((KL * N, N), F32), shape((8, form_count), F32)),
        in_specs=[VMEM] * 4,
        out_specs=(VMEM, VMEM),
        scratch_shapes=[
            pltpu.VMEM((CORES * KL, N, N), BF16),
            pltpu.VMEM((CORES * KL + KL - 1, KL * N, 2 * N), BF16),
            pltpu.VMEM((form_count, N), F32),
        ],
        compiler_params=params(28),
        cost_estimate=pl.CostEstimate(flops=5 * 10**9, bytes_accessed=5 * 10**6, transcendentals=0),
    )(own_chip, form_factors, deviation_sum, hartree_forms)
    outside = lax.all_gather(neighbour, "ka", axis_index_groups=chips)
    level, stats = pl.pallas_call(
        outer_kernel,
        out_shape=(shape((KL, N, N), F32), shape((count, KL, N), F32)),
        in_specs=[VMEM] * 6,
        out_specs=(VMEM, VMEM),
        scratch_shapes=[
            pltpu.VMEM((CORES * KL + KL, N, N), BF16),
            pltpu.VMEM((CORES * KL, KL * N, 2 * N), BF16),
            pltpu.VMEM((KL, KL * N, 2 * N), BF16),
            pltpu.VMEM((KL * N, N), F32),
            pltpu.VMEM((KL, N, N), F32),
            pltpu.VMEM((KL, form_count, N), F32),
        ],
        compiler_params=params(32),
    )(outside, form_factors, inner, hamiltonian, hartree_forms, charge)
    shared = lax.all_to_all(stats, "ka", 0, 0)
    return pl.pallas_call(
        final_kernel,
        out_shape=(shape((KL, N, N), F32), shape((KL, N, N), F32)),
        in_specs=[VMEM] * 4 + [SMEM],
        out_specs=(VMEM, VMEM),
        compiler_params=params(24),
    )(shared, level, hartree_forms, coupling.reshape(1, form_count), occupations)


def solution(mesh):
    placed = (P("ka", None, None), P("ka", None, None), P("ka"), P(), P(), P())
    return jax.shard_map(
        per_device,
        mesh=mesh,
        in_specs=placed,
        out_specs=(P("ka", None, None), P("ka", None, None)),
        check_vma=False,
    )
```

time: 204 us -> 45.7 us (0.22)
  blocking collectives: 120 us -> 14.2 us
  matrix products: 32.6 us -> 0 us
  Pallas kernels: 0 us -> 19.8 us
  local copies, waits for them, and re-layouts: 17.4 us -> 3.89 us
  loops' own time: 13.5 us -> 0 us
  other arithmetic: 5.63 us -> 0 us
  starting transfers between devices: 11.8 us -> 6.84 us
    psum x2 -> x0, blocking collectives: 77.3 us -> none  [the longest x1 38.9 us: per_device(): charge = lax.psum(partial_charge, 'ka') / total_kpoints]
    pmax x1 -> x0, blocking collectives: 42.7 us -> none  [per_device(): largest = lax.pmax(jnp.max(jnp.sum(centred * centred, axis=(1, 2))), 'ka')]
    dot_general x22 -> x0, matrix products: 32.6 us -> none  [the longest x8 20.7 us: one_kpoint(): jnp.einsum('sgac,sgdc->ad', half_prod, form_factors, preferred_element_ty...]
    pallas_call x0 -> x4, Pallas kernels: none -> 19.8 us  [the longest x1 9.49 us: per_device(): pl.pallas_call(outer_kernel, out_shape=(shape((KL, N, N), F32), shape((co...]
    another operation x1 -> x0, loops' own time: 13.5 us -> none  [exchange_rows(): return lax.map(one_kpoint, jnp.arange(kpoint_count, dtype=jnp.int32))]
    dynamic_slice x8 -> x0, local copies, waits for them, and re-layouts: 10.1 us -> none  [exchange_rows(): return lax.map(one_kpoint, jnp.arange(kpoint_count, dtype=jnp.int32))]
    all_to_all x0 -> x1, blocking collectives: none -> 9.93 us  [per_device(): shared = lax.all_to_all(stats, 'ka', 0, 0)]
    ppermute x4 -> x1, starting transfers between devices: 11.8 us -> 6.84 us  [per_device(): neighbour = lax.ppermute(own_chip, 'ka', pairs)]
  transfers between devices with their start and end apart: 4 -> 1, of which waited for: 1 -> 0; matrix products, arithmetic and copies ran while one was open for 6% -> 0% of each run, Pallas kernels for 0% -> 14%
where the time goes in v1:
time: 45.7 us; the launch traced here: 45.5 us
  Pallas kernels  19.8 us (43%)
  blocking collectives  14.2 us (31%)
  starting transfers between devices  6.84 us (15%)
  local copies, waits for them, and re-layouts  3.89 us (9%)
  between operations  0.68 us (1%)
    all_to_all x1, blocking collectives, per_device(): shared = lax.all_to_all(stats, 'ka', 0, 0)  9.93 us
    pallas_call x1, Pallas kernels, per_device(): pl.pallas_call(outer_kernel, out_shape=(shape((KL, N, N), F32), shape((co...  9.49 us
    ppermute x1, starting transfers between devices, per_device(): neighbour = lax.ppermute(own_chip, 'ka', pairs)  6.84 us
    pallas_call x1, Pallas kernels, per_device(): pl.pallas_call(inner_kernel, out_shape=(shape((KL * N, N), F32), shape((8...  6.32 us
    unnamed x16, local copies, waits for them, and re-layouts  3.89 us
    pallas_call x1, Pallas kernels, per_device(): pl.pallas_call(final_kernel, out_shape=(shape((KL, N, N), F32), shape((KL...  3.87 us
    all_gather x1, blocking collectives, per_device(): outside = lax.all_gather(neighbour, 'ka', axis_index_groups=chips)  2.19 us
    all_gather x1, blocking collectives, per_device(): own_chip = lax.all_gather(packed, 'ka', axis_index_groups=chips)  2.09 us
  transfers between devices with their start and end apart: 1, of which 0 were waited for; matrix products, arithmetic and copies ran while one was open for 0% of the time, Pallas kernels for 14%

profile of v1, /device:TPU:0, one launch (start us, length us, event | category | flops | bytes accessed | tf_op | source)
XLA Modules:
  0.0 45.5 jit_solution(18031017435617346301)
XLA Ops:
  0.6 0.0 copy-start.4
  0.6 1.0 %copy-done.4 = f32[8,128,128]{2,1,0:T(8,128)S(1)} copy-done((f32[8,128,128]{2,1,0:T(8,128)S(1)}, f32[8,128,128]{2,1,0:T(8,128)}, u32[]{:S(2)}) %copy-start.4) | copy-done | bytes 524312
  1.7 0.2 shard_map.77
  1.8 2.1 %all-gather = bf16[1056,128]{1,0:T(8,128)(2,1)S(1)} all-gather(bf16[528,128]{1,0:T(8,128)(2,1)S(1)} %get-tuple-element.8), channel_id=2, replica_groups={{0,1},{2,3},{4,5},{6,7},{8,9},{10,11},{12,13},{14,15},{16,17},{18,19},{..., dimensions={0}, use_global_device_ids=true | all-gather | bytes 405504 | tf_op jit(solution)/shard_map/all_gather | solution.py:274
  3.9 6.8 %collective-permute-start = (bf16[2,528,128]{2,1,0:T(8,128)(2,1)S(1)}, bf16[2,528,128]{2,1,0:T(8,128)(2,1)S(1)}, u32[]{:S(2)}, u32[]{:S(2)}) collective-permute-start(bf16[2,528,128]{2,1,0:T(8,128)(2,1)S(1)} %bitcast.4), channel_id=1, source_target_pairs={{0,30},{1,3},{2,0},{3,5},{4,2},{5,7},{6,4},{7,9},{8,6},{9,11},{10,... | collective-permute-start | bytes 811016 | tf_op jit(solution)/shard_map/ppermute | solution.py:276
  10.8 0.0 copy-start
  10.8 1.2 %copy-done = bf16[32,128,128]{2,1,0:T(8,128)(2,1)S(1)} copy-done((bf16[32,128,128]{2,1,0:T(8,128)(2,1)S(1)}, bf16[32,128,128]{2,1,0:T(8,128)(2,1)}, u32[]{:S(2)}) %copy-start) | copy-done | bytes 1048600
  12.0 0.0 copy-start.2
  12.0 1.6 %copy-done.2 = bf16[33,2,128,128]{3,2,1,0:T(8,128)(2,1)S(1)} copy-done((bf16[33,2,128,128]{3,2,1,0:T(8,128)(2,1)S(1)}, bf16[33,2,128,128]{3,2,1,0:T(8,128)(2,1)}, u32[]{:S(2)}) %copy-start.2) | copy-done | bytes 2162712
  13.6 0.0 copy-start.1
  13.6 0.0 copy-start.3
  13.6 0.0 copy-start.5
  13.6 6.3 %shard_map.78 = (f32[1024,128]{1,0:T(8,128)S(1)}, f32[8,32]{1,0:T(8,128)S(1)}) custom-call(bf16[2,528,128]{2,1,0:T(8,128)(2,1)S(1)} %bitcast.5, bf16[33,2,128,128]{3,2,1,0:T(8,128)(2,1)S(1)} %copy-done.2, f32[128,128]{1,0:T(8,128)S(1)} %get-tuple-element.9.sum_ref, bf16[32,128,128]{2,1,0:T(8,128)(2,1)S(1)} %copy-done), custom_call_target="tpu_custom_call" | custom-call | flops 5000000000 | bytes 5000000 | tf_op jit(solution)/shard_map/pallas_call | solution.py:277
  19.9 0.0 collective-permute-done
  19.9 2.2 %all-gather.1 = bf16[4,528,128]{2,1,0:T(8,128)(2,1)S(1)} all-gather(bf16[2,528,128]{2,1,0:T(8,128)(2,1)S(1)} %collective-permute-done), channel_id=3, replica_groups={{0,1},{2,3},{4,5},{6,7},{8,9},{10,11},{12,13},{14,15},{16,17},{18,19},{..., dimensions={0}, use_global_device_ids=true | all-gather | bytes 811008 | tf_op jit(solution)/shard_map/all_gather | solution.py:290
  22.1 0.0 copy-done.1
  22.1 0.0 copy-done.3
  22.1 0.0 copy-done.5
  22.1 0.0 copy-start.6
  22.1 0.0 copy-start.7
  22.2 9.5 %shard_map.79 = (f32[8,128,128]{2,1,0:T(8,128)S(1)}, f32[32,8,128]{2,1,0:T(8,128)S(1)}) custom-call(bf16[2,2,528,128]{3,2,1,0:T(8,128)(2,1)S(1)} %bitcast.3, bf16[33,2,128,128]{3,2,1,0:T(8,128)(2,1)S(1)} %copy-done.3, f32[1024,128]{1,0:T(8,128)S(1)} %get-tuple-element.10.inner_ref, f32[8,128,128]{2,1,0:T(8,128)S(1)} %copy-done.5, ...), custom_call_target="tpu_custom_call" | custom-call | tf_op jit(solution)/shard_map/pallas_call | solution.py:291
  31.7 9.9 %all_to_all.5.stats_ref = f32[32,8,128]{2,1,0:T(8,128)S(1)} all-to-all(f32[32,8,128]{2,1,0:T(8,128)S(1)} %get-tuple-element.12), channel_id=1, replica_groups=mesh['ka'=32] {'ka'}, dimensions={0} | all-to-all | bytes 262144 | tf_op jit(solution)/shard_map/all_to_all | solution.py:306
  41.6 0.0 copy-done.6
  41.6 0.0 copy-done.7
  41.6 3.9 %shard_map.80 = (f32[8,128,128]{2,1,0:T(8,128)}, f32[8,128,128]{2,1,0:T(8,128)}) custom-call(f32[32,8,128]{2,1,0:T(8,128)S(1)} %all_to_all.5.stats_ref, f32[8,128,128]{2,1,0:T(8,128)S(1)} %get-tuple-element.13.level_ref, bf16[32,128,128]{2,1,0:T(8,128)(2,1)S(1)} %copy-done.1, f32[1,32]{1,0:T(1,128)S(1)} %bitcast.6, s32[8]{0:T(128)S(1)} %copy-done.7), custom_call_target="tpu_custom_call" | custom-call | tf_op jit(solution)/shard_map/pallas_call | solution.py:307
Async XLA Ops:
  0.6 1.0 %copy-start.4 = (f32[8,128,128]{2,1,0:T(8,128)S(1)}, f32[8,128,128]{2,1,0:T(8,128)}, u32[]{:S(2)}) copy-start(f32[8,128,128]{2,1,0:T(8,128)} %density_ref.1) | copy-start | bytes 1572868
  3.9 16.0 %collective-permute-start = (bf16[2,528,128]{2,1,0:T(8,128)(2,1)S(1)}, bf16[2,528,128]{2,1,0:T(8,128)(2,1)S(1)}, u32[]{:S(2)}, u32[]{:S(2)}) collective-permute-start(bf16[2,528,128]{2,1,0:T(8,128)(2,1)S(1)} %bitcast.4), channel_id=1, source_target_pairs={{0,30},{1,3},{2,0},{3,5},{4,2},{5,7},{6,4},{7,9},{8,6},{9,11},{10,... | collective-permute-start | bytes 811016 | tf_op jit(solution)/shard_map/ppermute | solution.py:276
  10.8 1.2 %copy-start = (bf16[32,128,128]{2,1,0:T(8,128)(2,1)S(1)}, bf16[32,128,128]{2,1,0:T(8,128)(2,1)}, u32[]{:S(2)}) copy-start(bf16[32,128,128]{2,1,0:T(8,128)(2,1)} %forms_ref.5) | copy-start | bytes 3145732
  12.0 1.6 %copy-start.2 = (bf16[33,2,128,128]{3,2,1,0:T(8,128)(2,1)S(1)}, bf16[33,2,128,128]{3,2,1,0:T(8,128)(2,1)}, u32[]{:S(2)}) copy-start(bf16[33,2,128,128]{3,2,1,0:T(8,128)(2,1)} %factors_ref.3) | copy-start | bytes 6488068
  13.6 8.5 %copy-start.1 = (bf16[32,128,128]{2,1,0:T(8,128)(2,1)S(1)}, bf16[32,128,128]{2,1,0:T(8,128)(2,1)}, u32[]{:S(2)}) copy-start(bf16[32,128,128]{2,1,0:T(8,128)(2,1)} %forms_ref.5) | copy-start | bytes 3145732
  13.6 8.5 %copy-start.3 = (bf16[33,2,128,128]{3,2,1,0:T(8,128)(2,1)S(1)}, bf16[33,2,128,128]{3,2,1,0:T(8,128)(2,1)}, u32[]{:S(2)}) copy-start(bf16[33,2,128,128]{3,2,1,0:T(8,128)(2,1)} %factors_ref.3) | copy-start | bytes 6488068
  13.6 8.5 %copy-start.5 = (f32[8,128,128]{2,1,0:T(8,128)S(1)}, f32[8,128,128]{2,1,0:T(8,128)}, u32[]{:S(2)}) copy-start(f32[8,128,128]{2,1,0:T(8,128)} %hamiltonian_ref.1) | copy-start | bytes 1572868
  22.1 19.5 %copy-start.6 = (f32[32]{0:T(128)S(1)}, f32[32]{0:T(128)}, u32[]{:S(2)}) copy-start(f32[32]{0:T(128)} %param.11) | copy-start | bytes 388
  22.1 19.4 %copy-start.7 = (s32[8]{0:T(128)S(1)}, s32[8]{0:T(128)}, u32[]{:S(2)}) copy-start(s32[8]{0:T(128)} %occupations_ref.1) | copy-start | bytes 100

commit v2 on v1

v2 whole, which is shorter than its diff:
```python
import jax
import jax.numpy as jnp
from jax import lax
from jax.experimental import pallas as pl
from jax.experimental.pallas import tpu as pltpu
from jax.sharding import PartitionSpec as P

SPAN = 16
NPUR = 6
N = 128
KL = 8
CORES = 2
CHIP = CORES * KL
PACK = KL // 2 * N + 16
SHIFTS = CHIP + KL - 1
F32 = jnp.float32
BF16 = jnp.bfloat16
VMEM = pl.BlockSpec(memory_space=pltpu.VMEM)
SMEM = pl.BlockSpec(memory_space=pltpu.SMEM)
ANY = pl.BlockSpec(memory_space=pl.ANY)
LANES_LAST = (((1,), (1,)), ((), ()))


def square_iota():
    row = lax.broadcasted_iota(jnp.int32, (N, N), 0)
    col = lax.broadcasted_iota(jnp.int32, (N, N), 1)
    return row, col


def params(mib):
    return pltpu.CompilerParams(vmem_limit_bytes=mib << 20)


def lane_sums(rows):
    return lax.dot_general(
        jnp.ones((8, N), F32), rows, LANES_LAST, precision=lax.Precision.HIGHEST, preferred_element_type=F32
    )


def pack_kernel(density_hbm, packed_ref, sum_ref, density, arrived):
    copies = [pltpu.make_async_copy(density_hbm.at[k], density.at[k], arrived.at[k]) for k in range(KL)]
    for copy in copies:
        copy.start()
    row, col = square_iota()
    half_eye = jnp.where(row == col, 0.5, 0.0).astype(F32)
    total = jnp.zeros((N, N), F32)
    diagonals = []
    for pair in range(KL // 2):
        parts = []
        for member in range(2):
            copies[2 * pair + member].wait()
            deviation = (density[2 * pair + member] - half_eye).astype(BF16).astype(F32)
            total = total + deviation
            parts.append(0.5 * (deviation + deviation.T))
        packed_ref[pair * N : (pair + 1) * N, :] = jnp.where(row <= col, parts[0], parts[1]).astype(BF16)
        diagonals.append(jnp.sum(jnp.where(row == col, parts[1], 0.0), axis=0, keepdims=True))
    diagonals.append(jnp.zeros((16 - KL // 2, N), F32))
    packed_ref[KL // 2 * N :, :] = jnp.concatenate(diagonals, axis=0).astype(BF16)
    sum_ref[...] = total


def unpack(packed, blocks, place):
    row, col = square_iota()
    diagonals = packed[KL // 2 * N :, :].astype(F32)
    for pair in range(KL // 2):
        both = packed[pair * N : (pair + 1) * N, :].astype(F32)
        flipped = both.T
        blocks[place(2 * pair)] = jnp.where(row <= col, both, flipped).astype(BF16)
        second = jnp.where(row > col, both, jnp.where(row < col, flipped, diagonals[pair : pair + 1, :]))
        blocks[place(2 * pair + 1)] = second.astype(BF16)


def half_products(blocks, first, count, factor):
    left = blocks[first : first + count].reshape(count * N, N)
    return lax.dot_general(left, factor.reshape(2 * N, N), LANES_LAST, preferred_element_type=F32).astype(BF16)


def place_halves(products, k, slot, piece):
    lanes = slice(k % 2 * N, (k % 2 + 1) * N)
    for term in range(2):
        products[k // 2, (2 * slot + term) * N : (2 * slot + term + 1) * N, lanes] = piece[:, term * N : (term + 1) * N]


def clear_halves(products, k, slot):
    lanes = slice(k % 2 * N, (k % 2 + 1) * N)
    products[k // 2, 2 * slot * N : (2 * slot + 2) * N, lanes] = jnp.zeros((2 * N, N), BF16)


def second_product(products, pair, factors):
    left = jnp.concatenate([factor[term] for factor in factors for term in range(2)], axis=1)
    right = products[pair, : 2 * N * len(factors), :]
    return jnp.dot(left, right, preferred_element_type=F32)


def inner_kernel(
    packed_ref, factors_hbm, sum_ref, forms_hbm, exchange_ref, charge_ref,
    factors, forms, blocks, products, rows, arrived,
):
    core = lax.rem(lax.axis_index("ka"), CORES)
    base = SPAN - (KL - 1) - KL * core
    bounds = [0, 6, 12, 18, SHIFTS]
    copies = [
        pltpu.make_async_copy(
            factors_hbm.at[pl.ds(base + low, high - low)], factors.at[pl.ds(low, high - low)], arrived.at[i]
        )
        for i, (low, high) in enumerate(zip(bounds, bounds[1:]))
    ]
    forms_copy = pltpu.make_async_copy(forms_hbm, forms, arrived.at[len(copies)])
    for copy in copies + [forms_copy]:
        copy.start()
    for member in range(CORES):
        unpack(packed_ref.at[member], blocks, lambda i: member * KL + i)
    for k in range(0, KL, 2):
        clear_halves(products, k, 0)
        clear_halves(products, k + 1, CHIP)
    for shift in range(SHIFTS):
        if shift in bounds:
            copies[bounds.index(shift)].wait()
        low = max(0, KL - 1 - shift)
        high = min(KL, SHIFTS - shift)
        halves = half_products(blocks, low + shift - (KL - 1), high - low, factors[shift])
        for k in range(low, high):
            place_halves(products, k, shift - (KL - 2 - k // 2 * 2), halves[(k - low) * N : (k - low + 1) * N, :])
    for pair in range(KL // 2):
        first = KL - 2 - 2 * pair
        result = second_product(products, pair, [factors[first + slot] for slot in range(CHIP + 1)])
        for member in range(2):
            exchange_ref[2 * pair + member] = result[:, member * N : (member + 1) * N]
    forms_copy.wait()
    for j in range(forms.shape[0]):
        rows[j : j + 1, :] = jnp.sum(sum_ref[...] * forms[j].astype(F32), axis=0, keepdims=True)
    charge_ref[...] = lane_sums(rows[...])


def near_kernel(packed_ref, factors_ref, inner_ref, hamiltonian_ref, partial_ref, blocks, products):
    flipped = lax.rem(lax.axis_index("ka"), CORES) == 1
    last = 2 * SPAN
    for member in range(CORES):
        unpack(packed_ref.at[member], blocks, lambda i: jnp.where(flipped, CHIP - 1 - member * KL - i, member * KL + i))
    factors = [factors_ref.at[jnp.where(flipped, last - distance, distance)] for distance in range(CHIP)]
    for k in range(0, KL, 2):
        clear_halves(products, k + 1, CHIP - 1 - k)
    for distance in range(CHIP):
        high = min(KL, CHIP - distance)
        halves = half_products(blocks, distance, high, factors[distance][...])
        for k in range(high):
            place_halves(products, k, distance, halves[k * N : (k + 1) * N, :])
    for pair in range(KL // 2):
        result = second_product(products, pair, factors[: CHIP - 2 * pair])
        for member in range(2):
            k = 2 * pair + member
            k = jnp.where(flipped, KL - 1 - k, k)
            partial_ref[k] = hamiltonian_ref[k] - inner_ref[k] - result[:, member * N : (member + 1) * N]


def far_kernel(
    packed_ref, factors_ref, partial_ref, forms_ref, charge_ref, level_ref, stats_ref,
    blocks, products, traceless, rows,
):
    core = lax.rem(lax.axis_index("ka"), CORES)
    flipped = core == 1
    last = 2 * SPAN
    unpack(packed_ref.at[core], blocks, lambda i: jnp.where(flipped, KL - 1 - i, i))
    factors = [factors_ref.at[jnp.where(flipped, distance, last - distance)] for distance in range(KL)]
    for k in range(0, KL, 2):
        clear_halves(products, k, k + 1)
    for distance in range(KL):
        halves = half_products(blocks, 0, KL - distance, factors[distance][...])
        for k in range(distance, KL):
            place_halves(products, k, distance, halves[(k - distance) * N : (k - distance + 1) * N, :])
    row, col = square_iota()
    lane = lax.broadcasted_iota(jnp.int32, (1, N), 1)
    form_count = forms_ref.shape[0]
    numbers = jnp.zeros((1, N), F32)
    for pair in range(KL // 2):
        result = second_product(products, pair, factors[: 2 * pair + 2])
        for member in range(2):
            k = 2 * pair + member
            k = jnp.where(flipped, KL - 1 - k, k)
            combined = partial_ref[k] - result[:, member * N : (member + 1) * N]
            level = 0.5 * (combined + combined.T)
            level_ref[k] = level
            mean = jnp.sum(jnp.where(row == col, level, 0.0), keepdims=True) / N
            rest = level - jnp.where(row == col, mean, 0.0)
            traceless[k] = rest
            norm = jnp.sum(rest * rest, keepdims=True)
            numbers = jnp.where(lane == form_count + k, norm, numbers)
            numbers = jnp.where(lane == form_count + KL + k, mean, numbers)

    group = 4

    def overlaps(step, carry):
        sums = [[jnp.zeros((8, N), F32) for _ in range(group)] for _ in range(KL)]
        for part in range(N // 16):
            forms = [forms_ref[step * group + j, part * 16 : (part + 1) * 16, :].astype(F32) for j in range(group)]
            for k in range(KL):
                upper = traceless[k, part * 16 : part * 16 + 8, :]
                lower = traceless[k, part * 16 + 8 : part * 16 + 16, :]
                for j in range(group):
                    sums[k][j] = sums[k][j] + upper * forms[j][:8] + lower * forms[j][8:]
        for k in range(KL):
            for j in range(group):
                rows[pl.ds(k * form_count + step * group + j, 1), :] = jnp.sum(sums[k][j], axis=0, keepdims=True)
        return carry

    lax.fori_loop(0, form_count // group, overlaps, 0)
    charge = jnp.concatenate([charge_ref[0:1, :], jnp.zeros((1, N - form_count), F32)], axis=1)
    stats = jnp.concatenate([lane_sums(rows[...])[0:1, :], numbers + charge], axis=1)
    stats_ref[...] = jnp.broadcast_to(stats, stats_ref.shape)


def final_kernel(stats_ref, level_ref, forms_ref, coupling_ref, occupations_ref, fock_ref, density_ref):
    form_count = forms_ref.shape[0]
    count = stats_ref.shape[0]
    total = count * KL
    overlap_count = KL * form_count
    charge = jnp.sum(stats_ref[:, overlap_count : overlap_count + form_count], axis=0, keepdims=True) / total
    weights = coupling_ref[...] * charge
    row, col = square_iota()
    hartree = jnp.zeros((N, N), F32)
    for j in range(form_count):
        hartree = hartree + weights[:, j : j + 1] * forms_ref[j].astype(F32)
    hartree = 0.5 * (hartree + hartree.T)
    offset = jnp.sum(jnp.where(row == col, hartree, 0.0), keepdims=True) / N
    traceless = hartree - jnp.where(row == col, offset, 0.0)
    own = jnp.sum(traceless * traceless, keepdims=True)
    norms_at = overlap_count + form_count
    means = stats_ref[:, norms_at + KL : norms_at + 2 * KL]
    mean = jnp.sum(means, keepdims=True) / total
    cross = [
        jnp.sum(stats_ref[:, k * form_count : (k + 1) * form_count] * weights, axis=1, keepdims=True)
        for k in range(KL)
    ]
    cross = jnp.concatenate(cross, axis=1)
    norms = stats_ref[:, norms_at : norms_at + KL] + 2.0 * cross + own + N * (means - mean) ** 2
    radius = jnp.sqrt(1e-06 + jnp.max(norms, keepdims=True))
    scale = 0.5 / radius
    shift = offset + mean
    eye = jnp.where(row == col, 1.0, 0.0).astype(F32)
    current = []
    for k in range(KL):
        fock = level_ref[k] + hartree
        fock_ref[k] = fock
        filling = occupations_ref[k].astype(F32) / N - 0.5
        current.append((filling + scale * shift) * eye - scale * fock)
    for _ in range(NPUR):
        for k in range(KL):
            short = current[k].astype(BF16)
            square = jnp.dot(short, short, preferred_element_type=F32).astype(BF16)
            cube = jnp.dot(square, short, preferred_element_type=F32)
            current[k] = 1.5 * current[k] - 2.0 * cube
    for k in range(KL):
        density_ref[k] = current[k] + 0.5 * eye


def per_device(density, hamiltonian, occupations, form_factors, hartree_forms, coupling):
    kpoint_count = density.shape[0]
    count = lax.axis_size("ka")
    form_count = hartree_forms.shape[0]
    assert kpoint_count == KL and CHIP == SPAN and count % CORES == 0
    shape = jax.ShapeDtypeStruct
    chips = [list(range(first, first + CORES)) for first in range(0, count, CORES)]
    packed, deviation_sum = pl.pallas_call(
        pack_kernel,
        out_shape=(shape((PACK, N), BF16), shape((N, N), F32)),
        in_specs=[ANY],
        out_specs=(VMEM, VMEM),
        scratch_shapes=[pltpu.VMEM((KL, N, N), F32), pltpu.SemaphoreType.DMA((KL,))],
        compiler_params=params(16),
    )(density)
    own_chip = lax.all_gather(packed, "ka", axis_index_groups=chips)
    pairs = [(d, (d + CORES) % count if d % CORES == 0 else (d - CORES) % count) for d in range(count)]
    neighbour = lax.ppermute(own_chip, "ka", pairs)
    inner, charge = pl.pallas_call(
        inner_kernel,
        out_shape=(shape((KL, N, N), F32), shape((8, form_count), F32)),
        in_specs=[VMEM, ANY, VMEM, ANY],
        out_specs=(VMEM, VMEM),
        scratch_shapes=[
            pltpu.VMEM((SHIFTS, 2, N, N), BF16),
            pltpu.VMEM((form_count, N, N), BF16),
            pltpu.VMEM((CHIP, N, N), BF16),
            pltpu.VMEM((KL // 2, (CHIP + 1) * 2 * N, 2 * N), BF16),
            pltpu.VMEM((form_count, N), F32),
            pltpu.SemaphoreType.DMA((5,)),
        ],
        compiler_params=params(28),
        cost_estimate=pl.CostEstimate(flops=5 * 10**9, bytes_accessed=5 * 10**6, transcendentals=0),
    )(own_chip, form_factors, deviation_sum, hartree_forms)
    other_side = lax.ppermute(neighbour, "ka", [(d, d ^ 1) for d in range(count)])
    partial = pl.pallas_call(
        near_kernel,
        out_shape=shape((KL, N, N), F32),
        in_specs=[VMEM] * 4,
        out_specs=VMEM,
        scratch_shapes=[
            pltpu.VMEM((CHIP, N, N), BF16),
            pltpu.VMEM((KL // 2, CHIP * 2 * N, 2 * N), BF16),
        ],
        compiler_params=params(24),
        cost_estimate=pl.CostEstimate(flops=4 * 10**9, bytes_accessed=5 * 10**6, transcendentals=0),
    )(neighbour, form_factors, inner, hamiltonian)
    level, stats = pl.pallas_call(
        far_kernel,
        out_shape=(shape((KL, N, N), F32), shape((count, KL * form_count + N), F32)),
        in_specs=[VMEM] * 5,
        out_specs=(VMEM, VMEM),
        scratch_shapes=[
            pltpu.VMEM((KL, N, N), BF16),
            pltpu.VMEM((KL // 2, KL * 2 * N, 2 * N), BF16),
            pltpu.VMEM((KL, N, N), F32),
            pltpu.VMEM((KL * form_count, N), F32),
        ],
        compiler_params=params(24),
    )(other_side, form_factors, partial, hartree_forms, charge)
    shared = lax.all_to_all(stats, "ka", 0, 0, tiled=True)
    return pl.pallas_call(
        final_kernel,
        out_shape=(shape((KL, N, N), F32), shape((KL, N, N), F32)),
        in_specs=[VMEM] * 4 + [SMEM],
        out_specs=(VMEM, VMEM),
        compiler_params=params(24),
    )(shared, level, hartree_forms, coupling.reshape(1, form_count), occupations)


def solution(mesh):
    placed = (P("ka", None, None), P("ka", None, None), P("ka"), P(), P(), P())
    return jax.shard_map(
        per_device,
        mesh=mesh,
        in_specs=placed,
        out_specs=(P("ka", None, None), P("ka", None, None)),
        check_vma=False,
    )
```

time: 45.7 us -> 41 us (0.90)
  blocking collectives: 14.2 us -> 11.1 us
  Pallas kernels: 19.8 us -> 18.2 us
    ppermute x1, starting transfers between devices: 6.84 us -> 2.85 us  [per_device(): neighbour = lax.ppermute(own_chip, 'ka', pairs)]
    ppermute x0 -> x1, starting transfers between devices: none -> 3.93 us  [per_device(): lax.ppermute(neighbour, 'ka', [(d, d ^ 1) for d in range(count)])]
    pallas_call x2 -> x3, Pallas kernels: 15.8 us -> 12.7 us  [the longest x1 5.58 us: per_device(): pl.pallas_call(inner_kernel, out_shape=(shape((KL, N, N), F32), shape((8,...]
    all_gather x1 -> x0, blocking collectives: 2.19 us -> none  [per_device(): outside = lax.all_gather(neighbour, 'ka', axis_index_groups=chips)]
    pallas_call x1, Pallas kernels: 0.17 us -> 1.61 us  [per_device(): pl.pallas_call(pack_kernel, out_shape=(shape((PACK, N), BF16), shape((N,...]
    all_to_all x1, blocking collectives: 9.93 us -> 9.03 us  [per_device(): shared = lax.all_to_all(stats, 'ka', 0, 0, tiled=True)]
    unnamed x16 -> x15, local copies, waits for them, and re-layouts: 3.89 us -> 3.89 us
  transfers between devices with their start and end apart: 1 -> 2, of which waited for: 0 -> 0; matrix products, arithmetic and copies ran while one was open for 0% -> 0% of each run, Pallas kernels for 14% -> 21%
where the time goes in v2:
time: 41 us; the launch traced here: 40.8 us
  Pallas kernels  18.2 us (44%)
  blocking collectives  11.1 us (27%)
  starting transfers between devices  6.77 us (17%)
  local copies, waits for them, and re-layouts  3.97 us (10%)
  between operations  0.72 us (2%)
    all_to_all x1, blocking collectives, per_device(): shared = lax.all_to_all(stats, 'ka', 0, 0, tiled=True)  9.03 us
    pallas_call x1, Pallas kernels, per_device(): pl.pallas_call(inner_kernel, out_shape=(shape((KL, N, N), F32), shape((8,...  5.58 us
    pallas_call x1, Pallas kernels, per_device(): pl.pallas_call(far_kernel, out_shape=(shape((KL, N, N), F32), shape((coun...  4.01 us
    ppermute x1, starting transfers between devices, per_device(): lax.ppermute(neighbour, 'ka', [(d, d ^ 1) for d in range(count)])  3.93 us
    unnamed x15, local copies, waits for them, and re-layouts  3.89 us
    pallas_call x1, Pallas kernels, per_device(): pl.pallas_call(final_kernel, out_shape=(shape((KL, N, N), F32), shape((KL...  3.87 us
    pallas_call x1, Pallas kernels, per_device(): pl.pallas_call(near_kernel, out_shape=shape((KL, N, N), F32), in_specs=[V...  3.1 us
    ppermute x1, starting transfers between devices, per_device(): neighbour = lax.ppermute(own_chip, 'ka', pairs)  2.85 us
  transfers between devices with their start and end apart: 2, of which 0 were waited for; matrix products, arithmetic and copies ran while one was open for 0% of the time, Pallas kernels for 21%

profile of v2, /device:TPU:0, one launch (start us, length us, event | category | flops | bytes accessed | tf_op | source)
XLA Modules:
  0.0 40.8 jit_solution(6252379384288189071)
XLA Ops:
  0.6 0.0 copy-start.3
  0.6 1.0 %copy-done.3 = f32[8,128,128]{2,1,0:T(8,128)S(1)} copy-done((f32[8,128,128]{2,1,0:T(8,128)S(1)}, f32[8,128,128]{2,1,0:T(8,128)}, u32[]{:S(2)}) %copy-start.3) | copy-done | bytes 524312
  1.7 1.6 %shard_map.77 = (bf16[528,128]{1,0:T(8,128)(2,1)S(1)}, f32[128,128]{1,0:T(8,128)S(1)}) custom-call(f32[8,128,128]{2,1,0:T(8,128)S(1)} %copy-done.3), custom_call_target="tpu_custom_call" | custom-call | tf_op jit(solution)/shard_map/pallas_call | solution.py:263
  3.3 2.1 %all-gather = bf16[1056,128]{1,0:T(8,128)(2,1)S(1)} all-gather(bf16[528,128]{1,0:T(8,128)(2,1)S(1)} %get-tuple-element.8), channel_id=2, replica_groups={{0,1},{2,3},{4,5},{6,7},{8,9},{10,11},{12,13},{14,15},{16,17},{18,19},{..., dimensions={0}, use_global_device_ids=true | all-gather | bytes 405504 | tf_op jit(solution)/shard_map/all_gather | solution.py:271
  5.4 2.8 %collective-permute-start = (bf16[2,528,128]{2,1,0:T(8,128)(2,1)S(1)}, bf16[2,528,128]{2,1,0:T(8,128)(2,1)S(1)}, u32[]{:S(2)}, u32[]{:S(2)}) collective-permute-start(bf16[2,528,128]{2,1,0:T(8,128)(2,1)S(1)} %bitcast.6), channel_id=1, source_target_pairs={{0,2},{1,31},{2,4},{3,1},{4,6},{5,3},{6,8},{7,5},{8,10},{9,7},{10,... | collective-permute-start | bytes 811016 | tf_op jit(solution)/shard_map/ppermute | solution.py:273
  8.2 0.0 copy-start
  8.2 1.2 %copy-done = bf16[32,128,128]{2,1,0:T(8,128)(2,1)S(1)} copy-done((bf16[32,128,128]{2,1,0:T(8,128)(2,1)S(1)}, bf16[32,128,128]{2,1,0:T(8,128)(2,1)}, u32[]{:S(2)}) %copy-start) | copy-done | bytes 1048600
  9.5 0.0 copy-start.1
  9.5 1.6 %copy-done.1 = bf16[33,2,128,128]{3,2,1,0:T(8,128)(2,1)S(1)} copy-done((bf16[33,2,128,128]{3,2,1,0:T(8,128)(2,1)S(1)}, bf16[33,2,128,128]{3,2,1,0:T(8,128)(2,1)}, u32[]{:S(2)}) %copy-start.1) | copy-done | bytes 2162712
  11.1 0.0 copy-start.6
  11.1 5.6 %shard_map.78 = (f32[8,128,128]{2,1,0:T(8,128)S(1)}, f32[8,32]{1,0:T(8,128)S(1)}) custom-call(bf16[2,528,128]{2,1,0:T(8,128)(2,1)S(1)} %bitcast.7, bf16[33,2,128,128]{3,2,1,0:T(8,128)(2,1)S(1)} %copy-done.1, f32[128,128]{1,0:T(8,128)S(1)} %get-tuple-element.9.sum_ref, bf16[32,128,128]{2,1,0:T(8,128)(2,1)S(1)} %copy-done), custom_call_target="tpu_custom_call" | custom-call | flops 5000000000 | bytes 5000000 | tf_op jit(solution)/shard_map/pallas_call | solution.py:274
  16.7 0.0 collective-permute-done.packed_ref
  16.7 3.9 %collective-permute-start.1 = (bf16[2,528,128]{2,1,0:T(8,128)(2,1)S(1)}, bf16[2,528,128]{2,1,0:T(8,128)(2,1)S(1)}, u32[]{:S(2)}, u32[]{:S(2)}) collective-permute-start(bf16[2,528,128]{2,1,0:T(8,128)(2,1)S(1)} %collective-permute-done.packed_ref), channel_id=1, source_target_pairs={{0,1},{1,0},{2,3},{3,2},{4,5},{5,4},{6,7},{7,6},{8,9},{9,8},{10,11... | collective-permute-start | bytes 811016 | tf_op jit(solution)/shard_map/ppermute | solution.py:290
  20.6 0.0 copy-done.6
  20.6 0.0 copy-start.2
  20.6 3.1 %shard_map.79.partial_ref = f32[8,128,128]{2,1,0:T(8,128)S(1)} custom-call(bf16[2,528,128]{2,1,0:T(8,128)(2,1)S(1)} %collective-permute-done.packed_ref, bf16[33,2,128,128]{3,2,1,0:T(8,128)(2,1)S(1)} %copy-done.1, f32[8,128,128]{2,1,0:T(8,128)S(1)} %get-tuple-element.10.inner_ref, f32[8,128,128]{2,1,0:T(8,128)S(1)} %copy-done.6), custom_call_target="tpu_custom_call" | custom-call | flops 4000000000 | bytes 5000000 | tf_op jit(solution)/shard_map/pallas_call | solution.py:291
  23.7 0.0 copy-start.4
  23.7 0.0 copy-start.5
  23.7 0.0 collective-permute-done.1.packed_ref
  23.7 0.0 copy-done.2
  23.8 4.0 %shard_map.80 = (f32[8,128,128]{2,1,0:T(8,128)S(1)}, f32[32,384]{1,0:T(8,128)S(1)}) custom-call(bf16[2,528,128]{2,1,0:T(8,128)(2,1)S(1)} %collective-permute-done.1.packed_ref, bf16[33,2,128,128]{3,2,1,0:T(8,128)(2,1)S(1)} %copy-done.2, f32[8,128,128]{2,1,0:T(8,128)S(1)} %shard_map.79.partial_ref, bf16[32,128,128]{2,1,0:T(8,128)(2,1)S(1)} %copy-done, ...), custom_call_target="tpu_custom_call" | custom-call | tf_op jit(solution)/shard_map/pallas_call | solution.py:303
  27.8 0.1 copy.8
  27.8 9.0 %all_to_all.11 = f32[32,1,384]{2,1,0:T(1,128)S(1)} all-to-all(f32[32,1,384]{2,1,0:T(1,128)S(1)} %copy.8), channel_id=1, replica_groups=mesh['ka'=32] {'ka'}, dimensions={0} | all-to-all | bytes 98304 | tf_op jit(solution)/shard_map/all_to_all | solution.py:316
  36.9 0.0 copy-done.4
  36.9 0.0 copy-done.5
  36.9 3.9 %shard_map.81 = (f32[8,128,128]{2,1,0:T(8,128)}, f32[8,128,128]{2,1,0:T(8,128)}) custom-call(f32[32,384]{1,0:T(8,128)S(1)} %bitcast.8, f32[8,128,128]{2,1,0:T(8,128)S(1)} %get-tuple-element.13.level_ref, bf16[32,128,128]{2,1,0:T(8,128)(2,1)S(1)} %copy-done, f32[1,32]{1,0:T(1,128)S(1)} %bitcast.10, s32[8]{0:T(128)S(1)} %copy-done.5), custom_call_target="tpu_custom_call" | custom-call | tf_op jit(solution)/shard_map/pallas_call | solution.py:317
  (1 shorter events, 0.0 us)
Async XLA Ops:
  0.6 1.0 %copy-start.3 = (f32[8,128,128]{2,1,0:T(8,128)S(1)}, f32[8,128,128]{2,1,0:T(8,128)}, u32[]{:S(2)}) copy-start(f32[8,128,128]{2,1,0:T(8,128)} %density_hbm.1) | copy-start | bytes 1572868
  5.4 11.3 %collective-permute-start = (bf16[2,528,128]{2,1,0:T(8,128)(2,1)S(1)}, bf16[2,528,128]{2,1,0:T(8,128)(2,1)S(1)}, u32[]{:S(2)}, u32[]{:S(2)}) collective-permute-start(bf16[2,528,128]{2,1,0:T(8,128)(2,1)S(1)} %bitcast.6), channel_id=1, source_target_pairs={{0,2},{1,31},{2,4},{3,1},{4,6},{5,3},{6,8},{7,5},{8,10},{9,7},{10,... | collective-permute-start | bytes 811016 | tf_op jit(solution)/shard_map/ppermute | solution.py:273
  8.2 1.2 %copy-start = (bf16[32,128,128]{2,1,0:T(8,128)(2,1)S(1)}, bf16[32,128,128]{2,1,0:T(8,128)(2,1)}, u32[]{:S(2)}) copy-start(bf16[32,128,128]{2,1,0:T(8,128)(2,1)} %forms_ref.3) | copy-start | bytes 3145732
  9.5 1.6 %copy-start.1 = (bf16[33,2,128,128]{3,2,1,0:T(8,128)(2,1)S(1)}, bf16[33,2,128,128]{3,2,1,0:T(8,128)(2,1)}, u32[]{:S(2)}) copy-start(bf16[33,2,128,128]{3,2,1,0:T(8,128)(2,1)} %factors_ref.3) | copy-start | bytes 6488068
  11.1 9.5 %copy-start.6 = (f32[8,128,128]{2,1,0:T(8,128)S(1)}, f32[8,128,128]{2,1,0:T(8,128)}, u32[]{:S(2)}) copy-start(f32[8,128,128]{2,1,0:T(8,128)} %hamiltonian_ref.1) | copy-start | bytes 1572868
  16.7 7.1 %collective-permute-start.1 = (bf16[2,528,128]{2,1,0:T(8,128)(2,1)S(1)}, bf16[2,528,128]{2,1,0:T(8,128)(2,1)S(1)}, u32[]{:S(2)}, u32[]{:S(2)}) collective-permute-start(bf16[2,528,128]{2,1,0:T(8,128)(2,1)S(1)} %collective-permute-done.packed_ref), channel_id=1, source_target_pairs={{0,1},{1,0},{2,3},{3,2},{4,5},{5,4},{6,7},{7,6},{8,9},{9,8},{10,11... | collective-permute-start | bytes 811016 | tf_op jit(solution)/shard_map/ppermute | solution.py:290
  20.6 3.2 %copy-start.2 = (bf16[33,2,128,128]{3,2,1,0:T(8,128)(2,1)S(1)}, bf16[33,2,128,128]{3,2,1,0:T(8,128)(2,1)}, u32[]{:S(2)}) copy-start(bf16[33,2,128,128]{3,2,1,0:T(8,128)(2,1)} %factors_ref.3) | copy-start | bytes 6488068
  23.7 13.2 %copy-start.4 = (f32[32]{0:T(128)S(1)}, f32[32]{0:T(128)}, u32[]{:S(2)}) copy-start(f32[32]{0:T(128)} %param.11) | copy-start | bytes 388
  23.7 13.2 %copy-start.5 = (s32[8]{0:T(128)S(1)}, s32[8]{0:T(128)}, u32[]{:S(2)}) copy-start(s32[8]{0:T(128)} %occupations_ref.1) | copy-start | bytes 100

commit v3 on v2

v3 whole, which is shorter than its diff:
```python
import functools

import jax
import jax.numpy as jnp
from jax import lax
from jax.experimental import pallas as pl
from jax.experimental.pallas import tpu as pltpu
from jax.sharding import PartitionSpec as P

SPAN = 16
NPUR = 6
N = 128
KL = 8
CORES = 2
CHIP = CORES * KL
PACK = KL // 2 * N + 16
SHIFTS = CHIP + KL - 1
F32 = jnp.float32
BF16 = jnp.bfloat16
VMEM = pl.BlockSpec(memory_space=pltpu.VMEM)
SMEM = pl.BlockSpec(memory_space=pltpu.SMEM)
HBM = pl.BlockSpec(memory_space=pltpu.HBM)
LANES_LAST = (((1,), (1,)), ((), ()))


def square_iota():
    row = lax.broadcasted_iota(jnp.int32, (N, N), 0)
    col = lax.broadcasted_iota(jnp.int32, (N, N), 1)
    return row, col


def in_hbm(array):
    return pltpu.with_memory_space_constraint(array, pltpu.HBM)


def params(mib):
    return pltpu.CompilerParams(vmem_limit_bytes=mib << 20)


def lane_sums(rows):
    return lax.dot_general(
        jnp.ones((8, N), F32), rows, LANES_LAST, precision=lax.Precision.HIGHEST, preferred_element_type=F32
    )


def pack_kernel(density_hbm, packed_ref, sum_ref, density, arrived):
    copy = pltpu.make_async_copy(density_hbm, density, arrived)
    copy.start()
    row, col = square_iota()
    half_eye = jnp.where(row == col, 0.5, 0.0).astype(F32)
    total = jnp.zeros((N, N), F32)
    diagonals = []
    copy.wait()
    for pair in range(KL // 2):
        parts = []
        for member in range(2):
            deviation = (density[2 * pair + member] - half_eye).astype(BF16).astype(F32)
            total = total + deviation
            parts.append(0.5 * (deviation + deviation.T))
        packed_ref[pair * N : (pair + 1) * N, :] = jnp.where(row <= col, parts[0], parts[1]).astype(BF16)
        diagonals.append(jnp.sum(jnp.where(row == col, parts[1], 0.0), axis=0, keepdims=True))
    diagonals.append(jnp.zeros((16 - KL // 2, N), F32))
    packed_ref[KL // 2 * N :, :] = jnp.concatenate(diagonals, axis=0).astype(BF16)
    sum_ref[...] = total


def unpack(load, blocks, place):
    row, col = square_iota()
    diagonals = load(KL // 2 * N, PACK)
    for pair in range(KL // 2):
        both = load(pair * N, (pair + 1) * N)
        flipped = both.T
        blocks[place(2 * pair)] = jnp.where(row <= col, both, flipped).astype(BF16)
        second = jnp.where(row > col, both, jnp.where(row < col, flipped, diagonals[pair : pair + 1, :]))
        blocks[place(2 * pair + 1)] = second.astype(BF16)


def own_sum_is_even():
    index = lax.axis_index("ka")
    return lax.rem(index // CORES + index, 2) == 0


def rows_of(packed_ref):
    return lambda low, high: packed_ref[low:high, :].astype(F32)


def rows_of_either(choice, first_ref, second_ref):
    return lambda low, high: jnp.where(
        choice, first_ref[low:high, :].astype(F32), second_ref[low:high, :].astype(F32)
    )


def half_products(blocks, first, count, factor):
    left = blocks[first : first + count].reshape(count * N, N)
    return lax.dot_general(left, factor.reshape(2 * N, N), LANES_LAST, preferred_element_type=F32).astype(BF16)


def place_halves(products, k, slot, piece):
    lanes = slice(k % 2 * N, (k % 2 + 1) * N)
    for term in range(2):
        products[k // 2, (2 * slot + term) * N : (2 * slot + term + 1) * N, lanes] = piece[:, term * N : (term + 1) * N]


def clear_halves(products, k, slot):
    lanes = slice(k % 2 * N, (k % 2 + 1) * N)
    products[k // 2, 2 * slot * N : (2 * slot + 2) * N, lanes] = jnp.zeros((2 * N, N), BF16)


def second_product(products, pair, factors):
    left = jnp.concatenate([factor[term] for factor in factors for term in range(2)], axis=1)
    right = products[pair, : 2 * N * len(factors), :]
    return jnp.dot(left, right, preferred_element_type=F32)


def inner_kernel(
    own_ref, other_ref, factors_ref, hamiltonian_ref, sum_ref, forms_ref, partial_ref, charge_ref,
    blocks, products, rows,
):
    core = lax.rem(lax.axis_index("ka"), CORES)
    base = SPAN - (KL - 1) - KL * core
    factors = [factors_ref.at[base + shift] for shift in range(SHIFTS)]
    unpack(rows_of(own_ref), blocks, lambda i: core * KL + i)
    unpack(rows_of(other_ref), blocks, lambda i: (1 - core) * KL + i)
    for k in range(0, KL, 2):
        clear_halves(products, k, 0)
        clear_halves(products, k + 1, CHIP)
    for shift in range(SHIFTS):
        low = max(0, KL - 1 - shift)
        high = min(KL, SHIFTS - shift)
        halves = half_products(blocks, low + shift - (KL - 1), high - low, factors[shift][...])
        for k in range(low, high):
            place_halves(products, k, shift - (KL - 2 - k // 2 * 2), halves[(k - low) * N : (k - low + 1) * N, :])
    for pair in range(KL // 2):
        first = KL - 2 - 2 * pair
        result = second_product(products, pair, factors[first : first + CHIP + 1])
        for member in range(2):
            k = 2 * pair + member
            partial_ref[k] = hamiltonian_ref[k] - result[:, member * N : (member + 1) * N]
    for j in range(forms_ref.shape[0]):
        rows[j : j + 1, :] = jnp.sum(sum_ref[...] * forms_ref[j].astype(F32), axis=0, keepdims=True)
    charge_ref[...] = lane_sums(rows[...])


def first_side_kernel(block_ref, factors_ref, partial_ref, forms_ref, next_ref, turned_ref, blocks, products, wide):
    side_kernel(False, block_ref, factors_ref, partial_ref, next_ref, blocks, products)
    form_count = forms_ref.shape[0]
    for j in range(form_count):
        wide[j * N : (j + 1) * N, :] = forms_ref[j].astype(F32)
    for row in range(N):
        turned_ref[row] = wide[pl.ds(row, form_count, stride=N), :].astype(BF16)


def side_kernel(second, block_ref, factors_ref, partial_ref, next_ref, blocks, products):
    core = lax.rem(lax.axis_index("ka"), CORES)
    far = own_sum_is_even() != second
    flipped = (core == 1) == far
    last = 2 * SPAN
    unpack(rows_of(block_ref), blocks, lambda i: jnp.where(flipped, KL - 1 - i, i))
    factors = [factors_ref.at[jnp.where(flipped, distance, last - distance)] for distance in range(KL)]
    for k in range(0, KL, 2):
        clear_halves(products, k, k + 1)
    for distance in range(KL):
        halves = half_products(blocks, 0, KL - distance, factors[distance][...])
        for k in range(distance, KL):
            place_halves(products, k, distance, halves[(k - distance) * N : (k - distance + 1) * N, :])
    for pair in range(KL // 2):
        result = second_product(products, pair, factors[: 2 * pair + 2])
        for member in range(2):
            k = 2 * pair + member
            k = jnp.where(flipped, KL - 1 - k, k)
            next_ref[k] = partial_ref[k] - result[:, member * N : (member + 1) * N]


def last_kernel(
    even_ref, odd_ref, factors_ref, partial_ref, turned_ref, charge_ref, level_ref, stats_ref,
    blocks, products, diagonals, squares,
):
    flipped = lax.rem(lax.axis_index("ka"), CORES) == 1
    last = 2 * SPAN
    unpack(rows_of_either(own_sum_is_even(), odd_ref, even_ref), blocks, lambda i: jnp.where(flipped, KL - 1 - i, i))
    factors = [factors_ref.at[jnp.where(flipped, last - distance, distance)] for distance in range(CHIP)]
    for k in range(0, KL, 2):
        clear_halves(products, k, 0)
        clear_halves(products, k + 1, KL)
    for distance in range(1, CHIP):
        low = max(0, KL - distance)
        high = min(KL, CHIP - distance)
        halves = half_products(blocks, distance + low - KL, high - low, factors[distance][...])
        for k in range(low, high):
            place_halves(products, k, distance - (KL - 1 - k // 2 * 2), halves[(k - low) * N : (k - low + 1) * N, :])
    row, col = square_iota()
    for pair in range(KL // 2):
        first = KL - 1 - 2 * pair
        result = second_product(products, pair, factors[first : first + KL + 1])
        for member in range(2):
            k = 2 * pair + member
            k = jnp.where(flipped, KL - 1 - k, k)
            combined = partial_ref[k] - result[:, member * N : (member + 1) * N]
            level = 0.5 * (combined + combined.T)
            level_ref[pl.ds(pl.multiple_of(k * N, N), N), :] = level
            diagonals[pl.ds(k, 1), :] = jnp.sum(jnp.where(row == col, level, 0.0), axis=0, keepdims=True)
            outside = jnp.where(row == col, 0.0, level)
            squares[pl.ds(k, 1), :] = jnp.sum(outside * outside, axis=0, keepdims=True)

    mean = jnp.sum(diagonals[...], axis=1, keepdims=True) / N
    rest = diagonals[...] - mean
    norm = jnp.sum(squares[...] + rest * rest, axis=1, keepdims=True)
    form_count = turned_ref.shape[1]
    lane = lax.broadcasted_iota(jnp.int32, (KL, N), 1)
    place = lax.broadcasted_iota(jnp.int32, (KL, N), 0)
    chunk = 16
    dots = jnp.zeros((2 * KL, form_count), F32)
    for start in range(0, N, chunk):
        lefts, rights = [], []
        for at in range(start, start + chunk):
            values = level_ref[pl.ds(at, KL, stride=N), :]
            values = jnp.where(lane == at, values - mean, values)
            high = values.astype(BF16).astype(F32)
            lefts.append(jnp.concatenate([high, values - high], axis=0).astype(BF16))
            rights.append(turned_ref[at])
        dots = dots + lax.dot_general(
            jnp.concatenate(lefts, axis=1), jnp.concatenate(rights, axis=1), LANES_LAST, preferred_element_type=F32
        )
    overlaps = dots[:KL, :] + dots[KL:, :]
    numbers = jnp.where(lane == form_count + place, norm, 0.0)
    numbers = numbers + jnp.where(lane == form_count + KL + place, mean, 0.0)
    charge = jnp.concatenate([charge_ref[0:1, :], jnp.zeros((1, N - form_count), F32)], axis=1)
    numbers = jnp.sum(numbers, axis=0, keepdims=True) + charge
    stats = jnp.concatenate([overlaps[k : k + 1, :] for k in range(KL)] + [numbers], axis=1)
    stats_ref[...] = jnp.broadcast_to(stats, stats_ref.shape)


def final_kernel(
    stats_ref, level_ref, forms_ref, coupling_ref, occupations_ref, fock_hbm, density_hbm, fock, density, sent
):
    form_count = forms_ref.shape[0]
    count = stats_ref.shape[0]
    total = count * KL
    overlap_count = KL * form_count
    charge = jnp.sum(stats_ref[:, overlap_count : overlap_count + form_count], axis=0, keepdims=True) / total
    weights = coupling_ref[...] * charge
    row, col = square_iota()
    hartree = jnp.zeros((N, N), F32)
    for j in range(form_count):
        hartree = hartree + weights[:, j : j + 1] * forms_ref[j].astype(F32)
    hartree = 0.5 * (hartree + hartree.T)
    offset = jnp.sum(jnp.where(row == col, hartree, 0.0), keepdims=True) / N
    traceless = hartree - jnp.where(row == col, offset, 0.0)
    own = jnp.sum(traceless * traceless, keepdims=True)
    norms_at = overlap_count + form_count
    means = stats_ref[:, norms_at + KL : norms_at + 2 * KL]
    mean = jnp.sum(means, keepdims=True) / total
    cross = [
        jnp.sum(stats_ref[:, k * form_count : (k + 1) * form_count] * weights, axis=1, keepdims=True)
        for k in range(KL)
    ]
    cross = jnp.concatenate(cross, axis=1)
    norms = stats_ref[:, norms_at : norms_at + KL] + 2.0 * cross + own + N * (means - mean) ** 2
    radius = jnp.sqrt(1e-06 + jnp.max(norms, keepdims=True))
    scale = 0.5 / radius
    shift = offset + mean
    eye = jnp.where(row == col, 1.0, 0.0).astype(F32)
    current = []
    for k in range(KL):
        fock[k] = level_ref[k * N : (k + 1) * N, :] + hartree
        filling = occupations_ref[k].astype(F32) / N - 0.5
        current.append((filling + scale * shift) * eye - scale * fock[k])
    copies = [pltpu.make_async_copy(fock, fock_hbm, sent.at[0])]
    copies[0].start()
    for _ in range(NPUR):
        for k in range(KL):
            short = current[k].astype(BF16)
            square = jnp.dot(short, short, preferred_element_type=F32).astype(BF16)
            cube = jnp.dot(square, short, preferred_element_type=F32)
            current[k] = 1.5 * current[k] - 2.0 * cube
    for k in range(KL):
        density[k] = current[k] + 0.5 * eye
        if k % 2 == 1:
            ready = pl.ds(k - 1, 2)
            copies.append(pltpu.make_async_copy(density.at[ready], density_hbm.at[ready], sent.at[(k + 1) // 2]))
            copies[-1].start()
    for copy in copies:
        copy.wait()


def per_device(density, hamiltonian, occupations, form_factors, hartree_forms, coupling):
    kpoint_count = density.shape[0]
    count = lax.axis_size("ka")
    form_count = hartree_forms.shape[0]
    assert kpoint_count == KL and CHIP == SPAN and count % CORES == 0
    shape = jax.ShapeDtypeStruct
    packed, deviation_sum = pl.pallas_call(
        pack_kernel,
        out_shape=(shape((PACK, N), BF16), shape((N, N), F32)),
        in_specs=[HBM],
        out_specs=(VMEM, VMEM),
        scratch_shapes=[pltpu.VMEM((KL, N, N), F32), pltpu.SemaphoreType.DMA(())],
        compiler_params=params(16),
        cost_estimate=pl.CostEstimate(flops=5 * 10**9, bytes_accessed=2 * 10**6, transcendentals=0),
    )(in_hbm(density))
    across = [(d, d ^ 1) for d in range(count)]
    within = [(d, d ^ CORES) for d in range(count)]
    between = [(d, ((d + CORES) ^ CORES) - CORES) for d in range(count)]
    between = [(d, target % count) for d, target in between]
    other = lax.ppermute(packed, "ka", across)
    even = lax.ppermute(packed, "ka", within)
    packed, other = lax.optimization_barrier((packed, other))
    odd = lax.ppermute(packed, "ka", between)
    partial, charge = pl.pallas_call(
        inner_kernel,
        out_shape=(shape((KL, N, N), F32), shape((8, form_count), F32)),
        in_specs=[VMEM] * 6,
        out_specs=(VMEM, VMEM),
        scratch_shapes=[
            pltpu.VMEM((CHIP, N, N), BF16),
            pltpu.VMEM((KL // 2, (CHIP + 1) * 2 * N, 2 * N), BF16),
            pltpu.VMEM((form_count, N), F32),
        ],
        compiler_params=params(28),
        cost_estimate=pl.CostEstimate(flops=5 * 10**9, bytes_accessed=5 * 10**6, transcendentals=0),
    )(packed, other, form_factors, hamiltonian, deviation_sum, hartree_forms)

    side_scratch = [pltpu.VMEM((KL, N, N), BF16), pltpu.VMEM((KL // 2, KL * 2 * N, 2 * N), BF16)]
    side_cost = pl.CostEstimate(flops=2 * 10**9, bytes_accessed=5 * 10**6, transcendentals=0)
    partial, even = lax.optimization_barrier((partial, even))
    even_across = lax.ppermute(even, "ka", across)
    partial, turned = pl.pallas_call(
        first_side_kernel,
        out_shape=(shape((KL, N, N), F32), shape((N, form_count, N), BF16)),
        in_specs=[VMEM] * 4,
        out_specs=(VMEM, VMEM),
        scratch_shapes=side_scratch + [pltpu.VMEM((form_count * N, N), F32)],
        compiler_params=params(24),
        cost_estimate=side_cost,
    )(even, form_factors, partial, hartree_forms)
    partial, odd = lax.optimization_barrier((partial, odd))
    odd_across = lax.ppermute(odd, "ka", across)
    partial = pl.pallas_call(
        functools.partial(side_kernel, True),
        out_shape=shape((KL, N, N), F32),
        in_specs=[VMEM] * 3,
        out_specs=VMEM,
        scratch_shapes=side_scratch,
        compiler_params=params(24),
        cost_estimate=side_cost,
    )(odd, form_factors, partial)
    level, stats = pl.pallas_call(
        last_kernel,
        out_shape=(shape((KL * N, N), F32), shape((count, KL * form_count + N), F32)),
        in_specs=[VMEM] * 6,
        out_specs=(VMEM, VMEM),
        scratch_shapes=[
            pltpu.VMEM((KL, N, N), BF16),
            pltpu.VMEM((KL // 2, (KL + 1) * 2 * N, 2 * N), BF16),
            pltpu.VMEM((KL, N), F32),
            pltpu.VMEM((KL, N), F32),
        ],
        compiler_params=params(28),
    )(even_across, odd_across, form_factors, partial, turned, charge)
    shared = lax.all_to_all(stats, "ka", 0, 0, tiled=True)
    return pl.pallas_call(
        final_kernel,
        out_shape=(shape((KL, N, N), F32), shape((KL, N, N), F32)),
        in_specs=[VMEM] * 4 + [SMEM],
        out_specs=(HBM, HBM),
        scratch_shapes=[pltpu.VMEM((KL, N, N), F32), pltpu.VMEM((KL, N, N), F32), pltpu.SemaphoreType.DMA((1 + KL // 2,))],
        compiler_params=params(24),
    )(shared, level, hartree_forms, coupling.reshape(1, form_count), occupations)


def solution(mesh):
    placed = (P("ka", None, None), P("ka", None, None), P("ka"), P(), P(), P())
    return jax.shard_map(
        per_device,
        mesh=mesh,
        in_specs=placed,
        out_specs=(P("ka", None, None), P("ka", None, None)),
        check_vma=False,
    )
```

time: 41 us -> 36.2 us (0.88)
  local copies, waits for them, and re-layouts: 3.97 us -> 0.11 us
  starting transfers between devices: 6.77 us -> 8.93 us
  Pallas kernels: 18.2 us -> 16.2 us
  blocking collectives: 11.1 us -> 10.1 us
    unnamed x15 -> x11, local copies, waits for them, and re-layouts: 3.89 us -> 0.03 us
    ppermute x2 -> x5, starting transfers between devices: 6.77 us -> 8.93 us  [the longest x1 5.27 us: per_device(): odd = lax.ppermute(packed, 'ka', between)]
    all_gather x1 -> x0, blocking collectives: 2.09 us -> none  [per_device(): own_chip = lax.all_gather(packed, 'ka', axis_index_groups=chips)]
    pallas_call x1, Pallas kernels: 5.58 us -> 4.05 us  [per_device(): pl.pallas_call(inner_kernel, out_shape=(shape((KL, N, N), F32), shape((8,...]
    all_to_all x1, blocking collectives: 9.03 us -> 10.1 us  [per_device(): shared = lax.all_to_all(stats, 'ka', 0, 0, tiled=True)]
    pallas_call x2 -> x3, Pallas kernels: 7.11 us -> 6.97 us  [the longest x1 3.31 us: per_device(): pl.pallas_call(last_kernel, out_shape=(shape((KL * N, N), F32), shape((co...]
  transfers between devices with their start and end apart: 2 -> 5, of which waited for: 0 -> 0; matrix products, arithmetic and copies ran while one was open for 0% -> 0% of each run, Pallas kernels for 21% -> 21%
where the time goes in v3:
time: 36.2 us; the launch traced here: 36 us
  Pallas kernels  16.2 us (45%)
  blocking collectives  10.1 us (28%)
  starting transfers between devices  8.93 us (25%)
  between operations  0.74 us (2%)
    all_to_all x1, blocking collectives, per_device(): shared = lax.all_to_all(stats, 'ka', 0, 0, tiled=True)  10.1 us
    ppermute x1, starting transfers between devices, per_device(): odd = lax.ppermute(packed, 'ka', between)  5.27 us
    pallas_call x1, Pallas kernels, per_device(): pl.pallas_call(inner_kernel, out_shape=(shape((KL, N, N), F32), shape((8,...  4.05 us
    pallas_call x1, Pallas kernels, per_device(): pl.pallas_call(final_kernel, out_shape=(shape((KL, N, N), F32), shape((KL...  3.8 us
    pallas_call x1, Pallas kernels, per_device(): pl.pallas_call(last_kernel, out_shape=(shape((KL * N, N), F32), shape((co...  3.31 us
    ppermute x1, starting transfers between devices, per_device(): even = lax.ppermute(packed, 'ka', within)  2.56 us
    pallas_call x1, Pallas kernels, per_device(): pl.pallas_call(first_side_kernel, out_shape=(shape((KL, N, N), F32), shap...  2.41 us
    pallas_call x1, Pallas kernels, per_device(): pl.pallas_call(pack_kernel, out_shape=(shape((PACK, N), BF16), shape((N,...  1.36 us
  transfers between devices with their start and end apart: 5, of which 0 were waited for; matrix products, arithmetic and copies ran while one was open for 0% of the time, Pallas kernels for 21%

profile of v3, /device:TPU:0, one launch (start us, length us, event | category | flops | bytes accessed | tf_op | source)
XLA Modules:
  0.0 36.0 jit_solution(9478152494360336666)
XLA Ops:
  0.6 0.0 copy-start.1
  0.6 0.0 copy-start.4
  0.7 0.0 copy-start
  0.7 1.4 %shard_map.77 = (bf16[528,128]{1,0:T(8,128)(2,1)S(1)}, f32[128,128]{1,0:T(8,128)S(1)}) custom-call(f32[8,128,128]{2,1,0:T(8,128)} %density_hbm.1), custom_call_target="tpu_custom_call" | custom-call | flops 5000000000 | bytes 2000000 | tf_op jit(solution)/shard_map/pallas_call | solution.py:292
  2.0 0.5 %collective-permute-start = (bf16[528,128]{1,0:T(8,128)(2,1)S(1)}, bf16[528,128]{1,0:T(8,128)(2,1)S(1)}, u32[]{:S(2)}, u32[]{:S(2)}) collective-permute-start(bf16[528,128]{1,0:T(8,128)(2,1)S(1)} %get-tuple-element.17.own_ref), channel_id=1, source_target_pairs={{0,1},{1,0},{2,3},{3,2},{4,5},{5,4},{6,7},{7,6},{8,9},{9,8},{10,11... | collective-permute-start | bytes 405512 | tf_op jit(solution)/shard_map/ppermute | solution.py:305
  2.5 2.6 %collective-permute-start.1 = (bf16[528,128]{1,0:T(8,128)(2,1)S(1)}, bf16[528,128]{1,0:T(8,128)(2,1)S(1)}, u32[]{:S(2)}, u32[]{:S(2)}) collective-permute-start(bf16[528,128]{1,0:T(8,128)(2,1)S(1)} %get-tuple-element.17.own_ref), channel_id=1, source_target_pairs={{0,2},{1,3},{2,0},{3,1},{4,6},{5,7},{6,4},{7,5},{8,10},{9,11},{10,... | collective-permute-start | bytes 405512 | tf_op jit(solution)/shard_map/ppermute | solution.py:306
  5.1 0.0 collective-permute-done.other_ref
  5.1 5.3 %collective-permute-start.3 = (bf16[528,128]{1,0:T(8,128)(2,1)S(1)}, bf16[528,128]{1,0:T(8,128)(2,1)S(1)}, u32[]{:S(2)}, u32[]{:S(2)}) collective-permute-start(bf16[528,128]{1,0:T(8,128)(2,1)S(1)} %get-tuple-element.17.own_ref), channel_id=1, source_target_pairs={{0,30},{1,31},{2,4},{3,5},{4,2},{5,3},{6,8},{7,9},{8,6},{9,7},{10,... | collective-permute-start | bytes 405512 | tf_op jit(solution)/shard_map/ppermute | solution.py:308
  10.4 0.0 copy-done.1
  10.4 0.0 copy-done.4
  10.4 0.0 copy-done
  10.4 4.0 %shard_map.78 = (f32[8,128,128]{2,1,0:T(8,128)S(1)}, f32[8,32]{1,0:T(8,128)S(1)}) custom-call(bf16[528,128]{1,0:T(8,128)(2,1)S(1)} %get-tuple-element.17.own_ref, bf16[528,128]{1,0:T(8,128)(2,1)S(1)} %collective-permute-done.other_ref, bf16[33,2,128,128]{3,2,1,0:T(8,128)(2,1)S(1)} %copy-done, f32[8,128,128]{2,1,0:T(8,128)S(1)} %copy-done.4, ...), custom_call_target="tpu_custom_call" | custom-call | flops 5000000000 | bytes 5000000 | tf_op jit(solution)/shard_map/pallas_call | solution.py:309
  14.4 0.0 collective-permute-done.1.block_ref
  14.4 0.0 collective-permute-start.2
  14.5 2.4 %shard_map.79 = (f32[8,128,128]{2,1,0:T(8,128)S(1)}, bf16[128,32,128]{2,1,0:T(8,128)(2,1)S(1)}) custom-call(bf16[528,128]{1,0:T(8,128)(2,1)S(1)} %collective-permute-done.1.block_ref, bf16[33,2,128,128]{3,2,1,0:T(8,128)(2,1)S(1)} %copy-done, f32[8,128,128]{2,1,0:T(8,128)S(1)} %get-tuple-element.22.partial_ref, bf16[32,128,128]{2,1,0:T(8,128)(2,1)S(1)} %copy-done.1), custom_call_target="tpu_custom_call" | custom-call | flops 2000000000 | bytes 5000000 | tf_op jit(solution)/shard_map/pallas_call | solution.py:327
  16.9 0.0 collective-permute-done.3.block_ref
  16.9 0.6 %collective-permute-start.4 = (bf16[528,128]{1,0:T(8,128)(2,1)S(1)}, bf16[528,128]{1,0:T(8,128)(2,1)S(1)}, u32[]{:S(2)}, u32[]{:S(2)}) collective-permute-start(bf16[528,128]{1,0:T(8,128)(2,1)S(1)} %collective-permute-done.3.block_ref), channel_id=1, source_target_pairs={{0,1},{1,0},{2,3},{3,2},{4,5},{5,4},{6,7},{7,6},{8,9},{9,8},{10,11... | collective-permute-start | bytes 405512 | tf_op jit(solution)/shard_map/ppermute | solution.py:337
  17.5 1.2 %shard_map.80.partial_ref = f32[8,128,128]{2,1,0:T(8,128)S(1)} custom-call(bf16[528,128]{1,0:T(8,128)(2,1)S(1)} %collective-permute-done.3.block_ref, bf16[33,2,128,128]{3,2,1,0:T(8,128)(2,1)S(1)} %copy-done, f32[8,128,128]{2,1,0:T(8,128)S(1)} %get-tuple-element.25.partial_ref), custom_call_target="tpu_custom_call" | custom-call | flops 2000000000 | bytes 5000000 | tf_op jit(solution)/shard_map/pallas_call | solution.py:338
  18.7 0.0 copy-start.2
  18.7 0.0 copy-start.3
  18.7 0.0 collective-permute-done.2.even_ref
  18.7 0.0 collective-permute-done.4.odd_ref
  18.8 3.3 %shard_map.81 = (f32[1024,128]{1,0:T(8,128)S(1)}, f32[32,384]{1,0:T(8,128)S(1)}) custom-call(bf16[528,128]{1,0:T(8,128)(2,1)S(1)} %collective-permute-done.2.even_ref, bf16[528,128]{1,0:T(8,128)(2,1)S(1)} %collective-permute-done.4.odd_ref, bf16[33,2,128,128]{3,2,1,0:T(8,128)(2,1)S(1)} %copy-done, f32[8,128,128]{2,1,0:T(8,128)S(1)} %shard_map.80.partial_ref, ...), custom_call_target="tpu_custom_call" | custom-call | tf_op jit(solution)/shard_map/pallas_call | solution.py:347
  22.1 0.1 copy.8
  22.2 10.1 %all_to_all.11 = f32[32,1,384]{2,1,0:T(1,128)S(1)} all-to-all(f32[32,1,384]{2,1,0:T(1,128)S(1)} %copy.8), channel_id=1, replica_groups=mesh['ka'=32] {'ka'}, dimensions={0} | all-to-all | bytes 98304 | tf_op jit(solution)/shard_map/all_to_all | solution.py:360
  32.2 0.0 copy-done.2
  32.2 0.0 copy-done.3
  32.2 3.8 %shard_map.82 = (f32[8,128,128]{2,1,0:T(8,128)}, f32[8,128,128]{2,1,0:T(8,128)}) custom-call(f32[32,384]{1,0:T(8,128)S(1)} %bitcast.5, f32[1024,128]{1,0:T(8,128)S(1)} %get-tuple-element.29.level_ref, bf16[32,128,128]{2,1,0:T(8,128)(2,1)S(1)} %copy-done.1, f32[1,32]{1,0:T(1,128)S(1)} %bitcast.7, s32[8]{0:T(128)S(1)} %copy-done.3), custom_call_target="tpu_custom_call" | custom-call | tf_op jit(solution)/shard_map/pallas_call | solution.py:361
  (1 shorter events, 0.0 us)
Async XLA Ops:
  0.6 9.8 %copy-start.1 = (bf16[32,128,128]{2,1,0:T(8,128)(2,1)S(1)}, bf16[32,128,128]{2,1,0:T(8,128)(2,1)}, u32[]{:S(2)}) copy-start(bf16[32,128,128]{2,1,0:T(8,128)(2,1)} %forms_ref.5) | copy-start | bytes 3145732
  0.6 9.7 %copy-start.4 = (f32[8,128,128]{2,1,0:T(8,128)S(1)}, f32[8,128,128]{2,1,0:T(8,128)}, u32[]{:S(2)}) copy-start(f32[8,128,128]{2,1,0:T(8,128)} %hamiltonian_ref.1) | copy-start | bytes 1572868
  0.7 9.7 %copy-start = (bf16[33,2,128,128]{3,2,1,0:T(8,128)(2,1)S(1)}, bf16[33,2,128,128]{3,2,1,0:T(8,128)(2,1)}, u32[]{:S(2)}) copy-start(bf16[33,2,128,128]{3,2,1,0:T(8,128)(2,1)} %factors_ref.7) | copy-start | bytes 6488068
  2.0 3.1 %collective-permute-start = (bf16[528,128]{1,0:T(8,128)(2,1)S(1)}, bf16[528,128]{1,0:T(8,128)(2,1)S(1)}, u32[]{:S(2)}, u32[]{:S(2)}) collective-permute-start(bf16[528,128]{1,0:T(8,128)(2,1)S(1)} %get-tuple-element.17.own_ref), channel_id=1, source_target_pairs={{0,1},{1,0},{2,3},{3,2},{4,5},{5,4},{6,7},{7,6},{8,9},{9,8},{10,11... | collective-permute-start | bytes 405512 | tf_op jit(solution)/shard_map/ppermute | solution.py:305
  2.5 11.9 %collective-permute-start.1 = (bf16[528,128]{1,0:T(8,128)(2,1)S(1)}, bf16[528,128]{1,0:T(8,128)(2,1)S(1)}, u32[]{:S(2)}, u32[]{:S(2)}) collective-permute-start(bf16[528,128]{1,0:T(8,128)(2,1)S(1)} %get-tuple-element.17.own_ref), channel_id=1, source_target_pairs={{0,2},{1,3},{2,0},{3,1},{4,6},{5,7},{6,4},{7,5},{8,10},{9,11},{10,... | collective-permute-start | bytes 405512 | tf_op jit(solution)/shard_map/ppermute | solution.py:306
  5.1 11.8 %collective-permute-start.3 = (bf16[528,128]{1,0:T(8,128)(2,1)S(1)}, bf16[528,128]{1,0:T(8,128)(2,1)S(1)}, u32[]{:S(2)}, u32[]{:S(2)}) collective-permute-start(bf16[528,128]{1,0:T(8,128)(2,1)S(1)} %get-tuple-element.17.own_ref), channel_id=1, source_target_pairs={{0,30},{1,31},{2,4},{3,5},{4,2},{5,3},{6,8},{7,9},{8,6},{9,7},{10,... | collective-permute-start | bytes 405512 | tf_op jit(solution)/shard_map/ppermute | solution.py:308
  14.4 4.3 %collective-permute-start.2 = (bf16[528,128]{1,0:T(8,128)(2,1)S(1)}, bf16[528,128]{1,0:T(8,128)(2,1)S(1)}, u32[]{:S(2)}, u32[]{:S(2)}) collective-permute-start(bf16[528,128]{1,0:T(8,128)(2,1)S(1)} %collective-permute-done.1.block_ref), channel_id=1, source_target_pairs={{0,1},{1,0},{2,3},{3,2},{4,5},{5,4},{6,7},{7,6},{8,9},{9,8},{10,11... | collective-permute-start | bytes 405512 | tf_op jit(solution)/shard_map/ppermute | solution.py:326
  16.9 1.8 %collective-permute-start.4 = (bf16[528,128]{1,0:T(8,128)(2,1)S(1)}, bf16[528,128]{1,0:T(8,128)(2,1)S(1)}, u32[]{:S(2)}, u32[]{:S(2)}) collective-permute-start(bf16[528,128]{1,0:T(8,128)(2,1)S(1)} %collective-permute-done.3.block_ref), channel_id=1, source_target_pairs={{0,1},{1,0},{2,3},{3,2},{4,5},{5,4},{6,7},{7,6},{8,9},{9,8},{10,11... | collective-permute-start | bytes 405512 | tf_op jit(solution)/shard_map/ppermute | solution.py:337
  18.7 13.5 %copy-start.2 = (f32[32]{0:T(128)S(1)}, f32[32]{0:T(128)}, u32[]{:S(2)}) copy-start(f32[32]{0:T(128)} %param.11) | copy-start | bytes 388
  18.7 13.5 %copy-start.3 = (s32[8]{0:T(128)S(1)}, s32[8]{0:T(128)}, u32[]{:S(2)}) copy-start(s32[8]{0:T(128)} %occupations_ref.1) | copy-start | bytes 100

commit v4 on v3

--- a/solution.py
+++ b/solution.py
@@ -62,6 +62,10 @@
     diagonals.append(jnp.zeros((16 - KL // 2, N), F32))
     packed_ref[KL // 2 * N :, :] = jnp.concatenate(diagonals, axis=0).astype(BF16)
     sum_ref[...] = total
+
+
+def copy_kernel(packed_ref, again_ref):
+    again_ref[...] = packed_ref[...]
 
 
 def unpack(load, blocks, place):
@@ -141,8 +145,7 @@
     charge_ref[...] = lane_sums(rows[...])
 
 
-def first_side_kernel(block_ref, factors_ref, partial_ref, forms_ref, next_ref, turned_ref, blocks, products, wide):
-    side_kernel(False, block_ref, factors_ref, partial_ref, next_ref, blocks, products)
+def turn_kernel(forms_ref, turned_ref, wide):
     form_count = forms_ref.shape[0]
     for j in range(form_count):
         wide[j * N : (j + 1) * N, :] = forms_ref[j].astype(F32)
@@ -304,8 +307,10 @@
     between = [(d, target % count) for d, target in between]
     other = lax.ppermute(packed, "ka", across)
     even = lax.ppermute(packed, "ka", within)
-    packed, other = lax.optimization_barrier((packed, other))
-    odd = lax.ppermute(packed, "ka", between)
+    again = pl.pallas_call(
+        copy_kernel, out_shape=shape((PACK, N), BF16), in_specs=[VMEM], out_specs=VMEM, compiler_params=params(16)
+    )(packed)
+    odd = lax.ppermute(again, "ka", between)
     partial, charge = pl.pallas_call(
         inner_kernel,
         out_shape=(shape((KL, N, N), F32), shape((8, form_count), F32)),
@@ -320,30 +325,35 @@
         cost_estimate=pl.CostEstimate(flops=5 * 10**9, bytes_accessed=5 * 10**6, transcendentals=0),
     )(packed, other, form_factors, hamiltonian, deviation_sum, hartree_forms)
 
-    side_scratch = [pltpu.VMEM((KL, N, N), BF16), pltpu.VMEM((KL // 2, KL * 2 * N, 2 * N), BF16)]
     side_cost = pl.CostEstimate(flops=2 * 10**9, bytes_accessed=5 * 10**6, transcendentals=0)
-    partial, even = lax.optimization_barrier((partial, even))
+
+    def side(second, block, partial):
+        return pl.pallas_call(
+            functools.partial(side_kernel, second),
+            out_shape=shape((KL, N, N), F32),
+            in_specs=[VMEM] * 3,
+            out_specs=VMEM,
+            scratch_shapes=[pltpu.VMEM((KL, N, N), BF16), pltpu.VMEM((KL // 2, KL * 2 * N, 2 * N), BF16)],
+            compiler_params=params(24),
+            cost_estimate=side_cost,
+        )(block, form_factors, partial)
+
+    partial, hartree_forms = lax.optimization_barrier((partial, hartree_forms))
+    turned = pl.pallas_call(
+        turn_kernel,
+        out_shape=shape((N, form_count, N), BF16),
+        in_specs=[VMEM],
+        out_specs=VMEM,
+        scratch_shapes=[pltpu.VMEM((form_count * N, N), F32)],
+        compiler_params=params(16),
+        cost_estimate=side_cost,
+    )(hartree_forms)
+    partial, turned, even = lax.optimization_barrier((partial, turned, even))
     even_across = lax.ppermute(even, "ka", across)
-    partial, turned = pl.pallas_call(
-        first_side_kernel,
-        out_shape=(shape((KL, N, N), F32), shape((N, form_count, N), BF16)),
-        in_specs=[VMEM] * 4,
-        out_specs=(VMEM, VMEM),
-        scratch_shapes=side_scratch + [pltpu.VMEM((form_count * N, N), F32)],
-        compiler_params=params(24),
-        cost_estimate=side_cost,
-    )(even, form_factors, partial, hartree_forms)
+    partial = side(False, even, partial)
     partial, odd = lax.optimization_barrier((partial, odd))
     odd_across = lax.ppermute(odd, "ka", across)
-    partial = pl.pallas_call(
-        functools.partial(side_kernel, True),
-        out_shape=shape((KL, N, N), F32),
-        in_specs=[VMEM] * 3,
-        out_specs=VMEM,
-        scratch_shapes=side_scratch,
-        compiler_params=params(24),
-        cost_estimate=side_cost,
-    )(odd, form_factors, partial)
+    partial = side(True, odd, partial)
     level, stats = pl.pallas_call(
         last_kernel,
         out_shape=(shape((KL * N, N), F32), shape((count, KL * form_count + N), F32)),

time: 36.2 us -> 35.3 us (0.975)
  starting transfers between devices: 8.93 us -> 8.31 us
  blocking collectives: 10.1 us -> 9.6 us
    ppermute x1, starting transfers between devices: 5.27 us -> 4.59 us  [per_device(): odd = lax.ppermute(again, 'ka', between)]
    all_to_all x1, blocking collectives: 10.1 us -> 9.6 us  [per_device(): shared = lax.all_to_all(stats, 'ka', 0, 0, tiled=True)]
    pallas_call x2 -> x4, Pallas kernels: 3.66 us -> 3.76 us  [the longest x2 2.47 us: side(): pl.pallas_call(functools.partial(side_kernel, second), out_shape=shape((K...]
  transfers between devices with their start and end apart: 5 -> 5, of which waited for: 0 -> 0; matrix products, arithmetic and copies ran while one was open for 0% -> 0% of each run, Pallas kernels for 21% -> 22%
where the time goes in v4:
time: 35.3 us; the launch traced here: 35.1 us
  Pallas kernels  16.3 us (46%)
  blocking collectives  9.6 us (27%)
  starting transfers between devices  8.31 us (24%)
  between operations  0.77 us (2%)
    all_to_all x1, blocking collectives, per_device(): shared = lax.all_to_all(stats, 'ka', 0, 0, tiled=True)  9.6 us
    ppermute x1, starting transfers between devices, per_device(): odd = lax.ppermute(again, 'ka', between)  4.59 us
    pallas_call x1, Pallas kernels, per_device(): pl.pallas_call(inner_kernel, out_shape=(shape((KL, N, N), F32), shape((8,...  4.05 us
    pallas_call x1, Pallas kernels, per_device(): pl.pallas_call(final_kernel, out_shape=(shape((KL, N, N), F32), shape((KL...  3.8 us
    pallas_call x1, Pallas kernels, per_device(): pl.pallas_call(last_kernel, out_shape=(shape((KL * N, N), F32), shape((co...  3.32 us
    ppermute x1, starting transfers between devices, per_device(): even = lax.ppermute(packed, 'ka', within)  2.56 us
    pallas_call x2, Pallas kernels, side(): pl.pallas_call(functools.partial(side_kernel, second), out_shape=shape((K...  2.47 us
    pallas_call x1, Pallas kernels, per_device(): pl.pallas_call(pack_kernel, out_shape=(shape((PACK, N), BF16), shape((N,...  1.36 us
  transfers between devices with their start and end apart: 5, of which 0 were waited for; matrix products, arithmetic and copies ran while one was open for 0% of the time, Pallas kernels for 22%

profile of v4, /device:TPU:0, one launch (start us, length us, event | category | flops | bytes accessed | tf_op | source)
XLA Modules:
  0.0 35.1 jit_solution(16219057952260142688)
XLA Ops:
  0.6 0.0 copy-start
  0.6 0.0 copy-start.1
  0.7 0.0 copy-start.4
  0.7 1.4 %shard_map.77 = (bf16[528,128]{1,0:T(8,128)(2,1)S(1)}, f32[128,128]{1,0:T(8,128)S(1)}) custom-call(f32[8,128,128]{2,1,0:T(8,128)} %density_hbm.1), custom_call_target="tpu_custom_call" | custom-call | flops 5000000000 | bytes 2000000 | tf_op jit(solution)/shard_map/pallas_call | solution.py:295
  2.0 0.5 %collective-permute-start = (bf16[528,128]{1,0:T(8,128)(2,1)S(1)}, bf16[528,128]{1,0:T(8,128)(2,1)S(1)}, u32[]{:S(2)}, u32[]{:S(2)}) collective-permute-start(bf16[528,128]{1,0:T(8,128)(2,1)S(1)} %get-tuple-element.15.own_ref.packed_ref), channel_id=1, source_target_pairs={{0,1},{1,0},{2,3},{3,2},{4,5},{5,4},{6,7},{7,6},{8,9},{9,8},{10,11... | collective-permute-start | bytes 405512 | tf_op jit(solution)/shard_map/ppermute | solution.py:308
  2.5 2.6 %collective-permute-start.1 = (bf16[528,128]{1,0:T(8,128)(2,1)S(1)}, bf16[528,128]{1,0:T(8,128)(2,1)S(1)}, u32[]{:S(2)}, u32[]{:S(2)}) collective-permute-start(bf16[528,128]{1,0:T(8,128)(2,1)S(1)} %get-tuple-element.15.own_ref.packed_ref), channel_id=1, source_target_pairs={{0,2},{1,3},{2,0},{3,1},{4,6},{5,7},{6,4},{7,5},{8,10},{9,11},{10,... | collective-permute-start | bytes 405512 | tf_op jit(solution)/shard_map/ppermute | solution.py:309
  5.1 4.6 %collective-permute-start.3 = (bf16[528,128]{1,0:T(8,128)(2,1)S(1)}, bf16[528,128]{1,0:T(8,128)(2,1)S(1)}, u32[]{:S(2)}, u32[]{:S(2)}) collective-permute-start(bf16[528,128]{1,0:T(8,128)(2,1)S(1)} %shard_map.81), channel_id=1, source_target_pairs={{0,30},{1,31},{2,4},{3,5},{4,2},{5,3},{6,8},{7,9},{8,6},{9,7},{10,... | collective-permute-start | bytes 405512 | tf_op jit(solution)/shard_map/ppermute | solution.py:313
  9.7 0.0 collective-permute-done.other_ref
  9.7 0.0 copy-done
  9.7 0.0 copy-done.1
  9.7 0.0 copy-done.4
  9.7 4.1 %shard_map.78 = (f32[8,128,128]{2,1,0:T(8,128)S(1)}, f32[8,32]{1,0:T(8,128)S(1)}) custom-call(bf16[528,128]{1,0:T(8,128)(2,1)S(1)} %get-tuple-element.15.own_ref.packed_ref, bf16[528,128]{1,0:T(8,128)(2,1)S(1)} %collective-permute-done.other_ref, bf16[33,2,128,128]{3,2,1,0:T(8,128)(2,1)S(1)} %copy-done, f32[8,128,128]{2,1,0:T(8,128)S(1)} %copy-done.4, ...), custom_call_target="tpu_custom_call" | custom-call | flops 5000000000 | bytes 5000000 | tf_op jit(solution)/shard_map/pallas_call | solution.py:314
  13.8 1.3 %shard_map.79.turned_ref = bf16[128,32,128]{2,1,0:T(8,128)(2,1)S(1)} custom-call(bf16[32,128,128]{2,1,0:T(8,128)(2,1)S(1)} %copy-done.1), custom_call_target="tpu_custom_call" | custom-call | flops 2000000000 | bytes 5000000 | tf_op jit(solution)/shard_map/pallas_call | solution.py:342
  15.1 0.0 collective-permute-done.1.block_ref
  15.1 0.1 collective-permute-start.2
  15.2 1.2 %shard_map.80.partial_ref = f32[8,128,128]{2,1,0:T(8,128)S(1)} custom-call(bf16[528,128]{1,0:T(8,128)(2,1)S(1)} %collective-permute-done.1.block_ref, bf16[33,2,128,128]{3,2,1,0:T(8,128)(2,1)S(1)} %copy-done, f32[8,128,128]{2,1,0:T(8,128)S(1)} %get-tuple-element.21.partial_ref), custom_call_target="tpu_custom_call" | custom-call | flops 2000000000 | bytes 5000000 | tf_op jit(solution)/shard_map/pallas_call | solution.py:331
  16.4 0.0 collective-permute-done.3.block_ref
  16.4 0.6 %collective-permute-start.4 = (bf16[528,128]{1,0:T(8,128)(2,1)S(1)}, bf16[528,128]{1,0:T(8,128)(2,1)S(1)}, u32[]{:S(2)}, u32[]{:S(2)}) collective-permute-start(bf16[528,128]{1,0:T(8,128)(2,1)S(1)} %collective-permute-done.3.block_ref), channel_id=1, source_target_pairs={{0,1},{1,0},{2,3},{3,2},{4,5},{5,4},{6,7},{7,6},{8,9},{9,8},{10,11... | collective-permute-start | bytes 405512 | tf_op jit(solution)/shard_map/ppermute | solution.py:355
  17.0 1.2 %shard_map.82.partial_ref = f32[8,128,128]{2,1,0:T(8,128)S(1)} custom-call(bf16[528,128]{1,0:T(8,128)(2,1)S(1)} %collective-permute-done.3.block_ref, bf16[33,2,128,128]{3,2,1,0:T(8,128)(2,1)S(1)} %copy-done, f32[8,128,128]{2,1,0:T(8,128)S(1)} %shard_map.80.partial_ref), custom_call_target="tpu_custom_call" | custom-call | flops 2000000000 | bytes 5000000 | tf_op jit(solution)/shard_map/pallas_call | solution.py:331
  18.2 0.0 copy-start.2
  18.2 0.0 copy-start.3
  18.2 0.0 collective-permute-done.4.odd_ref
  18.3 0.0 collective-permute-done.2.even_ref
  18.3 3.3 %shard_map.83 = (f32[1024,128]{1,0:T(8,128)S(1)}, f32[32,384]{1,0:T(8,128)S(1)}) custom-call(bf16[528,128]{1,0:T(8,128)(2,1)S(1)} %collective-permute-done.2.even_ref, bf16[528,128]{1,0:T(8,128)(2,1)S(1)} %collective-permute-done.4.odd_ref, bf16[33,2,128,128]{3,2,1,0:T(8,128)(2,1)S(1)} %copy-done, f32[8,128,128]{2,1,0:T(8,128)S(1)} %shard_map.82.partial_ref, ...), custom_call_target="tpu_custom_call" | custom-call | tf_op jit(solution)/shard_map/pallas_call | solution.py:357
  21.6 0.1 copy.8
  21.7 9.6 %all_to_all.11 = f32[32,1,384]{2,1,0:T(1,128)S(1)} all-to-all(f32[32,1,384]{2,1,0:T(1,128)S(1)} %copy.8), channel_id=1, replica_groups=mesh['ka'=32] {'ka'}, dimensions={0} | all-to-all | bytes 98304 | tf_op jit(solution)/shard_map/all_to_all | solution.py:370
  31.3 0.0 copy-done.2
  31.3 0.0 copy-done.3
  31.3 3.8 %shard_map.84 = (f32[8,128,128]{2,1,0:T(8,128)}, f32[8,128,128]{2,1,0:T(8,128)}) custom-call(f32[32,384]{1,0:T(8,128)S(1)} %bitcast.5, f32[1024,128]{1,0:T(8,128)S(1)} %get-tuple-element.27.level_ref, bf16[32,128,128]{2,1,0:T(8,128)(2,1)S(1)} %copy-done.1, f32[1,32]{1,0:T(1,128)S(1)} %bitcast.7, s32[8]{0:T(128)S(1)} %copy-done.3), custom_call_target="tpu_custom_call" | custom-call | tf_op jit(solution)/shard_map/pallas_call | solution.py:371
  (2 shorter events, 0.0 us)
Async XLA Ops:
  0.6 9.1 %copy-start = (bf16[33,2,128,128]{3,2,1,0:T(8,128)(2,1)S(1)}, bf16[33,2,128,128]{3,2,1,0:T(8,128)(2,1)}, u32[]{:S(2)}) copy-start(bf16[33,2,128,128]{3,2,1,0:T(8,128)(2,1)} %factors_ref.7) | copy-start | bytes 6488068
  0.6 9.1 %copy-start.1 = (bf16[32,128,128]{2,1,0:T(8,128)(2,1)S(1)}, bf16[32,128,128]{2,1,0:T(8,128)(2,1)}, u32[]{:S(2)}) copy-start(bf16[32,128,128]{2,1,0:T(8,128)(2,1)} %forms_ref.3) | copy-start | bytes 3145732
  0.7 9.1 %copy-start.4 = (f32[8,128,128]{2,1,0:T(8,128)S(1)}, f32[8,128,128]{2,1,0:T(8,128)}, u32[]{:S(2)}) copy-start(f32[8,128,128]{2,1,0:T(8,128)} %hamiltonian_ref.1) | copy-start | bytes 1572868
  2.0 7.7 %collective-permute-start = (bf16[528,128]{1,0:T(8,128)(2,1)S(1)}, bf16[528,128]{1,0:T(8,128)(2,1)S(1)}, u32[]{:S(2)}, u32[]{:S(2)}) collective-permute-start(bf16[528,128]{1,0:T(8,128)(2,1)S(1)} %get-tuple-element.15.own_ref.packed_ref), channel_id=1, source_target_pairs={{0,1},{1,0},{2,3},{3,2},{4,5},{5,4},{6,7},{7,6},{8,9},{9,8},{10,11... | collective-permute-start | bytes 405512 | tf_op jit(solution)/shard_map/ppermute | solution.py:308
  2.5 12.5 %collective-permute-start.1 = (bf16[528,128]{1,0:T(8,128)(2,1)S(1)}, bf16[528,128]{1,0:T(8,128)(2,1)S(1)}, u32[]{:S(2)}, u32[]{:S(2)}) collective-permute-start(bf16[528,128]{1,0:T(8,128)(2,1)S(1)} %get-tuple-element.15.own_ref.packed_ref), channel_id=1, source_target_pairs={{0,2},{1,3},{2,0},{3,1},{4,6},{5,7},{6,4},{7,5},{8,10},{9,11},{10,... | collective-permute-start | bytes 405512 | tf_op jit(solution)/shard_map/ppermute | solution.py:309
  5.1 11.3 %collective-permute-start.3 = (bf16[528,128]{1,0:T(8,128)(2,1)S(1)}, bf16[528,128]{1,0:T(8,128)(2,1)S(1)}, u32[]{:S(2)}, u32[]{:S(2)}) collective-permute-start(bf16[528,128]{1,0:T(8,128)(2,1)S(1)} %shard_map.81), channel_id=1, source_target_pairs={{0,30},{1,31},{2,4},{3,5},{4,2},{5,3},{6,8},{7,9},{8,6},{9,7},{10,... | collective-permute-start | bytes 405512 | tf_op jit(solution)/shard_map/ppermute | solution.py:313
  15.1 3.2 %collective-permute-start.2 = (bf16[528,128]{1,0:T(8,128)(2,1)S(1)}, bf16[528,128]{1,0:T(8,128)(2,1)S(1)}, u32[]{:S(2)}, u32[]{:S(2)}) collective-permute-start(bf16[528,128]{1,0:T(8,128)(2,1)S(1)} %collective-permute-done.1.block_ref), channel_id=1, source_target_pairs={{0,1},{1,0},{2,3},{3,2},{4,5},{5,4},{6,7},{7,6},{8,9},{9,8},{10,11... | collective-permute-start | bytes 405512 | tf_op jit(solution)/shard_map/ppermute | solution.py:352
  16.4 1.8 %collective-permute-start.4 = (bf16[528,128]{1,0:T(8,128)(2,1)S(1)}, bf16[528,128]{1,0:T(8,128)(2,1)S(1)}, u32[]{:S(2)}, u32[]{:S(2)}) collective-permute-start(bf16[528,128]{1,0:T(8,128)(2,1)S(1)} %collective-permute-done.3.block_ref), channel_id=1, source_target_pairs={{0,1},{1,0},{2,3},{3,2},{4,5},{5,4},{6,7},{7,6},{8,9},{9,8},{10,11... | collective-permute-start | bytes 405512 | tf_op jit(solution)/shard_map/ppermute | solution.py:355
  18.2 13.1 %copy-start.2 = (f32[32]{0:T(128)S(1)}, f32[32]{0:T(128)}, u32[]{:S(2)}) copy-start(f32[32]{0:T(128)} %param.11) | copy-start | bytes 388
  18.2 13.0 %copy-start.3 = (s32[8]{0:T(128)S(1)}, s32[8]{0:T(128)}, u32[]{:S(2)}) copy-start(s32[8]{0:T(128)} %occupations_ref.1) | copy-start | bytes 100

commit v5 on v4

--- a/solution.py
+++ b/solution.py
@@ -247,9 +247,11 @@
     for j in range(form_count):
         hartree = hartree + weights[:, j : j + 1] * forms_ref[j].astype(F32)
     hartree = 0.5 * (hartree + hartree.T)
-    offset = jnp.sum(jnp.where(row == col, hartree, 0.0), keepdims=True) / N
-    traceless = hartree - jnp.where(row == col, offset, 0.0)
-    own = jnp.sum(traceless * traceless, keepdims=True)
+    diagonal = jnp.sum(jnp.where(row == col, hartree, 0.0), axis=0, keepdims=True)
+    offset = jnp.sum(diagonal, axis=1, keepdims=True) / N
+    beside = jnp.where(row == col, 0.0, hartree)
+    own = jnp.sum(beside * beside, axis=0, keepdims=True) + (diagonal - offset) ** 2
+    own = jnp.sum(own, axis=1, keepdims=True)
     norms_at = overlap_count + form_count
     means = stats_ref[:, norms_at + KL : norms_at + 2 * KL]
     mean = jnp.sum(means, keepdims=True) / total

time: 35.3 us -> 35.1 us (level)
  no operation moved by 1% of the time
where the time goes in v5:
time: 35.1 us; the launch traced here: 34.9 us
  Pallas kernels  16.1 us (46%)
  blocking collectives  9.6 us (27%)
  starting transfers between devices  8.31 us (24%)
  between operations  0.77 us (2%)
    all_to_all x1, blocking collectives, per_device(): shared = lax.all_to_all(stats, 'ka', 0, 0, tiled=True)  9.6 us
    ppermute x1, starting transfers between devices, per_device(): odd = lax.ppermute(again, 'ka', between)  4.59 us
    pallas_call x1, Pallas kernels, per_device(): pl.pallas_call(inner_kernel, out_shape=(shape((KL, N, N), F32), shape((8,...  4.05 us
    pallas_call x1, Pallas kernels, per_device(): pl.pallas_call(final_kernel, out_shape=(shape((KL, N, N), F32), shape((KL...  3.65 us
    pallas_call x1, Pallas kernels, per_device(): pl.pallas_call(last_kernel, out_shape=(shape((KL * N, N), F32), shape((co...  3.32 us
    ppermute x1, starting transfers between devices, per_device(): even = lax.ppermute(packed, 'ka', within)  2.56 us
    pallas_call x2, Pallas kernels, side(): pl.pallas_call(functools.partial(side_kernel, second), out_shape=shape((K...  2.47 us
    pallas_call x1, Pallas kernels, per_device(): pl.pallas_call(pack_kernel, out_shape=(shape((PACK, N), BF16), shape((N,...  1.36 us
  transfers between devices with their start and end apart: 5, of which 0 were waited for; matrix products, arithmetic and copies ran while one was open for 0% of the time, Pallas kernels for 22%

profile of v5, /device:TPU:0, one launch (start us, length us, event | category | flops | bytes accessed | tf_op | source)
XLA Modules:
  0.0 34.9 jit_solution(10174535564453720969)
XLA Ops:
  0.6 0.0 copy-start
  0.6 0.0 copy-start.1
  0.7 0.0 copy-start.4
  0.7 1.4 %shard_map.77 = (bf16[528,128]{1,0:T(8,128)(2,1)S(1)}, f32[128,128]{1,0:T(8,128)S(1)}) custom-call(f32[8,128,128]{2,1,0:T(8,128)} %density_hbm.1), custom_call_target="tpu_custom_call" | custom-call | flops 5000000000 | bytes 2000000 | tf_op jit(solution)/shard_map/pallas_call | solution.py:297
  2.0 0.5 %collective-permute-start = (bf16[528,128]{1,0:T(8,128)(2,1)S(1)}, bf16[528,128]{1,0:T(8,128)(2,1)S(1)}, u32[]{:S(2)}, u32[]{:S(2)}) collective-permute-start(bf16[528,128]{1,0:T(8,128)(2,1)S(1)} %get-tuple-element.15.own_ref.packed_ref), channel_id=1, source_target_pairs={{0,1},{1,0},{2,3},{3,2},{4,5},{5,4},{6,7},{7,6},{8,9},{9,8},{10,11... | collective-permute-start | bytes 405512 | tf_op jit(solution)/shard_map/ppermute | solution.py:310
  2.5 2.6 %collective-permute-start.1 = (bf16[528,128]{1,0:T(8,128)(2,1)S(1)}, bf16[528,128]{1,0:T(8,128)(2,1)S(1)}, u32[]{:S(2)}, u32[]{:S(2)}) collective-permute-start(bf16[528,128]{1,0:T(8,128)(2,1)S(1)} %get-tuple-element.15.own_ref.packed_ref), channel_id=1, source_target_pairs={{0,2},{1,3},{2,0},{3,1},{4,6},{5,7},{6,4},{7,5},{8,10},{9,11},{10,... | collective-permute-start | bytes 405512 | tf_op jit(solution)/shard_map/ppermute | solution.py:311
  5.1 4.6 %collective-permute-start.3 = (bf16[528,128]{1,0:T(8,128)(2,1)S(1)}, bf16[528,128]{1,0:T(8,128)(2,1)S(1)}, u32[]{:S(2)}, u32[]{:S(2)}) collective-permute-start(bf16[528,128]{1,0:T(8,128)(2,1)S(1)} %shard_map.81), channel_id=1, source_target_pairs={{0,30},{1,31},{2,4},{3,5},{4,2},{5,3},{6,8},{7,9},{8,6},{9,7},{10,... | collective-permute-start | bytes 405512 | tf_op jit(solution)/shard_map/ppermute | solution.py:315
  9.7 0.0 collective-permute-done.other_ref
  9.7 0.0 copy-done
  9.7 0.0 copy-done.1
  9.7 0.0 copy-done.4
  9.7 4.1 %shard_map.78 = (f32[8,128,128]{2,1,0:T(8,128)S(1)}, f32[8,32]{1,0:T(8,128)S(1)}) custom-call(bf16[528,128]{1,0:T(8,128)(2,1)S(1)} %get-tuple-element.15.own_ref.packed_ref, bf16[528,128]{1,0:T(8,128)(2,1)S(1)} %collective-permute-done.other_ref, bf16[33,2,128,128]{3,2,1,0:T(8,128)(2,1)S(1)} %copy-done, f32[8,128,128]{2,1,0:T(8,128)S(1)} %copy-done.4, ...), custom_call_target="tpu_custom_call" | custom-call | flops 5000000000 | bytes 5000000 | tf_op jit(solution)/shard_map/pallas_call | solution.py:316
  13.8 1.3 %shard_map.79.turned_ref = bf16[128,32,128]{2,1,0:T(8,128)(2,1)S(1)} custom-call(bf16[32,128,128]{2,1,0:T(8,128)(2,1)S(1)} %copy-done.1), custom_call_target="tpu_custom_call" | custom-call | flops 2000000000 | bytes 5000000 | tf_op jit(solution)/shard_map/pallas_call | solution.py:344
  15.1 0.0 collective-permute-done.1.block_ref
  15.1 0.1 collective-permute-start.2
  15.2 1.2 %shard_map.80.partial_ref = f32[8,128,128]{2,1,0:T(8,128)S(1)} custom-call(bf16[528,128]{1,0:T(8,128)(2,1)S(1)} %collective-permute-done.1.block_ref, bf16[33,2,128,128]{3,2,1,0:T(8,128)(2,1)S(1)} %copy-done, f32[8,128,128]{2,1,0:T(8,128)S(1)} %get-tuple-element.21.partial_ref), custom_call_target="tpu_custom_call" | custom-call | flops 2000000000 | bytes 5000000 | tf_op jit(solution)/shard_map/pallas_call | solution.py:333
  16.4 0.0 collective-permute-done.3.block_ref
  16.4 0.6 %collective-permute-start.4 = (bf16[528,128]{1,0:T(8,128)(2,1)S(1)}, bf16[528,128]{1,0:T(8,128)(2,1)S(1)}, u32[]{:S(2)}, u32[]{:S(2)}) collective-permute-start(bf16[528,128]{1,0:T(8,128)(2,1)S(1)} %collective-permute-done.3.block_ref), channel_id=1, source_target_pairs={{0,1},{1,0},{2,3},{3,2},{4,5},{5,4},{6,7},{7,6},{8,9},{9,8},{10,11... | collective-permute-start | bytes 405512 | tf_op jit(solution)/shard_map/ppermute | solution.py:357
  17.0 1.2 %shard_map.82.partial_ref = f32[8,128,128]{2,1,0:T(8,128)S(1)} custom-call(bf16[528,128]{1,0:T(8,128)(2,1)S(1)} %collective-permute-done.3.block_ref, bf16[33,2,128,128]{3,2,1,0:T(8,128)(2,1)S(1)} %copy-done, f32[8,128,128]{2,1,0:T(8,128)S(1)} %shard_map.80.partial_ref), custom_call_target="tpu_custom_call" | custom-call | flops 2000000000 | bytes 5000000 | tf_op jit(solution)/shard_map/pallas_call | solution.py:333
  18.2 0.0 copy-start.2
  18.2 0.0 copy-start.3
  18.2 0.0 collective-permute-done.4.odd_ref
  18.3 0.0 collective-permute-done.2.even_ref
  18.3 3.3 %shard_map.83 = (f32[1024,128]{1,0:T(8,128)S(1)}, f32[32,384]{1,0:T(8,128)S(1)}) custom-call(bf16[528,128]{1,0:T(8,128)(2,1)S(1)} %collective-permute-done.2.even_ref, bf16[528,128]{1,0:T(8,128)(2,1)S(1)} %collective-permute-done.4.odd_ref, bf16[33,2,128,128]{3,2,1,0:T(8,128)(2,1)S(1)} %copy-done, f32[8,128,128]{2,1,0:T(8,128)S(1)} %shard_map.82.partial_ref, ...), custom_call_target="tpu_custom_call" | custom-call | tf_op jit(solution)/shard_map/pallas_call | solution.py:359
  21.6 0.1 copy.8
  21.7 9.6 %all_to_all.11 = f32[32,1,384]{2,1,0:T(1,128)S(1)} all-to-all(f32[32,1,384]{2,1,0:T(1,128)S(1)} %copy.8), channel_id=1, replica_groups=mesh['ka'=32] {'ka'}, dimensions={0} | all-to-all | bytes 98304 | tf_op jit(solution)/shard_map/all_to_all | solution.py:372
  31.3 0.0 copy-done.2
  31.3 0.0 copy-done.3
  31.3 3.6 %shard_map.84 = (f32[8,128,128]{2,1,0:T(8,128)}, f32[8,128,128]{2,1,0:T(8,128)}) custom-call(f32[32,384]{1,0:T(8,128)S(1)} %bitcast.5, f32[1024,128]{1,0:T(8,128)S(1)} %get-tuple-element.27.level_ref, bf16[32,128,128]{2,1,0:T(8,128)(2,1)S(1)} %copy-done.1, f32[1,32]{1,0:T(1,128)S(1)} %bitcast.7, s32[8]{0:T(128)S(1)} %copy-done.3), custom_call_target="tpu_custom_call" | custom-call | tf_op jit(solution)/shard_map/pallas_call | solution.py:373
  (2 shorter events, 0.0 us)
Async XLA Ops:
  0.6 9.1 %copy-start = (bf16[33,2,128,128]{3,2,1,0:T(8,128)(2,1)S(1)}, bf16[33,2,128,128]{3,2,1,0:T(8,128)(2,1)}, u32[]{:S(2)}) copy-start(bf16[33,2,128,128]{3,2,1,0:T(8,128)(2,1)} %factors_ref.7) | copy-start | bytes 6488068
  0.6 9.1 %copy-start.1 = (bf16[32,128,128]{2,1,0:T(8,128)(2,1)S(1)}, bf16[32,128,128]{2,1,0:T(8,128)(2,1)}, u32[]{:S(2)}) copy-start(bf16[32,128,128]{2,1,0:T(8,128)(2,1)} %forms_ref.3) | copy-start | bytes 3145732
  0.7 9.1 %copy-start.4 = (f32[8,128,128]{2,1,0:T(8,128)S(1)}, f32[8,128,128]{2,1,0:T(8,128)}, u32[]{:S(2)}) copy-start(f32[8,128,128]{2,1,0:T(8,128)} %hamiltonian_ref.1) | copy-start | bytes 1572868
  2.0 7.7 %collective-permute-start = (bf16[528,128]{1,0:T(8,128)(2,1)S(1)}, bf16[528,128]{1,0:T(8,128)(2,1)S(1)}, u32[]{:S(2)}, u32[]{:S(2)}) collective-permute-start(bf16[528,128]{1,0:T(8,128)(2,1)S(1)} %get-tuple-element.15.own_ref.packed_ref), channel_id=1, source_target_pairs={{0,1},{1,0},{2,3},{3,2},{4,5},{5,4},{6,7},{7,6},{8,9},{9,8},{10,11... | collective-permute-start | bytes 405512 | tf_op jit(solution)/shard_map/ppermute | solution.py:310
  2.5 12.5 %collective-permute-start.1 = (bf16[528,128]{1,0:T(8,128)(2,1)S(1)}, bf16[528,128]{1,0:T(8,128)(2,1)S(1)}, u32[]{:S(2)}, u32[]{:S(2)}) collective-permute-start(bf16[528,128]{1,0:T(8,128)(2,1)S(1)} %get-tuple-element.15.own_ref.packed_ref), channel_id=1, source_target_pairs={{0,2},{1,3},{2,0},{3,1},{4,6},{5,7},{6,4},{7,5},{8,10},{9,11},{10,... | collective-permute-start | bytes 405512 | tf_op jit(solution)/shard_map/ppermute | solution.py:311
  5.1 11.3 %collective-permute-start.3 = (bf16[528,128]{1,0:T(8,128)(2,1)S(1)}, bf16[528,128]{1,0:T(8,128)(2,1)S(1)}, u32[]{:S(2)}, u32[]{:S(2)}) collective-permute-start(bf16[528,128]{1,0:T(8,128)(2,1)S(1)} %shard_map.81), channel_id=1, source_target_pairs={{0,30},{1,31},{2,4},{3,5},{4,2},{5,3},{6,8},{7,9},{8,6},{9,7},{10,... | collective-permute-start | bytes 405512 | tf_op jit(solution)/shard_map/ppermute | solution.py:315
  15.1 3.2 %collective-permute-start.2 = (bf16[528,128]{1,0:T(8,128)(2,1)S(1)}, bf16[528,128]{1,0:T(8,128)(2,1)S(1)}, u32[]{:S(2)}, u32[]{:S(2)}) collective-permute-start(bf16[528,128]{1,0:T(8,128)(2,1)S(1)} %collective-permute-done.1.block_ref), channel_id=1, source_target_pairs={{0,1},{1,0},{2,3},{3,2},{4,5},{5,4},{6,7},{7,6},{8,9},{9,8},{10,11... | collective-permute-start | bytes 405512 | tf_op jit(solution)/shard_map/ppermute | solution.py:354
  16.4 1.8 %collective-permute-start.4 = (bf16[528,128]{1,0:T(8,128)(2,1)S(1)}, bf16[528,128]{1,0:T(8,128)(2,1)S(1)}, u32[]{:S(2)}, u32[]{:S(2)}) collective-permute-start(bf16[528,128]{1,0:T(8,128)(2,1)S(1)} %collective-permute-done.3.block_ref), channel_id=1, source_target_pairs={{0,1},{1,0},{2,3},{3,2},{4,5},{5,4},{6,7},{7,6},{8,9},{9,8},{10,11... | collective-permute-start | bytes 405512 | tf_op jit(solution)/shard_map/ppermute | solution.py:357
  18.2 13.1 %copy-start.2 = (f32[32]{0:T(128)S(1)}, f32[32]{0:T(128)}, u32[]{:S(2)}) copy-start(f32[32]{0:T(128)} %param.11) | copy-start | bytes 388
  18.2 13.0 %copy-start.3 = (s32[8]{0:T(128)S(1)}, s32[8]{0:T(128)}, u32[]{:S(2)}) copy-start(s32[8]{0:T(128)} %occupations_ref.1) | copy-start | bytes 100

commit v6 on v5

--- a/solution.py
+++ b/solution.py
@@ -147,10 +147,12 @@
 
 def turn_kernel(forms_ref, turned_ref, wide):
     form_count = forms_ref.shape[0]
+    group = N // turned_ref.shape[0]
     for j in range(form_count):
         wide[j * N : (j + 1) * N, :] = forms_ref[j].astype(F32)
-    for row in range(N):
-        turned_ref[row] = wide[pl.ds(row, form_count, stride=N), :].astype(BF16)
+    for at in range(turned_ref.shape[0]):
+        rows = [wide[pl.ds(at * group + row, form_count, stride=N), :] for row in range(group)]
+        turned_ref[at] = jnp.concatenate(rows, axis=0).T.astype(BF16)
 
 
 def side_kernel(second, block_ref, factors_ref, partial_ref, next_ref, blocks, products):
@@ -208,23 +210,33 @@
     mean = jnp.sum(diagonals[...], axis=1, keepdims=True) / N
     rest = diagonals[...] - mean
     norm = jnp.sum(squares[...] + rest * rest, axis=1, keepdims=True)
-    form_count = turned_ref.shape[1]
     lane = lax.broadcasted_iota(jnp.int32, (KL, N), 1)
     place = lax.broadcasted_iota(jnp.int32, (KL, N), 0)
-    chunk = 16
-    dots = jnp.zeros((2 * KL, form_count), F32)
-    for start in range(0, N, chunk):
-        lefts, rights = [], []
-        for at in range(start, start + chunk):
-            values = level_ref[pl.ds(at, KL, stride=N), :]
-            values = jnp.where(lane == at, values - mean, values)
-            high = values.astype(BF16).astype(F32)
-            lefts.append(jnp.concatenate([high, values - high], axis=0).astype(BF16))
-            rights.append(turned_ref[at])
-        dots = dots + lax.dot_general(
-            jnp.concatenate(lefts, axis=1), jnp.concatenate(rights, axis=1), LANES_LAST, preferred_element_type=F32
+    group = N // turned_ref.shape[0]
+    form_count = turned_ref.shape[2] // group
+    eye = jnp.where(row == col, 1.0, 0.0).astype(F32)
+    table = jnp.zeros((2 * KL * group, group * form_count), F32)
+    for at in range(0, N // group, 2):
+        lefts = []
+        for first in (at * group, (at + 1) * group):
+            highs, lows = [], []
+            for k in range(KL):
+                values = level_ref[k * N + first : k * N + first + group, :]
+                values = values - mean[k : k + 1, :] * eye[first : first + group, :]
+                highs.append(values.astype(BF16).astype(F32))
+                lows.append(values - highs[-1])
+            lefts.append(jnp.concatenate(highs + lows, axis=0).astype(BF16))
+        table = table + jnp.dot(
+            jnp.concatenate(lefts, axis=1), turned_ref[at : at + 2].reshape(2 * N, -1), preferred_element_type=F32
         )
-    overlaps = dots[:KL, :] + dots[KL:, :]
+    at_row = lax.broadcasted_iota(jnp.int32, table.shape, 0) % group
+    at_lane = lax.broadcasted_iota(jnp.int32, table.shape, 1) // form_count
+    table = jnp.where(at_row == at_lane, table, 0.0)
+    table = jnp.sum(table.reshape(2 * KL, group, group * form_count), axis=1)
+    table = table[:KL, :] + table[KL:, :]
+    overlaps = jnp.zeros((KL, form_count), F32)
+    for at in range(group):
+        overlaps = overlaps + table[:, at * form_count : (at + 1) * form_count]
     numbers = jnp.where(lane == form_count + place, norm, 0.0)
     numbers = numbers + jnp.where(lane == form_count + KL + place, mean, 0.0)
     charge = jnp.concatenate([charge_ref[0:1, :], jnp.zeros((1, N - form_count), F32)], axis=1)
@@ -343,7 +355,7 @@
     partial, hartree_forms = lax.optimization_barrier((partial, hartree_forms))
     turned = pl.pallas_call(
         turn_kernel,
-        out_shape=shape((N, form_count, N), BF16),
+        out_shape=shape((N * form_count // (2 * N), N, 2 * N), BF16),
         in_specs=[VMEM],
         out_specs=VMEM,
         scratch_shapes=[pltpu.VMEM((form_count * N, N), F32)],

time: 35.1 us -> 34.7 us (0.989)
  transfers between devices with their start and end apart: 5 -> 5, of which waited for: 0 -> 0; matrix products, arithmetic and copies ran while one was open for 0% -> 0% of each run, Pallas kernels for 22% -> 23%
where the time goes in v6:
time: 34.7 us; the launch traced here: 34.6 us
  Pallas kernels  15.9 us (46%)
  blocking collectives  9.54 us (27%)
  starting transfers between devices  8.31 us (24%)
  between operations  0.77 us (2%)
    all_to_all x1, blocking collectives, per_device(): shared = lax.all_to_all(stats, 'ka', 0, 0, tiled=True)  9.54 us
    ppermute x1, starting transfers between devices, per_device(): odd = lax.ppermute(again, 'ka', between)  4.59 us
    pallas_call x1, Pallas kernels, per_device(): pl.pallas_call(inner_kernel, out_shape=(shape((KL, N, N), F32), shape((8,...  4.05 us
    pallas_call x1, Pallas kernels, per_device(): pl.pallas_call(final_kernel, out_shape=(shape((KL, N, N), F32), shape((KL...  3.65 us
    pallas_call x1, Pallas kernels, per_device(): pl.pallas_call(last_kernel, out_shape=(shape((KL * N, N), F32), shape((co...  2.98 us
    ppermute x1, starting transfers between devices, per_device(): even = lax.ppermute(packed, 'ka', within)  2.56 us
    pallas_call x2, Pallas kernels, side(): pl.pallas_call(functools.partial(side_kernel, second), out_shape=shape((K...  2.47 us
    pallas_call x1, Pallas kernels, per_device(): pl.pallas_call(pack_kernel, out_shape=(shape((PACK, N), BF16), shape((N,...  1.36 us
  transfers between devices with their start and end apart: 5, of which 0 were waited for; matrix products, arithmetic and copies ran while one was open for 0% of the time, Pallas kernels for 23%

profile of v6, /device:TPU:0, one launch (start us, length us, event | category | flops | bytes accessed | tf_op | source)
XLA Modules:
  0.0 34.6 jit_solution(11586702984072408964)
XLA Ops:
  0.6 0.0 copy-start
  0.6 0.0 copy-start.1
  0.7 0.0 copy-start.4
  0.7 1.4 %shard_map.77 = (bf16[528,128]{1,0:T(8,128)(2,1)S(1)}, f32[128,128]{1,0:T(8,128)S(1)}) custom-call(f32[8,128,128]{2,1,0:T(8,128)} %density_hbm.1), custom_call_target="tpu_custom_call" | custom-call | flops 5000000000 | bytes 2000000 | tf_op jit(solution)/shard_map/pallas_call | solution.py:309
  2.0 0.5 %collective-permute-start = (bf16[528,128]{1,0:T(8,128)(2,1)S(1)}, bf16[528,128]{1,0:T(8,128)(2,1)S(1)}, u32[]{:S(2)}, u32[]{:S(2)}) collective-permute-start(bf16[528,128]{1,0:T(8,128)(2,1)S(1)} %get-tuple-element.15.own_ref.packed_ref), channel_id=1, source_target_pairs={{0,1},{1,0},{2,3},{3,2},{4,5},{5,4},{6,7},{7,6},{8,9},{9,8},{10,11... | collective-permute-start | bytes 405512 | tf_op jit(solution)/shard_map/ppermute | solution.py:322
  2.5 2.6 %collective-permute-start.1 = (bf16[528,128]{1,0:T(8,128)(2,1)S(1)}, bf16[528,128]{1,0:T(8,128)(2,1)S(1)}, u32[]{:S(2)}, u32[]{:S(2)}) collective-permute-start(bf16[528,128]{1,0:T(8,128)(2,1)S(1)} %get-tuple-element.15.own_ref.packed_ref), channel_id=1, source_target_pairs={{0,2},{1,3},{2,0},{3,1},{4,6},{5,7},{6,4},{7,5},{8,10},{9,11},{10,... | collective-permute-start | bytes 405512 | tf_op jit(solution)/shard_map/ppermute | solution.py:323
  5.1 4.6 %collective-permute-start.3 = (bf16[528,128]{1,0:T(8,128)(2,1)S(1)}, bf16[528,128]{1,0:T(8,128)(2,1)S(1)}, u32[]{:S(2)}, u32[]{:S(2)}) collective-permute-start(bf16[528,128]{1,0:T(8,128)(2,1)S(1)} %shard_map.81), channel_id=1, source_target_pairs={{0,30},{1,31},{2,4},{3,5},{4,2},{5,3},{6,8},{7,9},{8,6},{9,7},{10,... | collective-permute-start | bytes 405512 | tf_op jit(solution)/shard_map/ppermute | solution.py:327
  9.7 0.0 collective-permute-done.other_ref
  9.7 0.0 copy-done
  9.7 0.0 copy-done.1
  9.7 0.0 copy-done.4
  9.7 4.1 %shard_map.78 = (f32[8,128,128]{2,1,0:T(8,128)S(1)}, f32[8,32]{1,0:T(8,128)S(1)}) custom-call(bf16[528,128]{1,0:T(8,128)(2,1)S(1)} %get-tuple-element.15.own_ref.packed_ref, bf16[528,128]{1,0:T(8,128)(2,1)S(1)} %collective-permute-done.other_ref, bf16[33,2,128,128]{3,2,1,0:T(8,128)(2,1)S(1)} %copy-done, f32[8,128,128]{2,1,0:T(8,128)S(1)} %copy-done.4, ...), custom_call_target="tpu_custom_call" | custom-call | flops 5000000000 | bytes 5000000 | tf_op jit(solution)/shard_map/pallas_call | solution.py:328
  13.8 1.4 %shard_map.79.turned_ref = bf16[16,128,256]{2,1,0:T(8,128)(2,1)S(1)} custom-call(bf16[32,128,128]{2,1,0:T(8,128)(2,1)S(1)} %copy-done.1), custom_call_target="tpu_custom_call" | custom-call | flops 2000000000 | bytes 5000000 | tf_op jit(solution)/shard_map/pallas_call | solution.py:356
  15.1 0.0 collective-permute-done.1.block_ref
  15.2 0.1 collective-permute-start.2
  15.2 1.2 %shard_map.80.partial_ref = f32[8,128,128]{2,1,0:T(8,128)S(1)} custom-call(bf16[528,128]{1,0:T(8,128)(2,1)S(1)} %collective-permute-done.1.block_ref, bf16[33,2,128,128]{3,2,1,0:T(8,128)(2,1)S(1)} %copy-done, f32[8,128,128]{2,1,0:T(8,128)S(1)} %get-tuple-element.21.partial_ref), custom_call_target="tpu_custom_call" | custom-call | flops 2000000000 | bytes 5000000 | tf_op jit(solution)/shard_map/pallas_call | solution.py:345
  16.5 0.0 collective-permute-done.3.block_ref
  16.5 0.6 %collective-permute-start.4 = (bf16[528,128]{1,0:T(8,128)(2,1)S(1)}, bf16[528,128]{1,0:T(8,128)(2,1)S(1)}, u32[]{:S(2)}, u32[]{:S(2)}) collective-permute-start(bf16[528,128]{1,0:T(8,128)(2,1)S(1)} %collective-permute-done.3.block_ref), channel_id=1, source_target_pairs={{0,1},{1,0},{2,3},{3,2},{4,5},{5,4},{6,7},{7,6},{8,9},{9,8},{10,11... | collective-permute-start | bytes 405512 | tf_op jit(solution)/shard_map/ppermute | solution.py:369
  17.0 1.2 %shard_map.82.partial_ref = f32[8,128,128]{2,1,0:T(8,128)S(1)} custom-call(bf16[528,128]{1,0:T(8,128)(2,1)S(1)} %collective-permute-done.3.block_ref, bf16[33,2,128,128]{3,2,1,0:T(8,128)(2,1)S(1)} %copy-done, f32[8,128,128]{2,1,0:T(8,128)S(1)} %shard_map.80.partial_ref), custom_call_target="tpu_custom_call" | custom-call | flops 2000000000 | bytes 5000000 | tf_op jit(solution)/shard_map/pallas_call | solution.py:345
  18.3 0.0 copy-start.2
  18.3 0.0 copy-start.3
  18.3 0.0 collective-permute-done.4.odd_ref
  18.3 0.0 collective-permute-done.2.even_ref
  18.3 3.0 %shard_map.83 = (f32[1024,128]{1,0:T(8,128)S(1)}, f32[32,384]{1,0:T(8,128)S(1)}) custom-call(bf16[528,128]{1,0:T(8,128)(2,1)S(1)} %collective-permute-done.2.even_ref, bf16[528,128]{1,0:T(8,128)(2,1)S(1)} %collective-permute-done.4.odd_ref, bf16[33,2,128,128]{3,2,1,0:T(8,128)(2,1)S(1)} %copy-done, f32[8,128,128]{2,1,0:T(8,128)S(1)} %shard_map.82.partial_ref, ...), custom_call_target="tpu_custom_call" | custom-call | tf_op jit(solution)/shard_map/pallas_call | solution.py:371
  21.3 0.1 copy.8
  21.4 9.5 %all_to_all.11 = f32[32,1,384]{2,1,0:T(1,128)S(1)} all-to-all(f32[32,1,384]{2,1,0:T(1,128)S(1)} %copy.8), channel_id=1, replica_groups=mesh['ka'=32] {'ka'}, dimensions={0} | all-to-all | bytes 98304 | tf_op jit(solution)/shard_map/all_to_all | solution.py:384
  30.9 0.0 copy-done.2
  30.9 0.0 copy-done.3
  30.9 3.6 %shard_map.84 = (f32[8,128,128]{2,1,0:T(8,128)}, f32[8,128,128]{2,1,0:T(8,128)}) custom-call(f32[32,384]{1,0:T(8,128)S(1)} %bitcast.5, f32[1024,128]{1,0:T(8,128)S(1)} %get-tuple-element.27.level_ref, bf16[32,128,128]{2,1,0:T(8,128)(2,1)S(1)} %copy-done.1, f32[1,32]{1,0:T(1,128)S(1)} %bitcast.7, s32[8]{0:T(128)S(1)} %copy-done.3), custom_call_target="tpu_custom_call" | custom-call | tf_op jit(solution)/shard_map/pallas_call | solution.py:385
  (2 shorter events, 0.0 us)
Async XLA Ops:
  0.6 9.1 %copy-start = (bf16[33,2,128,128]{3,2,1,0:T(8,128)(2,1)S(1)}, bf16[33,2,128,128]{3,2,1,0:T(8,128)(2,1)}, u32[]{:S(2)}) copy-start(bf16[33,2,128,128]{3,2,1,0:T(8,128)(2,1)} %factors_ref.7) | copy-start | bytes 6488068
  0.6 9.1 %copy-start.1 = (bf16[32,128,128]{2,1,0:T(8,128)(2,1)S(1)}, bf16[32,128,128]{2,1,0:T(8,128)(2,1)}, u32[]{:S(2)}) copy-start(bf16[32,128,128]{2,1,0:T(8,128)(2,1)} %forms_ref.3) | copy-start | bytes 3145732
  0.7 9.1 %copy-start.4 = (f32[8,128,128]{2,1,0:T(8,128)S(1)}, f32[8,128,128]{2,1,0:T(8,128)}, u32[]{:S(2)}) copy-start(f32[8,128,128]{2,1,0:T(8,128)} %hamiltonian_ref.1) | copy-start | bytes 1572868
  2.0 7.7 %collective-permute-start = (bf16[528,128]{1,0:T(8,128)(2,1)S(1)}, bf16[528,128]{1,0:T(8,128)(2,1)S(1)}, u32[]{:S(2)}, u32[]{:S(2)}) collective-permute-start(bf16[528,128]{1,0:T(8,128)(2,1)S(1)} %get-tuple-element.15.own_ref.packed_ref), channel_id=1, source_target_pairs={{0,1},{1,0},{2,3},{3,2},{4,5},{5,4},{6,7},{7,6},{8,9},{9,8},{10,11... | collective-permute-start | bytes 405512 | tf_op jit(solution)/shard_map/ppermute | solution.py:322
  2.5 12.6 %collective-permute-start.1 = (bf16[528,128]{1,0:T(8,128)(2,1)S(1)}, bf16[528,128]{1,0:T(8,128)(2,1)S(1)}, u32[]{:S(2)}, u32[]{:S(2)}) collective-permute-start(bf16[528,128]{1,0:T(8,128)(2,1)S(1)} %get-tuple-element.15.own_ref.packed_ref), channel_id=1, source_target_pairs={{0,2},{1,3},{2,0},{3,1},{4,6},{5,7},{6,4},{7,5},{8,10},{9,11},{10,... | collective-permute-start | bytes 405512 | tf_op jit(solution)/shard_map/ppermute | solution.py:323
  5.1 11.3 %collective-permute-start.3 = (bf16[528,128]{1,0:T(8,128)(2,1)S(1)}, bf16[528,128]{1,0:T(8,128)(2,1)S(1)}, u32[]{:S(2)}, u32[]{:S(2)}) collective-permute-start(bf16[528,128]{1,0:T(8,128)(2,1)S(1)} %shard_map.81), channel_id=1, source_target_pairs={{0,30},{1,31},{2,4},{3,5},{4,2},{5,3},{6,8},{7,9},{8,6},{9,7},{10,... | collective-permute-start | bytes 405512 | tf_op jit(solution)/shard_map/ppermute | solution.py:327
  15.2 3.2 %collective-permute-start.2 = (bf16[528,128]{1,0:T(8,128)(2,1)S(1)}, bf16[528,128]{1,0:T(8,128)(2,1)S(1)}, u32[]{:S(2)}, u32[]{:S(2)}) collective-permute-start(bf16[528,128]{1,0:T(8,128)(2,1)S(1)} %collective-permute-done.1.block_ref), channel_id=1, source_target_pairs={{0,1},{1,0},{2,3},{3,2},{4,5},{5,4},{6,7},{7,6},{8,9},{9,8},{10,11... | collective-permute-start | bytes 405512 | tf_op jit(solution)/shard_map/ppermute | solution.py:366
  16.5 1.8 %collective-permute-start.4 = (bf16[528,128]{1,0:T(8,128)(2,1)S(1)}, bf16[528,128]{1,0:T(8,128)(2,1)S(1)}, u32[]{:S(2)}, u32[]{:S(2)}) collective-permute-start(bf16[528,128]{1,0:T(8,128)(2,1)S(1)} %collective-permute-done.3.block_ref), channel_id=1, source_target_pairs={{0,1},{1,0},{2,3},{3,2},{4,5},{5,4},{6,7},{7,6},{8,9},{9,8},{10,11... | collective-permute-start | bytes 405512 | tf_op jit(solution)/shard_map/ppermute | solution.py:369
  18.3 12.6 %copy-start.2 = (f32[32]{0:T(128)S(1)}, f32[32]{0:T(128)}, u32[]{:S(2)}) copy-start(f32[32]{0:T(128)} %param.11) | copy-start | bytes 388
  18.3 12.6 %copy-start.3 = (s32[8]{0:T(128)S(1)}, s32[8]{0:T(128)}, u32[]{:S(2)}) copy-start(s32[8]{0:T(128)} %occupations_ref.1) | copy-start | bytes 100

commit v7 on v6

--- a/solution.py
+++ b/solution.py
@@ -145,14 +145,18 @@
     charge_ref[...] = lane_sums(rows[...])
 
 
-def turn_kernel(forms_ref, turned_ref, wide):
+def turn_kernel(forms_ref, turned_ref, traces_ref, wide, rows):
     form_count = forms_ref.shape[0]
+    row, col = square_iota()
     group = N // turned_ref.shape[0]
     for j in range(form_count):
-        wide[j * N : (j + 1) * N, :] = forms_ref[j].astype(F32)
+        form = forms_ref[j].astype(F32)
+        wide[j * N : (j + 1) * N, :] = form
+        rows[j : j + 1, :] = jnp.sum(jnp.where(row == col, form, 0.0), axis=0, keepdims=True)
     for at in range(turned_ref.shape[0]):
-        rows = [wide[pl.ds(at * group + row, form_count, stride=N), :] for row in range(group)]
-        turned_ref[at] = jnp.concatenate(rows, axis=0).T.astype(BF16)
+        parts = [wide[pl.ds(at * group + place, form_count, stride=N), :] for place in range(group)]
+        turned_ref[at] = jnp.concatenate(parts, axis=0).T.astype(BF16)
+    traces_ref[...] = lane_sums(rows[...])
 
 
 def side_kernel(second, block_ref, factors_ref, partial_ref, next_ref, blocks, products):
@@ -177,7 +181,7 @@
 
 
 def last_kernel(
-    even_ref, odd_ref, factors_ref, partial_ref, turned_ref, charge_ref, level_ref, stats_ref,
+    even_ref, odd_ref, factors_ref, partial_ref, turned_ref, traces_ref, charge_ref, level_ref, stats_ref,
     blocks, products, diagonals, squares,
 ):
     flipped = lax.rem(lax.axis_index("ka"), CORES) == 1
@@ -214,7 +218,6 @@
     place = lax.broadcasted_iota(jnp.int32, (KL, N), 0)
     group = N // turned_ref.shape[0]
     form_count = turned_ref.shape[2] // group
-    eye = jnp.where(row == col, 1.0, 0.0).astype(F32)
     table = jnp.zeros((2 * KL * group, group * form_count), F32)
     for at in range(0, N // group, 2):
         lefts = []
@@ -222,7 +225,6 @@
             highs, lows = [], []
             for k in range(KL):
                 values = level_ref[k * N + first : k * N + first + group, :]
-                values = values - mean[k : k + 1, :] * eye[first : first + group, :]
                 highs.append(values.astype(BF16).astype(F32))
                 lows.append(values - highs[-1])
             lefts.append(jnp.concatenate(highs + lows, axis=0).astype(BF16))
@@ -237,6 +239,7 @@
     overlaps = jnp.zeros((KL, form_count), F32)
     for at in range(group):
         overlaps = overlaps + table[:, at * form_count : (at + 1) * form_count]
+    overlaps = overlaps - mean * traces_ref[0:1, :]
     numbers = jnp.where(lane == form_count + place, norm, 0.0)
     numbers = numbers + jnp.where(lane == form_count + KL + place, mean, 0.0)
     charge = jnp.concatenate([charge_ref[0:1, :], jnp.zeros((1, N - form_count), F32)], axis=1)
@@ -353,12 +356,12 @@
         )(block, form_factors, partial)
 
     partial, hartree_forms = lax.optimization_barrier((partial, hartree_forms))
-    turned = pl.pallas_call(
+    turned, traces = pl.pallas_call(
         turn_kernel,
-        out_shape=shape((N * form_count // (2 * N), N, 2 * N), BF16),
+        out_shape=(shape((N * form_count // (2 * N), N, 2 * N), BF16), shape((8, form_count), F32)),
         in_specs=[VMEM],
-        out_specs=VMEM,
-        scratch_shapes=[pltpu.VMEM((form_count * N, N), F32)],
+        out_specs=(VMEM, VMEM),
+        scratch_shapes=[pltpu.VMEM((form_count * N, N), F32), pltpu.VMEM((form_count, N), F32)],
         compiler_params=params(16),
         cost_estimate=side_cost,
     )(hartree_forms)
@@ -371,7 +374,7 @@
     level, stats = pl.pallas_call(
         last_kernel,
         out_shape=(shape((KL * N, N), F32), shape((count, KL * form_count + N), F32)),
-        in_specs=[VMEM] * 6,
+        in_specs=[VMEM] * 7,
         out_specs=(VMEM, VMEM),
         scratch_shapes=[
             pltpu.VMEM((KL, N, N), BF16),
@@ -380,7 +383,7 @@
             pltpu.VMEM((KL, N), F32),
         ],
         compiler_params=params(28),
-    )(even_across, odd_across, form_factors, partial, turned, charge)
+    )(even_across, odd_across, form_factors, partial, turned, traces, charge)
     shared = lax.all_to_all(stats, "ka", 0, 0, tiled=True)
     return pl.pallas_call(
         final_kernel,

time: 34.7 us -> 34.7 us (level)
  no operation moved by 1% of the time
where the time goes in v7:
time: 34.7 us; the launch traced here: 34.5 us
  Pallas kernels  16 us (46%)
  blocking collectives  9.42 us (27%)
  starting transfers between devices  8.31 us (24%)
  between operations  0.77 us (2%)
    all_to_all x1, blocking collectives, per_device(): shared = lax.all_to_all(stats, 'ka', 0, 0, tiled=True)  9.42 us
    ppermute x1, starting transfers between devices, per_device(): odd = lax.ppermute(again, 'ka', between)  4.59 us
    pallas_call x1, Pallas kernels, per_device(): pl.pallas_call(inner_kernel, out_shape=(shape((KL, N, N), F32), shape((8,...  4.05 us
    pallas_call x1, Pallas kernels, per_device(): pl.pallas_call(final_kernel, out_shape=(shape((KL, N, N), F32), shape((KL...  3.64 us
    pallas_call x1, Pallas kernels, per_device(): pl.pallas_call(last_kernel, out_shape=(shape((KL * N, N), F32), shape((co...  2.94 us
    ppermute x1, starting transfers between devices, per_device(): even = lax.ppermute(packed, 'ka', within)  2.56 us
    pallas_call x2, Pallas kernels, side(): pl.pallas_call(functools.partial(side_kernel, second), out_shape=shape((K...  2.46 us
    pallas_call x1, Pallas kernels, per_device(): pl.pallas_call(turn_kernel, out_shape=(shape((N * form_count // (2 * N),...  1.48 us
  transfers between devices with their start and end apart: 5, of which 0 were waited for; matrix products, arithmetic and copies ran while one was open for 0% of the time, Pallas kernels for 23%

profile of v7, /device:TPU:0, one launch (start us, length us, event | category | flops | bytes accessed | tf_op | source)
XLA Modules:
  0.0 34.5 jit_solution(9050185807504736078)
XLA Ops:
  0.6 0.0 copy-start
  0.6 0.0 copy-start.1
  0.7 0.0 copy-start.4
  0.7 1.4 %shard_map.77 = (bf16[528,128]{1,0:T(8,128)(2,1)S(1)}, f32[128,128]{1,0:T(8,128)S(1)}) custom-call(f32[8,128,128]{2,1,0:T(8,128)} %density_hbm.1), custom_call_target="tpu_custom_call" | custom-call | flops 5000000000 | bytes 2000000 | tf_op jit(solution)/shard_map/pallas_call | solution.py:312
  2.0 0.5 %collective-permute-start = (bf16[528,128]{1,0:T(8,128)(2,1)S(1)}, bf16[528,128]{1,0:T(8,128)(2,1)S(1)}, u32[]{:S(2)}, u32[]{:S(2)}) collective-permute-start(bf16[528,128]{1,0:T(8,128)(2,1)S(1)} %get-tuple-element.17.own_ref.packed_ref), channel_id=1, source_target_pairs={{0,1},{1,0},{2,3},{3,2},{4,5},{5,4},{6,7},{7,6},{8,9},{9,8},{10,11... | collective-permute-start | bytes 405512 | tf_op jit(solution)/shard_map/ppermute | solution.py:325
  2.5 2.6 %collective-permute-start.1 = (bf16[528,128]{1,0:T(8,128)(2,1)S(1)}, bf16[528,128]{1,0:T(8,128)(2,1)S(1)}, u32[]{:S(2)}, u32[]{:S(2)}) collective-permute-start(bf16[528,128]{1,0:T(8,128)(2,1)S(1)} %get-tuple-element.17.own_ref.packed_ref), channel_id=1, source_target_pairs={{0,2},{1,3},{2,0},{3,1},{4,6},{5,7},{6,4},{7,5},{8,10},{9,11},{10,... | collective-permute-start | bytes 405512 | tf_op jit(solution)/shard_map/ppermute | solution.py:326
  5.1 4.6 %collective-permute-start.3 = (bf16[528,128]{1,0:T(8,128)(2,1)S(1)}, bf16[528,128]{1,0:T(8,128)(2,1)S(1)}, u32[]{:S(2)}, u32[]{:S(2)}) collective-permute-start(bf16[528,128]{1,0:T(8,128)(2,1)S(1)} %shard_map.81), channel_id=1, source_target_pairs={{0,30},{1,31},{2,4},{3,5},{4,2},{5,3},{6,8},{7,9},{8,6},{9,7},{10,... | collective-permute-start | bytes 405512 | tf_op jit(solution)/shard_map/ppermute | solution.py:330
  9.7 0.0 collective-permute-done.other_ref
  9.7 0.0 copy-done
  9.7 0.0 copy-done.1
  9.7 0.0 copy-done.4
  9.7 4.1 %shard_map.78 = (f32[8,128,128]{2,1,0:T(8,128)S(1)}, f32[8,32]{1,0:T(8,128)S(1)}) custom-call(bf16[528,128]{1,0:T(8,128)(2,1)S(1)} %get-tuple-element.17.own_ref.packed_ref, bf16[528,128]{1,0:T(8,128)(2,1)S(1)} %collective-permute-done.other_ref, bf16[33,2,128,128]{3,2,1,0:T(8,128)(2,1)S(1)} %copy-done, f32[8,128,128]{2,1,0:T(8,128)S(1)} %copy-done.4, ...), custom_call_target="tpu_custom_call" | custom-call | flops 5000000000 | bytes 5000000 | tf_op jit(solution)/shard_map/pallas_call | solution.py:331
  13.8 1.5 %shard_map.79 = (bf16[16,128,256]{2,1,0:T(8,128)(2,1)S(1)}, f32[8,32]{1,0:T(8,128)S(1)}) custom-call(bf16[32,128,128]{2,1,0:T(8,128)(2,1)S(1)} %copy-done.1), custom_call_target="tpu_custom_call" | custom-call | flops 2000000000 | bytes 5000000 | tf_op jit(solution)/shard_map/pallas_call | solution.py:359
  15.3 0.0 collective-permute-done.1.block_ref
  15.3 0.1 collective-permute-start.2
  15.4 1.2 %shard_map.80.partial_ref = f32[8,128,128]{2,1,0:T(8,128)S(1)} custom-call(bf16[528,128]{1,0:T(8,128)(2,1)S(1)} %collective-permute-done.1.block_ref, bf16[33,2,128,128]{3,2,1,0:T(8,128)(2,1)S(1)} %copy-done, f32[8,128,128]{2,1,0:T(8,128)S(1)} %get-tuple-element.24.partial_ref), custom_call_target="tpu_custom_call" | custom-call | flops 2000000000 | bytes 5000000 | tf_op jit(solution)/shard_map/pallas_call | solution.py:348
  16.6 0.0 collective-permute-done.3.block_ref
  16.6 0.6 %collective-permute-start.4 = (bf16[528,128]{1,0:T(8,128)(2,1)S(1)}, bf16[528,128]{1,0:T(8,128)(2,1)S(1)}, u32[]{:S(2)}, u32[]{:S(2)}) collective-permute-start(bf16[528,128]{1,0:T(8,128)(2,1)S(1)} %collective-permute-done.3.block_ref), channel_id=1, source_target_pairs={{0,1},{1,0},{2,3},{3,2},{4,5},{5,4},{6,7},{7,6},{8,9},{9,8},{10,11... | collective-permute-start | bytes 405512 | tf_op jit(solution)/shard_map/ppermute | solution.py:372
  17.2 1.2 %shard_map.82.partial_ref = f32[8,128,128]{2,1,0:T(8,128)S(1)} custom-call(bf16[528,128]{1,0:T(8,128)(2,1)S(1)} %collective-permute-done.3.block_ref, bf16[33,2,128,128]{3,2,1,0:T(8,128)(2,1)S(1)} %copy-done, f32[8,128,128]{2,1,0:T(8,128)S(1)} %shard_map.80.partial_ref), custom_call_target="tpu_custom_call" | custom-call | flops 2000000000 | bytes 5000000 | tf_op jit(solution)/shard_map/pallas_call | solution.py:348
  18.4 0.0 copy-start.2
  18.4 0.0 copy-start.3
  18.4 0.0 collective-permute-done.4.odd_ref
  18.4 0.0 collective-permute-done.2.even_ref
  18.5 2.9 %shard_map.83 = (f32[1024,128]{1,0:T(8,128)S(1)}, f32[32,384]{1,0:T(8,128)S(1)}) custom-call(bf16[528,128]{1,0:T(8,128)(2,1)S(1)} %collective-permute-done.2.even_ref, bf16[528,128]{1,0:T(8,128)(2,1)S(1)} %collective-permute-done.4.odd_ref, bf16[33,2,128,128]{3,2,1,0:T(8,128)(2,1)S(1)} %copy-done, f32[8,128,128]{2,1,0:T(8,128)S(1)} %shard_map.82.partial_ref, ...), custom_call_target="tpu_custom_call" | custom-call | tf_op jit(solution)/shard_map/pallas_call | solution.py:374
  21.4 0.1 copy.8
  21.5 9.4 %all_to_all.11 = f32[32,1,384]{2,1,0:T(1,128)S(1)} all-to-all(f32[32,1,384]{2,1,0:T(1,128)S(1)} %copy.8), channel_id=1, replica_groups=mesh['ka'=32] {'ka'}, dimensions={0} | all-to-all | bytes 98304 | tf_op jit(solution)/shard_map/all_to_all | solution.py:387
  30.9 0.0 copy-done.2
  30.9 0.0 copy-done.3
  30.9 3.6 %shard_map.84 = (f32[8,128,128]{2,1,0:T(8,128)}, f32[8,128,128]{2,1,0:T(8,128)}) custom-call(f32[32,384]{1,0:T(8,128)S(1)} %bitcast.5, f32[1024,128]{1,0:T(8,128)S(1)} %get-tuple-element.31.level_ref, bf16[32,128,128]{2,1,0:T(8,128)(2,1)S(1)} %copy-done.1, f32[1,32]{1,0:T(1,128)S(1)} %bitcast.7, s32[8]{0:T(128)S(1)} %copy-done.3), custom_call_target="tpu_custom_call" | custom-call | tf_op jit(solution)/shard_map/pallas_call | solution.py:388
  (2 shorter events, 0.0 us)
Async XLA Ops:
  0.6 9.1 %copy-start = (bf16[33,2,128,128]{3,2,1,0:T(8,128)(2,1)S(1)}, bf16[33,2,128,128]{3,2,1,0:T(8,128)(2,1)}, u32[]{:S(2)}) copy-start(bf16[33,2,128,128]{3,2,1,0:T(8,128)(2,1)} %factors_ref.7) | copy-start | bytes 6488068
  0.6 9.1 %copy-start.1 = (bf16[32,128,128]{2,1,0:T(8,128)(2,1)S(1)}, bf16[32,128,128]{2,1,0:T(8,128)(2,1)}, u32[]{:S(2)}) copy-start(bf16[32,128,128]{2,1,0:T(8,128)(2,1)} %forms_ref.3) | copy-start | bytes 3145732
  0.7 9.1 %copy-start.4 = (f32[8,128,128]{2,1,0:T(8,128)S(1)}, f32[8,128,128]{2,1,0:T(8,128)}, u32[]{:S(2)}) copy-start(f32[8,128,128]{2,1,0:T(8,128)} %hamiltonian_ref.1) | copy-start | bytes 1572868
  2.0 7.7 %collective-permute-start = (bf16[528,128]{1,0:T(8,128)(2,1)S(1)}, bf16[528,128]{1,0:T(8,128)(2,1)S(1)}, u32[]{:S(2)}, u32[]{:S(2)}) collective-permute-start(bf16[528,128]{1,0:T(8,128)(2,1)S(1)} %get-tuple-element.17.own_ref.packed_ref), channel_id=1, source_target_pairs={{0,1},{1,0},{2,3},{3,2},{4,5},{5,4},{6,7},{7,6},{8,9},{9,8},{10,11... | collective-permute-start | bytes 405512 | tf_op jit(solution)/shard_map/ppermute | solution.py:325
  2.5 12.7 %collective-permute-start.1 = (bf16[528,128]{1,0:T(8,128)(2,1)S(1)}, bf16[528,128]{1,0:T(8,128)(2,1)S(1)}, u32[]{:S(2)}, u32[]{:S(2)}) collective-permute-start(bf16[528,128]{1,0:T(8,128)(2,1)S(1)} %get-tuple-element.17.own_ref.packed_ref), channel_id=1, source_target_pairs={{0,2},{1,3},{2,0},{3,1},{4,6},{5,7},{6,4},{7,5},{8,10},{9,11},{10,... | collective-permute-start | bytes 405512 | tf_op jit(solution)/shard_map/ppermute | solution.py:326
  5.1 11.5 %collective-permute-start.3 = (bf16[528,128]{1,0:T(8,128)(2,1)S(1)}, bf16[528,128]{1,0:T(8,128)(2,1)S(1)}, u32[]{:S(2)}, u32[]{:S(2)}) collective-permute-start(bf16[528,128]{1,0:T(8,128)(2,1)S(1)} %shard_map.81), channel_id=1, source_target_pairs={{0,30},{1,31},{2,4},{3,5},{4,2},{5,3},{6,8},{7,9},{8,6},{9,7},{10,... | collective-permute-start | bytes 405512 | tf_op jit(solution)/shard_map/ppermute | solution.py:330
  15.3 3.2 %collective-permute-start.2 = (bf16[528,128]{1,0:T(8,128)(2,1)S(1)}, bf16[528,128]{1,0:T(8,128)(2,1)S(1)}, u32[]{:S(2)}, u32[]{:S(2)}) collective-permute-start(bf16[528,128]{1,0:T(8,128)(2,1)S(1)} %collective-permute-done.1.block_ref), channel_id=1, source_target_pairs={{0,1},{1,0},{2,3},{3,2},{4,5},{5,4},{6,7},{7,6},{8,9},{9,8},{10,11... | collective-permute-start | bytes 405512 | tf_op jit(solution)/shard_map/ppermute | solution.py:369
  16.6 1.8 %collective-permute-start.4 = (bf16[528,128]{1,0:T(8,128)(2,1)S(1)}, bf16[528,128]{1,0:T(8,128)(2,1)S(1)}, u32[]{:S(2)}, u32[]{:S(2)}) collective-permute-start(bf16[528,128]{1,0:T(8,128)(2,1)S(1)} %collective-permute-done.3.block_ref), channel_id=1, source_target_pairs={{0,1},{1,0},{2,3},{3,2},{4,5},{5,4},{6,7},{7,6},{8,9},{9,8},{10,11... | collective-permute-start | bytes 405512 | tf_op jit(solution)/shard_map/ppermute | solution.py:372
  18.4 12.5 %copy-start.2 = (f32[32]{0:T(128)S(1)}, f32[32]{0:T(128)}, u32[]{:S(2)}) copy-start(f32[32]{0:T(128)} %param.11) | copy-start | bytes 388
  18.4 12.5 %copy-start.3 = (s32[8]{0:T(128)S(1)}, s32[8]{0:T(128)}, u32[]{:S(2)}) copy-start(s32[8]{0:T(128)} %occupations_ref.1) | copy-start | bytes 100

commit v8 on v6

--- a/solution.py
+++ b/solution.py
@@ -145,14 +145,13 @@
     charge_ref[...] = lane_sums(rows[...])
 
 
-def turn_kernel(forms_ref, turned_ref, wide):
-    form_count = forms_ref.shape[0]
+def turn_kernel(forms_ref, turned_ref):
     group = N // turned_ref.shape[0]
-    for j in range(form_count):
-        wide[j * N : (j + 1) * N, :] = forms_ref[j].astype(F32)
-    for at in range(turned_ref.shape[0]):
-        rows = [wide[pl.ds(at * group + row, form_count, stride=N), :] for row in range(group)]
-        turned_ref[at] = jnp.concatenate(rows, axis=0).T.astype(BF16)
+    for at in range(0, turned_ref.shape[0], 2):
+        rows = forms_ref[:, at * group : (at + 2) * group, :].astype(F32)
+        for half in range(2):
+            part = rows[:, half * group : (half + 1) * group, :]
+            turned_ref[at + half] = part.reshape(-1, N).T.astype(BF16)
 
 
 def side_kernel(second, block_ref, factors_ref, partial_ref, next_ref, blocks, products):
@@ -230,13 +229,17 @@
             jnp.concatenate(lefts, axis=1), turned_ref[at : at + 2].reshape(2 * N, -1), preferred_element_type=F32
         )
     at_row = lax.broadcasted_iota(jnp.int32, table.shape, 0) % group
-    at_lane = lax.broadcasted_iota(jnp.int32, table.shape, 1) // form_count
+    at_lane = lax.broadcasted_iota(jnp.int32, table.shape, 1) % group
     table = jnp.where(at_row == at_lane, table, 0.0)
     table = jnp.sum(table.reshape(2 * KL, group, group * form_count), axis=1)
     table = table[:KL, :] + table[KL:, :]
-    overlaps = jnp.zeros((KL, form_count), F32)
-    for at in range(group):
-        overlaps = overlaps + table[:, at * form_count : (at + 1) * form_count]
+    high = table.astype(BF16)
+    low = (table - high.astype(F32)).astype(BF16)
+    of_form = lax.broadcasted_iota(jnp.int32, (2 * group * form_count, form_count), 0) // group % form_count
+    ones = lax.broadcasted_iota(jnp.int32, of_form.shape, 1) == of_form
+    overlaps = jnp.dot(
+        jnp.concatenate([high, low], axis=1), jnp.where(ones, 1.0, 0.0).astype(BF16), preferred_element_type=F32
+    )
     numbers = jnp.where(lane == form_count + place, norm, 0.0)
     numbers = numbers + jnp.where(lane == form_count + KL + place, mean, 0.0)
     charge = jnp.concatenate([charge_ref[0:1, :], jnp.zeros((1, N - form_count), F32)], axis=1)
@@ -358,7 +361,6 @@
         out_shape=shape((N * form_count // (2 * N), N, 2 * N), BF16),
         in_specs=[VMEM],
         out_specs=VMEM,
-        scratch_shapes=[pltpu.VMEM((form_count * N, N), F32)],
         compiler_params=params(16),
         cost_estimate=side_cost,
     )(hartree_forms)

time: 34.7 us -> 34.8 us (level)
  Pallas kernels: 15.9 us -> 14.9 us
  blocking collectives: 9.54 us -> 10.5 us
    all_to_all x1, blocking collectives: 9.54 us -> 10.5 us  [per_device(): shared = lax.all_to_all(stats, 'ka', 0, 0, tiled=True)]
    pallas_call x1, Pallas kernels: 1.35 us -> 0.34 us  [per_device(): pl.pallas_call(turn_kernel, out_shape=shape((N * form_count // (2 * N), N...]
  transfers between devices with their start and end apart: 5 -> 5, of which waited for: 0 -> 0; matrix products, arithmetic and copies ran while one was open for 0% -> 0% of each run, Pallas kernels for 23% -> 20%
where the time goes in v8:
time: 34.8 us; the launch traced here: 34.6 us
  Pallas kernels  14.9 us (43%)
  blocking collectives  10.5 us (30%)
  starting transfers between devices  8.31 us (24%)
  between operations  0.77 us (2%)
    all_to_all x1, blocking collectives, per_device(): shared = lax.all_to_all(stats, 'ka', 0, 0, tiled=True)  10.5 us
    ppermute x1, starting transfers between devices, per_device(): odd = lax.ppermute(again, 'ka', between)  4.59 us
    pallas_call x1, Pallas kernels, per_device(): pl.pallas_call(inner_kernel, out_shape=(shape((KL, N, N), F32), shape((8,...  4.05 us
    pallas_call x1, Pallas kernels, per_device(): pl.pallas_call(final_kernel, out_shape=(shape((KL, N, N), F32), shape((KL...  3.65 us
    pallas_call x1, Pallas kernels, per_device(): pl.pallas_call(last_kernel, out_shape=(shape((KL * N, N), F32), shape((co...  3.03 us
    ppermute x1, starting transfers between devices, per_device(): even = lax.ppermute(packed, 'ka', within)  2.56 us
    pallas_call x2, Pallas kernels, side(): pl.pallas_call(functools.partial(side_kernel, second), out_shape=shape((K...  2.47 us
    pallas_call x1, Pallas kernels, per_device(): pl.pallas_call(pack_kernel, out_shape=(shape((PACK, N), BF16), shape((N,...  1.36 us
  transfers between devices with their start and end apart: 5, of which 0 were waited for; matrix products, arithmetic and copies ran while one was open for 0% of the time, Pallas kernels for 20%

profile of v8, /device:TPU:0, one launch (start us, length us, event | category | flops | bytes accessed | tf_op | source)
XLA Modules:
  0.0 34.6 jit_solution(11692648855114190536)
XLA Ops:
  0.6 0.0 copy-start
  0.6 0.0 copy-start.1
  0.7 0.0 copy-start.4
  0.7 1.4 %shard_map.77 = (bf16[528,128]{1,0:T(8,128)(2,1)S(1)}, f32[128,128]{1,0:T(8,128)S(1)}) custom-call(f32[8,128,128]{2,1,0:T(8,128)} %density_hbm.1), custom_call_target="tpu_custom_call" | custom-call | flops 5000000000 | bytes 2000000 | tf_op jit(solution)/shard_map/pallas_call | solution.py:312
  2.0 0.5 %collective-permute-start = (bf16[528,128]{1,0:T(8,128)(2,1)S(1)}, bf16[528,128]{1,0:T(8,128)(2,1)S(1)}, u32[]{:S(2)}, u32[]{:S(2)}) collective-permute-start(bf16[528,128]{1,0:T(8,128)(2,1)S(1)} %get-tuple-element.15.own_ref.packed_ref), channel_id=1, source_target_pairs={{0,1},{1,0},{2,3},{3,2},{4,5},{5,4},{6,7},{7,6},{8,9},{9,8},{10,11... | collective-permute-start | bytes 405512 | tf_op jit(solution)/shard_map/ppermute | solution.py:325
  2.5 2.6 %collective-permute-start.1 = (bf16[528,128]{1,0:T(8,128)(2,1)S(1)}, bf16[528,128]{1,0:T(8,128)(2,1)S(1)}, u32[]{:S(2)}, u32[]{:S(2)}) collective-permute-start(bf16[528,128]{1,0:T(8,128)(2,1)S(1)} %get-tuple-element.15.own_ref.packed_ref), channel_id=1, source_target_pairs={{0,2},{1,3},{2,0},{3,1},{4,6},{5,7},{6,4},{7,5},{8,10},{9,11},{10,... | collective-permute-start | bytes 405512 | tf_op jit(solution)/shard_map/ppermute | solution.py:326
  5.1 4.6 %collective-permute-start.3 = (bf16[528,128]{1,0:T(8,128)(2,1)S(1)}, bf16[528,128]{1,0:T(8,128)(2,1)S(1)}, u32[]{:S(2)}, u32[]{:S(2)}) collective-permute-start(bf16[528,128]{1,0:T(8,128)(2,1)S(1)} %shard_map.81), channel_id=1, source_target_pairs={{0,30},{1,31},{2,4},{3,5},{4,2},{5,3},{6,8},{7,9},{8,6},{9,7},{10,... | collective-permute-start | bytes 405512 | tf_op jit(solution)/shard_map/ppermute | solution.py:330
  9.7 0.0 collective-permute-done.other_ref
  9.7 0.0 copy-done
  9.7 0.0 copy-done.1
  9.7 0.0 copy-done.4
  9.7 4.1 %shard_map.78 = (f32[8,128,128]{2,1,0:T(8,128)S(1)}, f32[8,32]{1,0:T(8,128)S(1)}) custom-call(bf16[528,128]{1,0:T(8,128)(2,1)S(1)} %get-tuple-element.15.own_ref.packed_ref, bf16[528,128]{1,0:T(8,128)(2,1)S(1)} %collective-permute-done.other_ref, bf16[33,2,128,128]{3,2,1,0:T(8,128)(2,1)S(1)} %copy-done, f32[8,128,128]{2,1,0:T(8,128)S(1)} %copy-done.4, ...), custom_call_target="tpu_custom_call" | custom-call | flops 5000000000 | bytes 5000000 | tf_op jit(solution)/shard_map/pallas_call | solution.py:331
  13.8 0.3 shard_map.79.turned_ref
  14.1 0.0 collective-permute-done.1.block_ref
  14.1 0.1 collective-permute-start.2
  14.2 1.2 %shard_map.80.partial_ref = f32[8,128,128]{2,1,0:T(8,128)S(1)} custom-call(bf16[528,128]{1,0:T(8,128)(2,1)S(1)} %collective-permute-done.1.block_ref, bf16[33,2,128,128]{3,2,1,0:T(8,128)(2,1)S(1)} %copy-done, f32[8,128,128]{2,1,0:T(8,128)S(1)} %get-tuple-element.21.partial_ref), custom_call_target="tpu_custom_call" | custom-call | flops 2000000000 | bytes 5000000 | tf_op jit(solution)/shard_map/pallas_call | solution.py:348
  15.5 0.0 collective-permute-done.3.block_ref
  15.5 0.6 %collective-permute-start.4 = (bf16[528,128]{1,0:T(8,128)(2,1)S(1)}, bf16[528,128]{1,0:T(8,128)(2,1)S(1)}, u32[]{:S(2)}, u32[]{:S(2)}) collective-permute-start(bf16[528,128]{1,0:T(8,128)(2,1)S(1)} %collective-permute-done.3.block_ref), channel_id=1, source_target_pairs={{0,1},{1,0},{2,3},{3,2},{4,5},{5,4},{6,7},{7,6},{8,9},{9,8},{10,11... | collective-permute-start | bytes 405512 | tf_op jit(solution)/shard_map/ppermute | solution.py:371
  16.0 1.2 %shard_map.82.partial_ref = f32[8,128,128]{2,1,0:T(8,128)S(1)} custom-call(bf16[528,128]{1,0:T(8,128)(2,1)S(1)} %collective-permute-done.3.block_ref, bf16[33,2,128,128]{3,2,1,0:T(8,128)(2,1)S(1)} %copy-done, f32[8,128,128]{2,1,0:T(8,128)S(1)} %shard_map.80.partial_ref), custom_call_target="tpu_custom_call" | custom-call | flops 2000000000 | bytes 5000000 | tf_op jit(solution)/shard_map/pallas_call | solution.py:348
  17.3 0.0 copy-start.2
  17.3 0.0 copy-start.3
  17.3 0.0 collective-permute-done.4.odd_ref
  17.3 0.0 collective-permute-done.2.even_ref
  17.3 3.0 %shard_map.83 = (f32[1024,128]{1,0:T(8,128)S(1)}, f32[32,384]{1,0:T(8,128)S(1)}) custom-call(bf16[528,128]{1,0:T(8,128)(2,1)S(1)} %collective-permute-done.2.even_ref, bf16[528,128]{1,0:T(8,128)(2,1)S(1)} %collective-permute-done.4.odd_ref, bf16[33,2,128,128]{3,2,1,0:T(8,128)(2,1)S(1)} %copy-done, f32[8,128,128]{2,1,0:T(8,128)S(1)} %shard_map.82.partial_ref, ...), custom_call_target="tpu_custom_call" | custom-call | tf_op jit(solution)/shard_map/pallas_call | solution.py:373
  20.4 0.1 copy.8
  20.4 10.5 %all_to_all.11 = f32[32,1,384]{2,1,0:T(1,128)S(1)} all-to-all(f32[32,1,384]{2,1,0:T(1,128)S(1)} %copy.8), channel_id=1, replica_groups=mesh['ka'=32] {'ka'}, dimensions={0} | all-to-all | bytes 98304 | tf_op jit(solution)/shard_map/all_to_all | solution.py:386
  31.0 0.0 copy-done.2
  31.0 0.0 copy-done.3
  31.0 3.6 %shard_map.84 = (f32[8,128,128]{2,1,0:T(8,128)}, f32[8,128,128]{2,1,0:T(8,128)}) custom-call(f32[32,384]{1,0:T(8,128)S(1)} %bitcast.5, f32[1024,128]{1,0:T(8,128)S(1)} %get-tuple-element.27.level_ref, bf16[32,128,128]{2,1,0:T(8,128)(2,1)S(1)} %copy-done.1, f32[1,32]{1,0:T(1,128)S(1)} %bitcast.7, s32[8]{0:T(128)S(1)} %copy-done.3), custom_call_target="tpu_custom_call" | custom-call | tf_op jit(solution)/shard_map/pallas_call | solution.py:387
  (2 shorter events, 0.0 us)
Async XLA Ops:
  0.6 9.1 %copy-start = (bf16[33,2,128,128]{3,2,1,0:T(8,128)(2,1)S(1)}, bf16[33,2,128,128]{3,2,1,0:T(8,128)(2,1)}, u32[]{:S(2)}) copy-start(bf16[33,2,128,128]{3,2,1,0:T(8,128)(2,1)} %factors_ref.7) | copy-start | bytes 6488068
  0.6 9.1 %copy-start.1 = (bf16[32,128,128]{2,1,0:T(8,128)(2,1)S(1)}, bf16[32,128,128]{2,1,0:T(8,128)(2,1)}, u32[]{:S(2)}) copy-start(bf16[32,128,128]{2,1,0:T(8,128)(2,1)} %forms_ref.3) | copy-start | bytes 3145732
  0.7 9.1 %copy-start.4 = (f32[8,128,128]{2,1,0:T(8,128)S(1)}, f32[8,128,128]{2,1,0:T(8,128)}, u32[]{:S(2)}) copy-start(f32[8,128,128]{2,1,0:T(8,128)} %hamiltonian_ref.1) | copy-start | bytes 1572868
  2.0 7.7 %collective-permute-start = (bf16[528,128]{1,0:T(8,128)(2,1)S(1)}, bf16[528,128]{1,0:T(8,128)(2,1)S(1)}, u32[]{:S(2)}, u32[]{:S(2)}) collective-permute-start(bf16[528,128]{1,0:T(8,128)(2,1)S(1)} %get-tuple-element.15.own_ref.packed_ref), channel_id=1, source_target_pairs={{0,1},{1,0},{2,3},{3,2},{4,5},{5,4},{6,7},{7,6},{8,9},{9,8},{10,11... | collective-permute-start | bytes 405512 | tf_op jit(solution)/shard_map/ppermute | solution.py:325
  2.5 11.6 %collective-permute-start.1 = (bf16[528,128]{1,0:T(8,128)(2,1)S(1)}, bf16[528,128]{1,0:T(8,128)(2,1)S(1)}, u32[]{:S(2)}, u32[]{:S(2)}) collective-permute-start(bf16[528,128]{1,0:T(8,128)(2,1)S(1)} %get-tuple-element.15.own_ref.packed_ref), channel_id=1, source_target_pairs={{0,2},{1,3},{2,0},{3,1},{4,6},{5,7},{6,4},{7,5},{8,10},{9,11},{10,... | collective-permute-start | bytes 405512 | tf_op jit(solution)/shard_map/ppermute | solution.py:326
  5.1 10.3 %collective-permute-start.3 = (bf16[528,128]{1,0:T(8,128)(2,1)S(1)}, bf16[528,128]{1,0:T(8,128)(2,1)S(1)}, u32[]{:S(2)}, u32[]{:S(2)}) collective-permute-start(bf16[528,128]{1,0:T(8,128)(2,1)S(1)} %shard_map.81), channel_id=1, source_target_pairs={{0,30},{1,31},{2,4},{3,5},{4,2},{5,3},{6,8},{7,9},{8,6},{9,7},{10,... | collective-permute-start | bytes 405512 | tf_op jit(solution)/shard_map/ppermute | solution.py:330
  14.1 3.2 %collective-permute-start.2 = (bf16[528,128]{1,0:T(8,128)(2,1)S(1)}, bf16[528,128]{1,0:T(8,128)(2,1)S(1)}, u32[]{:S(2)}, u32[]{:S(2)}) collective-permute-start(bf16[528,128]{1,0:T(8,128)(2,1)S(1)} %collective-permute-done.1.block_ref), channel_id=1, source_target_pairs={{0,1},{1,0},{2,3},{3,2},{4,5},{5,4},{6,7},{7,6},{8,9},{9,8},{10,11... | collective-permute-start | bytes 405512 | tf_op jit(solution)/shard_map/ppermute | solution.py:368
  15.5 1.8 %collective-permute-start.4 = (bf16[528,128]{1,0:T(8,128)(2,1)S(1)}, bf16[528,128]{1,0:T(8,128)(2,1)S(1)}, u32[]{:S(2)}, u32[]{:S(2)}) collective-permute-start(bf16[528,128]{1,0:T(8,128)(2,1)S(1)} %collective-permute-done.3.block_ref), channel_id=1, source_target_pairs={{0,1},{1,0},{2,3},{3,2},{4,5},{5,4},{6,7},{7,6},{8,9},{9,8},{10,11... | collective-permute-start | bytes 405512 | tf_op jit(solution)/shard_map/ppermute | solution.py:371
  17.3 13.7 %copy-start.2 = (f32[32]{0:T(128)S(1)}, f32[32]{0:T(128)}, u32[]{:S(2)}) copy-start(f32[32]{0:T(128)} %param.11) | copy-start | bytes 388
  17.3 13.7 %copy-start.3 = (s32[8]{0:T(128)S(1)}, s32[8]{0:T(128)}, u32[]{:S(2)}) copy-start(s32[8]{0:T(128)} %occupations_ref.1) | copy-start | bytes 100

commit v9 on v8

--- a/solution.py
+++ b/solution.py
@@ -145,7 +145,11 @@
     charge_ref[...] = lane_sums(rows[...])
 
 
-def turn_kernel(forms_ref, turned_ref):
+def turn_kernel(forms_ref, turned_ref, traces_ref, rows):
+    row, col = square_iota()
+    for j in range(forms_ref.shape[0]):
+        rows[j : j + 1, :] = jnp.sum(jnp.where(row == col, forms_ref[j].astype(F32), 0.0), axis=0, keepdims=True)
+    traces_ref[...] = lane_sums(rows[...])
     group = N // turned_ref.shape[0]
     for at in range(0, turned_ref.shape[0], 2):
         rows = forms_ref[:, at * group : (at + 2) * group, :].astype(F32)
@@ -176,7 +180,7 @@
 
 
 def last_kernel(
-    even_ref, odd_ref, factors_ref, partial_ref, turned_ref, charge_ref, level_ref, stats_ref,
+    even_ref, odd_ref, factors_ref, partial_ref, turned_ref, traces_ref, charge_ref, level_ref, stats_ref,
     blocks, products, diagonals, squares,
 ):
     flipped = lax.rem(lax.axis_index("ka"), CORES) == 1
@@ -213,7 +217,6 @@
     place = lax.broadcasted_iota(jnp.int32, (KL, N), 0)
     group = N // turned_ref.shape[0]
     form_count = turned_ref.shape[2] // group
-    eye = jnp.where(row == col, 1.0, 0.0).astype(F32)
     table = jnp.zeros((2 * KL * group, group * form_count), F32)
     for at in range(0, N // group, 2):
         lefts = []
@@ -221,7 +224,6 @@
             highs, lows = [], []
             for k in range(KL):
                 values = level_ref[k * N + first : k * N + first + group, :]
-                values = values - mean[k : k + 1, :] * eye[first : first + group, :]
                 highs.append(values.astype(BF16).astype(F32))
                 lows.append(values - highs[-1])
             lefts.append(jnp.concatenate(highs + lows, axis=0).astype(BF16))
@@ -240,6 +242,7 @@
     overlaps = jnp.dot(
         jnp.concatenate([high, low], axis=1), jnp.where(ones, 1.0, 0.0).astype(BF16), preferred_element_type=F32
     )
+    overlaps = overlaps - mean * traces_ref[0:1, :]
     numbers = jnp.where(lane == form_count + place, norm, 0.0)
     numbers = numbers + jnp.where(lane == form_count + KL + place, mean, 0.0)
     charge = jnp.concatenate([charge_ref[0:1, :], jnp.zeros((1, N - form_count), F32)], axis=1)
@@ -356,11 +359,12 @@
         )(block, form_factors, partial)
 
     partial, hartree_forms = lax.optimization_barrier((partial, hartree_forms))
-    turned = pl.pallas_call(
+    turned, traces = pl.pallas_call(
         turn_kernel,
-        out_shape=shape((N * form_count // (2 * N), N, 2 * N), BF16),
+        out_shape=(shape((N * form_count // (2 * N), N, 2 * N), BF16), shape((8, form_count), F32)),
         in_specs=[VMEM],
-        out_specs=VMEM,
+        out_specs=(VMEM, VMEM),
+        scratch_shapes=[pltpu.VMEM((form_count, N), F32)],
         compiler_params=params(16),
         cost_estimate=side_cost,
     )(hartree_forms)
@@ -373,7 +377,7 @@
     level, stats = pl.pallas_call(
         last_kernel,
         out_shape=(shape((KL * N, N), F32), shape((count, KL * form_count + N), F32)),
-        in_specs=[VMEM] * 6,
+        in_specs=[VMEM] * 7,
         out_specs=(VMEM, VMEM),
         scratch_shapes=[
             pltpu.VMEM((KL, N, N), BF16),
@@ -382,7 +386,7 @@
             pltpu.VMEM((KL, N), F32),
         ],
         compiler_params=params(28),
-    )(even_across, odd_across, form_factors, partial, turned, charge)
+    )(even_across, odd_across, form_factors, partial, turned, traces, charge)
     shared = lax.all_to_all(stats, "ka", 0, 0, tiled=True)
     return pl.pallas_call(
         final_kernel,

time: 34.8 us -> 34.7 us (level)
  no operation moved by 1% of the time
where the time goes in v9:
time: 34.7 us; the launch traced here: 34.6 us
  Pallas kernels  15.1 us (44%)
  blocking collectives  10.3 us (30%)
  starting transfers between devices  8.31 us (24%)
  between operations  0.77 us (2%)
    all_to_all x1, blocking collectives, per_device(): shared = lax.all_to_all(stats, 'ka', 0, 0, tiled=True)  10.3 us
    ppermute x1, starting transfers between devices, per_device(): odd = lax.ppermute(again, 'ka', between)  4.59 us
    pallas_call x1, Pallas kernels, per_device(): pl.pallas_call(inner_kernel, out_shape=(shape((KL, N, N), F32), shape((8,...  4.05 us
    pallas_call x1, Pallas kernels, per_device(): pl.pallas_call(final_kernel, out_shape=(shape((KL, N, N), F32), shape((KL...  3.65 us
    pallas_call x1, Pallas kernels, per_device(): pl.pallas_call(last_kernel, out_shape=(shape((KL * N, N), F32), shape((co...  2.96 us
    ppermute x1, starting transfers between devices, per_device(): even = lax.ppermute(packed, 'ka', within)  2.56 us
    pallas_call x2, Pallas kernels, side(): pl.pallas_call(functools.partial(side_kernel, second), out_shape=shape((K...  2.46 us
    pallas_call x1, Pallas kernels, per_device(): pl.pallas_call(pack_kernel, out_shape=(shape((PACK, N), BF16), shape((N,...  1.36 us
  transfers between devices with their start and end apart: 5, of which 0 were waited for; matrix products, arithmetic and copies ran while one was open for 0% of the time, Pallas kernels for 20%

profile of v9, /device:TPU:0, one launch (start us, length us, event | category | flops | bytes accessed | tf_op | source)
XLA Modules:
  0.0 34.6 jit_solution(12714611293547917103)
XLA Ops:
  0.6 0.0 copy-start
  0.6 0.0 copy-start.1
  0.7 0.0 copy-start.4
  0.7 1.4 %shard_map.77 = (bf16[528,128]{1,0:T(8,128)(2,1)S(1)}, f32[128,128]{1,0:T(8,128)S(1)}) custom-call(f32[8,128,128]{2,1,0:T(8,128)} %density_hbm.1), custom_call_target="tpu_custom_call" | custom-call | flops 5000000000 | bytes 2000000 | tf_op jit(solution)/shard_map/pallas_call | solution.py:315
  2.0 0.5 %collective-permute-start = (bf16[528,128]{1,0:T(8,128)(2,1)S(1)}, bf16[528,128]{1,0:T(8,128)(2,1)S(1)}, u32[]{:S(2)}, u32[]{:S(2)}) collective-permute-start(bf16[528,128]{1,0:T(8,128)(2,1)S(1)} %get-tuple-element.17.own_ref.packed_ref), channel_id=1, source_target_pairs={{0,1},{1,0},{2,3},{3,2},{4,5},{5,4},{6,7},{7,6},{8,9},{9,8},{10,11... | collective-permute-start | bytes 405512 | tf_op jit(solution)/shard_map/ppermute | solution.py:328
  2.5 2.6 %collective-permute-start.1 = (bf16[528,128]{1,0:T(8,128)(2,1)S(1)}, bf16[528,128]{1,0:T(8,128)(2,1)S(1)}, u32[]{:S(2)}, u32[]{:S(2)}) collective-permute-start(bf16[528,128]{1,0:T(8,128)(2,1)S(1)} %get-tuple-element.17.own_ref.packed_ref), channel_id=1, source_target_pairs={{0,2},{1,3},{2,0},{3,1},{4,6},{5,7},{6,4},{7,5},{8,10},{9,11},{10,... | collective-permute-start | bytes 405512 | tf_op jit(solution)/shard_map/ppermute | solution.py:329
  5.1 4.6 %collective-permute-start.3 = (bf16[528,128]{1,0:T(8,128)(2,1)S(1)}, bf16[528,128]{1,0:T(8,128)(2,1)S(1)}, u32[]{:S(2)}, u32[]{:S(2)}) collective-permute-start(bf16[528,128]{1,0:T(8,128)(2,1)S(1)} %shard_map.81), channel_id=1, source_target_pairs={{0,30},{1,31},{2,4},{3,5},{4,2},{5,3},{6,8},{7,9},{8,6},{9,7},{10,... | collective-permute-start | bytes 405512 | tf_op jit(solution)/shard_map/ppermute | solution.py:333
  9.7 0.0 collective-permute-done.other_ref
  9.7 0.0 copy-done
  9.7 0.0 copy-done.1
  9.7 0.0 copy-done.4
  9.7 4.1 %shard_map.78 = (f32[8,128,128]{2,1,0:T(8,128)S(1)}, f32[8,32]{1,0:T(8,128)S(1)}) custom-call(bf16[528,128]{1,0:T(8,128)(2,1)S(1)} %get-tuple-element.17.own_ref.packed_ref, bf16[528,128]{1,0:T(8,128)(2,1)S(1)} %collective-permute-done.other_ref, bf16[33,2,128,128]{3,2,1,0:T(8,128)(2,1)S(1)} %copy-done, f32[8,128,128]{2,1,0:T(8,128)S(1)} %copy-done.4, ...), custom_call_target="tpu_custom_call" | custom-call | flops 5000000000 | bytes 5000000 | tf_op jit(solution)/shard_map/pallas_call | solution.py:334
  13.8 0.6 %shard_map.79 = (bf16[16,128,256]{2,1,0:T(8,128)(2,1)S(1)}, f32[8,32]{1,0:T(8,128)S(1)}) custom-call(bf16[32,128,128]{2,1,0:T(8,128)(2,1)S(1)} %copy-done.1), custom_call_target="tpu_custom_call" | custom-call | flops 2000000000 | bytes 5000000 | tf_op jit(solution)/shard_map/pallas_call | solution.py:362
  14.4 0.0 collective-permute-done.1.block_ref
  14.4 0.1 collective-permute-start.2
  14.4 1.2 %shard_map.80.partial_ref = f32[8,128,128]{2,1,0:T(8,128)S(1)} custom-call(bf16[528,128]{1,0:T(8,128)(2,1)S(1)} %collective-permute-done.1.block_ref, bf16[33,2,128,128]{3,2,1,0:T(8,128)(2,1)S(1)} %copy-done, f32[8,128,128]{2,1,0:T(8,128)S(1)} %get-tuple-element.24.partial_ref), custom_call_target="tpu_custom_call" | custom-call | flops 2000000000 | bytes 5000000 | tf_op jit(solution)/shard_map/pallas_call | solution.py:351
  15.7 0.0 collective-permute-done.3.block_ref
  15.7 0.6 %collective-permute-start.4 = (bf16[528,128]{1,0:T(8,128)(2,1)S(1)}, bf16[528,128]{1,0:T(8,128)(2,1)S(1)}, u32[]{:S(2)}, u32[]{:S(2)}) collective-permute-start(bf16[528,128]{1,0:T(8,128)(2,1)S(1)} %collective-permute-done.3.block_ref), channel_id=1, source_target_pairs={{0,1},{1,0},{2,3},{3,2},{4,5},{5,4},{6,7},{7,6},{8,9},{9,8},{10,11... | collective-permute-start | bytes 405512 | tf_op jit(solution)/shard_map/ppermute | solution.py:375
  16.2 1.2 %shard_map.82.partial_ref = f32[8,128,128]{2,1,0:T(8,128)S(1)} custom-call(bf16[528,128]{1,0:T(8,128)(2,1)S(1)} %collective-permute-done.3.block_ref, bf16[33,2,128,128]{3,2,1,0:T(8,128)(2,1)S(1)} %copy-done, f32[8,128,128]{2,1,0:T(8,128)S(1)} %shard_map.80.partial_ref), custom_call_target="tpu_custom_call" | custom-call | flops 2000000000 | bytes 5000000 | tf_op jit(solution)/shard_map/pallas_call | solution.py:351
  17.5 0.0 copy-start.2
  17.5 0.0 copy-start.3
  17.5 0.0 collective-permute-done.4.odd_ref
  17.5 0.0 collective-permute-done.2.even_ref
  17.5 3.0 %shard_map.83 = (f32[1024,128]{1,0:T(8,128)S(1)}, f32[32,384]{1,0:T(8,128)S(1)}) custom-call(bf16[528,128]{1,0:T(8,128)(2,1)S(1)} %collective-permute-done.2.even_ref, bf16[528,128]{1,0:T(8,128)(2,1)S(1)} %collective-permute-done.4.odd_ref, bf16[33,2,128,128]{3,2,1,0:T(8,128)(2,1)S(1)} %copy-done, f32[8,128,128]{2,1,0:T(8,128)S(1)} %shard_map.82.partial_ref, ...), custom_call_target="tpu_custom_call" | custom-call | tf_op jit(solution)/shard_map/pallas_call | solution.py:377
  20.5 0.1 copy.8
  20.6 10.3 %all_to_all.11 = f32[32,1,384]{2,1,0:T(1,128)S(1)} all-to-all(f32[32,1,384]{2,1,0:T(1,128)S(1)} %copy.8), channel_id=1, replica_groups=mesh['ka'=32] {'ka'}, dimensions={0} | all-to-all | bytes 98304 | tf_op jit(solution)/shard_map/all_to_all | solution.py:390
  30.9 0.0 copy-done.2
  30.9 0.0 copy-done.3
  30.9 3.6 %shard_map.84 = (f32[8,128,128]{2,1,0:T(8,128)}, f32[8,128,128]{2,1,0:T(8,128)}) custom-call(f32[32,384]{1,0:T(8,128)S(1)} %bitcast.5, f32[1024,128]{1,0:T(8,128)S(1)} %get-tuple-element.31.level_ref, bf16[32,128,128]{2,1,0:T(8,128)(2,1)S(1)} %copy-done.1, f32[1,32]{1,0:T(1,128)S(1)} %bitcast.7, s32[8]{0:T(128)S(1)} %copy-done.3), custom_call_target="tpu_custom_call" | custom-call | tf_op jit(solution)/shard_map/pallas_call | solution.py:391
  (2 shorter events, 0.0 us)
Async XLA Ops:
  0.6 9.1 %copy-start = (bf16[33,2,128,128]{3,2,1,0:T(8,128)(2,1)S(1)}, bf16[33,2,128,128]{3,2,1,0:T(8,128)(2,1)}, u32[]{:S(2)}) copy-start(bf16[33,2,128,128]{3,2,1,0:T(8,128)(2,1)} %factors_ref.7) | copy-start | bytes 6488068
  0.6 9.1 %copy-start.1 = (bf16[32,128,128]{2,1,0:T(8,128)(2,1)S(1)}, bf16[32,128,128]{2,1,0:T(8,128)(2,1)}, u32[]{:S(2)}) copy-start(bf16[32,128,128]{2,1,0:T(8,128)(2,1)} %forms_ref.3) | copy-start | bytes 3145732
  0.7 9.1 %copy-start.4 = (f32[8,128,128]{2,1,0:T(8,128)S(1)}, f32[8,128,128]{2,1,0:T(8,128)}, u32[]{:S(2)}) copy-start(f32[8,128,128]{2,1,0:T(8,128)} %hamiltonian_ref.1) | copy-start | bytes 1572868
  2.0 7.7 %collective-permute-start = (bf16[528,128]{1,0:T(8,128)(2,1)S(1)}, bf16[528,128]{1,0:T(8,128)(2,1)S(1)}, u32[]{:S(2)}, u32[]{:S(2)}) collective-permute-start(bf16[528,128]{1,0:T(8,128)(2,1)S(1)} %get-tuple-element.17.own_ref.packed_ref), channel_id=1, source_target_pairs={{0,1},{1,0},{2,3},{3,2},{4,5},{5,4},{6,7},{7,6},{8,9},{9,8},{10,11... | collective-permute-start | bytes 405512 | tf_op jit(solution)/shard_map/ppermute | solution.py:328
  2.5 11.8 %collective-permute-start.1 = (bf16[528,128]{1,0:T(8,128)(2,1)S(1)}, bf16[528,128]{1,0:T(8,128)(2,1)S(1)}, u32[]{:S(2)}, u32[]{:S(2)}) collective-permute-start(bf16[528,128]{1,0:T(8,128)(2,1)S(1)} %get-tuple-element.17.own_ref.packed_ref), channel_id=1, source_target_pairs={{0,2},{1,3},{2,0},{3,1},{4,6},{5,7},{6,4},{7,5},{8,10},{9,11},{10,... | collective-permute-start | bytes 405512 | tf_op jit(solution)/shard_map/ppermute | solution.py:329
  5.1 10.6 %collective-permute-start.3 = (bf16[528,128]{1,0:T(8,128)(2,1)S(1)}, bf16[528,128]{1,0:T(8,128)(2,1)S(1)}, u32[]{:S(2)}, u32[]{:S(2)}) collective-permute-start(bf16[528,128]{1,0:T(8,128)(2,1)S(1)} %shard_map.81), channel_id=1, source_target_pairs={{0,30},{1,31},{2,4},{3,5},{4,2},{5,3},{6,8},{7,9},{8,6},{9,7},{10,... | collective-permute-start | bytes 405512 | tf_op jit(solution)/shard_map/ppermute | solution.py:333
  14.4 3.2 %collective-permute-start.2 = (bf16[528,128]{1,0:T(8,128)(2,1)S(1)}, bf16[528,128]{1,0:T(8,128)(2,1)S(1)}, u32[]{:S(2)}, u32[]{:S(2)}) collective-permute-start(bf16[528,128]{1,0:T(8,128)(2,1)S(1)} %collective-permute-done.1.block_ref), channel_id=1, source_target_pairs={{0,1},{1,0},{2,3},{3,2},{4,5},{5,4},{6,7},{7,6},{8,9},{9,8},{10,11... | collective-permute-start | bytes 405512 | tf_op jit(solution)/shard_map/ppermute | solution.py:372
  15.7 1.8 %collective-permute-start.4 = (bf16[528,128]{1,0:T(8,128)(2,1)S(1)}, bf16[528,128]{1,0:T(8,128)(2,1)S(1)}, u32[]{:S(2)}, u32[]{:S(2)}) collective-permute-start(bf16[528,128]{1,0:T(8,128)(2,1)S(1)} %collective-permute-done.3.block_ref), channel_id=1, source_target_pairs={{0,1},{1,0},{2,3},{3,2},{4,5},{5,4},{6,7},{7,6},{8,9},{9,8},{10,11... | collective-permute-start | bytes 405512 | tf_op jit(solution)/shard_map/ppermute | solution.py:375
  17.5 13.4 %copy-start.2 = (f32[32]{0:T(128)S(1)}, f32[32]{0:T(128)}, u32[]{:S(2)}) copy-start(f32[32]{0:T(128)} %param.11) | copy-start | bytes 388
  17.5 13.4 %copy-start.3 = (s32[8]{0:T(128)S(1)}, s32[8]{0:T(128)}, u32[]{:S(2)}) copy-start(s32[8]{0:T(128)} %occupations_ref.1) | copy-start | bytes 100

commit v10 on v9

--- a/solution.py
+++ b/solution.py
@@ -248,7 +248,7 @@
     charge = jnp.concatenate([charge_ref[0:1, :], jnp.zeros((1, N - form_count), F32)], axis=1)
     numbers = jnp.sum(numbers, axis=0, keepdims=True) + charge
     stats = jnp.concatenate([overlaps[k : k + 1, :] for k in range(KL)] + [numbers], axis=1)
-    stats_ref[...] = jnp.broadcast_to(stats, stats_ref.shape)
+    stats_ref[...] = jnp.broadcast_to(stats[None], stats_ref.shape)
 
 
 def final_kernel(
@@ -376,7 +376,7 @@
     partial = side(True, odd, partial)
     level, stats = pl.pallas_call(
         last_kernel,
-        out_shape=(shape((KL * N, N), F32), shape((count, KL * form_count + N), F32)),
+        out_shape=(shape((KL * N, N), F32), shape((count, 1, KL * form_count + N), F32)),
         in_specs=[VMEM] * 7,
         out_specs=(VMEM, VMEM),
         scratch_shapes=[
@@ -387,7 +387,7 @@
         ],
         compiler_params=params(28),
     )(even_across, odd_across, form_factors, partial, turned, traces, charge)
-    shared = lax.all_to_all(stats, "ka", 0, 0, tiled=True)
+    shared = lax.all_to_all(stats, "ka", 0, 0, tiled=True).reshape(count, -1)
     return pl.pallas_call(
         final_kernel,
         out_shape=(shape((KL, N, N), F32), shape((KL, N, N), F32)),

time: 34.7 us -> 34.7 us (level)
  transfers between devices with their start and end apart: 5 -> 5, of which waited for: 0 -> 0; matrix products, arithmetic and copies ran while one was open for 0% -> 0% of each run, Pallas kernels for 20% -> 21%
where the time goes in v10:
time: 34.7 us; the launch traced here: 34.5 us
  Pallas kernels  15.1 us (44%)
  blocking collectives  10.3 us (30%)
  starting transfers between devices  8.31 us (24%)
  between operations  0.77 us (2%)
    all_to_all x1, blocking collectives, per_device(): shared = lax.all_to_all(stats, 'ka', 0, 0, tiled=True).reshape(count, -1)  10.3 us
    ppermute x1, starting transfers between devices, per_device(): odd = lax.ppermute(again, 'ka', between)  4.59 us
    pallas_call x1, Pallas kernels, per_device(): pl.pallas_call(inner_kernel, out_shape=(shape((KL, N, N), F32), shape((8,...  4.05 us
    pallas_call x1, Pallas kernels, per_device(): pl.pallas_call(final_kernel, out_shape=(shape((KL, N, N), F32), shape((KL...  3.64 us
    pallas_call x1, Pallas kernels, per_device(): pl.pallas_call(last_kernel, out_shape=(shape((KL * N, N), F32), shape((co...  2.98 us
    ppermute x1, starting transfers between devices, per_device(): even = lax.ppermute(packed, 'ka', within)  2.56 us
    pallas_call x2, Pallas kernels, side(): pl.pallas_call(functools.partial(side_kernel, second), out_shape=shape((K...  2.46 us
    pallas_call x1, Pallas kernels, per_device(): pl.pallas_call(pack_kernel, out_shape=(shape((PACK, N), BF16), shape((N,...  1.36 us
  transfers between devices with their start and end apart: 5, of which 0 were waited for; matrix products, arithmetic and copies ran while one was open for 0% of the time, Pallas kernels for 21%

profile of v10, /device:TPU:0, one launch (start us, length us, event | category | flops | bytes accessed | tf_op | source)
XLA Modules:
  0.0 34.5 jit_solution(17656814799154632049)
XLA Ops:
  0.6 0.0 copy-start
  0.6 0.0 copy-start.1
  0.7 0.0 copy-start.4
  0.7 1.4 %shard_map.77 = (bf16[528,128]{1,0:T(8,128)(2,1)S(1)}, f32[128,128]{1,0:T(8,128)S(1)}) custom-call(f32[8,128,128]{2,1,0:T(8,128)} %density_hbm.1), custom_call_target="tpu_custom_call" | custom-call | flops 5000000000 | bytes 2000000 | tf_op jit(solution)/shard_map/pallas_call | solution.py:315
  2.0 0.5 %collective-permute-start = (bf16[528,128]{1,0:T(8,128)(2,1)S(1)}, bf16[528,128]{1,0:T(8,128)(2,1)S(1)}, u32[]{:S(2)}, u32[]{:S(2)}) collective-permute-start(bf16[528,128]{1,0:T(8,128)(2,1)S(1)} %get-tuple-element.17.own_ref.packed_ref), channel_id=1, source_target_pairs={{0,1},{1,0},{2,3},{3,2},{4,5},{5,4},{6,7},{7,6},{8,9},{9,8},{10,11... | collective-permute-start | bytes 405512 | tf_op jit(solution)/shard_map/ppermute | solution.py:328
  2.5 2.6 %collective-permute-start.1 = (bf16[528,128]{1,0:T(8,128)(2,1)S(1)}, bf16[528,128]{1,0:T(8,128)(2,1)S(1)}, u32[]{:S(2)}, u32[]{:S(2)}) collective-permute-start(bf16[528,128]{1,0:T(8,128)(2,1)S(1)} %get-tuple-element.17.own_ref.packed_ref), channel_id=1, source_target_pairs={{0,2},{1,3},{2,0},{3,1},{4,6},{5,7},{6,4},{7,5},{8,10},{9,11},{10,... | collective-permute-start | bytes 405512 | tf_op jit(solution)/shard_map/ppermute | solution.py:329
  5.1 4.6 %collective-permute-start.3 = (bf16[528,128]{1,0:T(8,128)(2,1)S(1)}, bf16[528,128]{1,0:T(8,128)(2,1)S(1)}, u32[]{:S(2)}, u32[]{:S(2)}) collective-permute-start(bf16[528,128]{1,0:T(8,128)(2,1)S(1)} %shard_map.81), channel_id=1, source_target_pairs={{0,30},{1,31},{2,4},{3,5},{4,2},{5,3},{6,8},{7,9},{8,6},{9,7},{10,... | collective-permute-start | bytes 405512 | tf_op jit(solution)/shard_map/ppermute | solution.py:333
  9.7 0.0 collective-permute-done.other_ref
  9.7 0.0 copy-done
  9.7 0.0 copy-done.1
  9.7 0.0 copy-done.4
  9.7 4.1 %shard_map.78 = (f32[8,128,128]{2,1,0:T(8,128)S(1)}, f32[8,32]{1,0:T(8,128)S(1)}) custom-call(bf16[528,128]{1,0:T(8,128)(2,1)S(1)} %get-tuple-element.17.own_ref.packed_ref, bf16[528,128]{1,0:T(8,128)(2,1)S(1)} %collective-permute-done.other_ref, bf16[33,2,128,128]{3,2,1,0:T(8,128)(2,1)S(1)} %copy-done, f32[8,128,128]{2,1,0:T(8,128)S(1)} %copy-done.4, ...), custom_call_target="tpu_custom_call" | custom-call | flops 5000000000 | bytes 5000000 | tf_op jit(solution)/shard_map/pallas_call | solution.py:334
  13.8 0.6 %shard_map.79 = (bf16[16,128,256]{2,1,0:T(8,128)(2,1)S(1)}, f32[8,32]{1,0:T(8,128)S(1)}) custom-call(bf16[32,128,128]{2,1,0:T(8,128)(2,1)S(1)} %copy-done.1), custom_call_target="tpu_custom_call" | custom-call | flops 2000000000 | bytes 5000000 | tf_op jit(solution)/shard_map/pallas_call | solution.py:362
  14.4 0.0 collective-permute-done.1.block_ref
  14.4 0.1 collective-permute-start.2
  14.4 1.2 %shard_map.80.partial_ref = f32[8,128,128]{2,1,0:T(8,128)S(1)} custom-call(bf16[528,128]{1,0:T(8,128)(2,1)S(1)} %collective-permute-done.1.block_ref, bf16[33,2,128,128]{3,2,1,0:T(8,128)(2,1)S(1)} %copy-done, f32[8,128,128]{2,1,0:T(8,128)S(1)} %get-tuple-element.24.partial_ref), custom_call_target="tpu_custom_call" | custom-call | flops 2000000000 | bytes 5000000 | tf_op jit(solution)/shard_map/pallas_call | solution.py:351
  15.7 0.0 collective-permute-done.3.block_ref
  15.7 0.6 %collective-permute-start.4 = (bf16[528,128]{1,0:T(8,128)(2,1)S(1)}, bf16[528,128]{1,0:T(8,128)(2,1)S(1)}, u32[]{:S(2)}, u32[]{:S(2)}) collective-permute-start(bf16[528,128]{1,0:T(8,128)(2,1)S(1)} %collective-permute-done.3.block_ref), channel_id=1, source_target_pairs={{0,1},{1,0},{2,3},{3,2},{4,5},{5,4},{6,7},{7,6},{8,9},{9,8},{10,11... | collective-permute-start | bytes 405512 | tf_op jit(solution)/shard_map/ppermute | solution.py:375
  16.2 1.2 %shard_map.82.partial_ref = f32[8,128,128]{2,1,0:T(8,128)S(1)} custom-call(bf16[528,128]{1,0:T(8,128)(2,1)S(1)} %collective-permute-done.3.block_ref, bf16[33,2,128,128]{3,2,1,0:T(8,128)(2,1)S(1)} %copy-done, f32[8,128,128]{2,1,0:T(8,128)S(1)} %shard_map.80.partial_ref), custom_call_target="tpu_custom_call" | custom-call | flops 2000000000 | bytes 5000000 | tf_op jit(solution)/shard_map/pallas_call | solution.py:351
  17.5 0.0 copy-start.2
  17.5 0.0 copy-start.3
  17.5 0.0 collective-permute-done.4.odd_ref
  17.5 0.0 collective-permute-done.2.even_ref
  17.5 3.0 %shard_map.83 = (f32[1024,128]{1,0:T(8,128)S(1)}, f32[32,1,384]{2,1,0:T(1,128)S(1)}) custom-call(bf16[528,128]{1,0:T(8,128)(2,1)S(1)} %collective-permute-done.2.even_ref, bf16[528,128]{1,0:T(8,128)(2,1)S(1)} %collective-permute-done.4.odd_ref, bf16[33,2,128,128]{3,2,1,0:T(8,128)(2,1)S(1)} %copy-done, f32[8,128,128]{2,1,0:T(8,128)S(1)} %shard_map.82.partial_ref, ...), custom_call_target="tpu_custom_call" | custom-call | tf_op jit(solution)/shard_map/pallas_call | solution.py:377
  20.5 10.3 %all_to_all.5 = f32[32,1,384]{2,1,0:T(1,128)S(1)} all-to-all(f32[32,1,384]{2,1,0:T(1,128)S(1)} %get-tuple-element.30), channel_id=1, replica_groups=mesh['ka'=32] {'ka'}, dimensions={0} | all-to-all | bytes 98304 | tf_op jit(solution)/shard_map/all_to_all | solution.py:390
  30.9 0.0 copy-done.2
  30.9 0.0 copy-done.3
  30.9 3.6 %shard_map.84 = (f32[8,128,128]{2,1,0:T(8,128)}, f32[8,128,128]{2,1,0:T(8,128)}) custom-call(f32[32,384]{1,0:T(8,128)S(1)} %bitcast.4, f32[1024,128]{1,0:T(8,128)S(1)} %get-tuple-element.31.level_ref, bf16[32,128,128]{2,1,0:T(8,128)(2,1)S(1)} %copy-done.1, f32[1,32]{1,0:T(1,128)S(1)} %bitcast.5, s32[8]{0:T(128)S(1)} %copy-done.3), custom_call_target="tpu_custom_call" | custom-call | tf_op jit(solution)/shard_map/pallas_call | solution.py:391
  (2 shorter events, 0.0 us)
Async XLA Ops:
  0.6 9.1 %copy-start = (bf16[33,2,128,128]{3,2,1,0:T(8,128)(2,1)S(1)}, bf16[33,2,128,128]{3,2,1,0:T(8,128)(2,1)}, u32[]{:S(2)}) copy-start(bf16[33,2,128,128]{3,2,1,0:T(8,128)(2,1)} %factors_ref.7) | copy-start | bytes 6488068
  0.6 9.1 %copy-start.1 = (bf16[32,128,128]{2,1,0:T(8,128)(2,1)S(1)}, bf16[32,128,128]{2,1,0:T(8,128)(2,1)}, u32[]{:S(2)}) copy-start(bf16[32,128,128]{2,1,0:T(8,128)(2,1)} %forms_ref.3) | copy-start | bytes 3145732
  0.7 9.1 %copy-start.4 = (f32[8,128,128]{2,1,0:T(8,128)S(1)}, f32[8,128,128]{2,1,0:T(8,128)}, u32[]{:S(2)}) copy-start(f32[8,128,128]{2,1,0:T(8,128)} %hamiltonian_ref.1) | copy-start | bytes 1572868
  2.0 7.7 %collective-permute-start = (bf16[528,128]{1,0:T(8,128)(2,1)S(1)}, bf16[528,128]{1,0:T(8,128)(2,1)S(1)}, u32[]{:S(2)}, u32[]{:S(2)}) collective-permute-start(bf16[528,128]{1,0:T(8,128)(2,1)S(1)} %get-tuple-element.17.own_ref.packed_ref), channel_id=1, source_target_pairs={{0,1},{1,0},{2,3},{3,2},{4,5},{5,4},{6,7},{7,6},{8,9},{9,8},{10,11... | collective-permute-start | bytes 405512 | tf_op jit(solution)/shard_map/ppermute | solution.py:328
  2.5 11.8 %collective-permute-start.1 = (bf16[528,128]{1,0:T(8,128)(2,1)S(1)}, bf16[528,128]{1,0:T(8,128)(2,1)S(1)}, u32[]{:S(2)}, u32[]{:S(2)}) collective-permute-start(bf16[528,128]{1,0:T(8,128)(2,1)S(1)} %get-tuple-element.17.own_ref.packed_ref), channel_id=1, source_target_pairs={{0,2},{1,3},{2,0},{3,1},{4,6},{5,7},{6,4},{7,5},{8,10},{9,11},{10,... | collective-permute-start | bytes 405512 | tf_op jit(solution)/shard_map/ppermute | solution.py:329
  5.1 10.6 %collective-permute-start.3 = (bf16[528,128]{1,0:T(8,128)(2,1)S(1)}, bf16[528,128]{1,0:T(8,128)(2,1)S(1)}, u32[]{:S(2)}, u32[]{:S(2)}) collective-permute-start(bf16[528,128]{1,0:T(8,128)(2,1)S(1)} %shard_map.81), channel_id=1, source_target_pairs={{0,30},{1,31},{2,4},{3,5},{4,2},{5,3},{6,8},{7,9},{8,6},{9,7},{10,... | collective-permute-start | bytes 405512 | tf_op jit(solution)/shard_map/ppermute | solution.py:333
  14.4 3.2 %collective-permute-start.2 = (bf16[528,128]{1,0:T(8,128)(2,1)S(1)}, bf16[528,128]{1,0:T(8,128)(2,1)S(1)}, u32[]{:S(2)}, u32[]{:S(2)}) collective-permute-start(bf16[528,128]{1,0:T(8,128)(2,1)S(1)} %collective-permute-done.1.block_ref), channel_id=1, source_target_pairs={{0,1},{1,0},{2,3},{3,2},{4,5},{5,4},{6,7},{7,6},{8,9},{9,8},{10,11... | collective-permute-start | bytes 405512 | tf_op jit(solution)/shard_map/ppermute | solution.py:372
  15.7 1.8 %collective-permute-start.4 = (bf16[528,128]{1,0:T(8,128)(2,1)S(1)}, bf16[528,128]{1,0:T(8,128)(2,1)S(1)}, u32[]{:S(2)}, u32[]{:S(2)}) collective-permute-start(bf16[528,128]{1,0:T(8,128)(2,1)S(1)} %collective-permute-done.3.block_ref), channel_id=1, source_target_pairs={{0,1},{1,0},{2,3},{3,2},{4,5},{5,4},{6,7},{7,6},{8,9},{9,8},{10,11... | collective-permute-start | bytes 405512 | tf_op jit(solution)/shard_map/ppermute | solution.py:375
  17.5 13.4 %copy-start.2 = (f32[32]{0:T(128)S(1)}, f32[32]{0:T(128)}, u32[]{:S(2)}) copy-start(f32[32]{0:T(128)} %param.11) | copy-start | bytes 388
  17.5 13.4 %copy-start.3 = (s32[8]{0:T(128)S(1)}, s32[8]{0:T(128)}, u32[]{:S(2)}) copy-start(s32[8]{0:T(128)} %occupations_ref.1) | copy-start | bytes 100
